TPU v7x, 32 devices: a whole 2x2x4 slice. The times are simulated.
32 devices in a mesh: groups: 2 (over x), tensor: 16 (over z, y, core).
Axes of the slice: x: 2, y: 2, z: 4, core: 2. Of those that a mesh axis runs over, the one named last changes fastest.
Arguments:
- hidden: bfloat16 [4, 256, 16384], P(None, 'groups', 'tensor'), parts along dimension 1, may hold values from -6 to 6
- down_matrix: bfloat16 [16384, 8192], P('tensor'), may hold values from -0.046875 to 0.046875
- first_factor_table: bfloat16 [256, 16, 16384], P(('groups', 'tensor')), parts along dimension 0, may hold values from -0.046875 to 0.046875
- second_factor_table: bfloat16 [256, 16, 8192], P(('groups', 'tensor')), parts along dimension 0, may hold values from -1.5 to 1.5
- adapter_storage_index: int32 [256], P('groups'), parts along dimension 0, may hold values from 0 to 127, as said below
- request_adapter: int32 [256], P('groups'), parts along dimension 0, may hold values from 0 to 127, as said below
Outputs:
- mixed: bfloat16 [4, 256, 8192], P(None, 'groups', 'tensor'), parts along dimension 1
There are 2 independent parts, one for each index of `groups`. A program takes and returns all parts, laid end to end along the dimension named above; an argument that names none is the same for every part. Nothing has to cross between parts.
Inputs may be any that keep to these rules, and one draw needn't show every extreme that they name: `adapter_storage_index`: a permutation: each slot holds one adapter. `request_adapter`: at most 32 requests name adapters whose slots lie in one aligned block of 8 slots, and some block has exactly 32.
All inputs are finite; a program needn't handle non-finite values.
Results may differ from a plain program's by a relative error of at most 0.0041.
Values may be sent and summed in bfloat16 or wider, within the bound.
No kernel may reach another device: no remote copies, remote signals or barrier semaphores. Data moves between devices by JAX's collectives and lax.ppermute only.
A program may use at most 192 MiB of HBM per device.

v0:
```python
import jax
import jax.numpy as jnp
from jax import lax
from jax.sharding import PartitionSpec as P


def fold_table(columns, rank_count):
    positions = jnp.arange(columns, dtype=jnp.int32) % rank_count
    return (positions[:, None] == jnp.arange(rank_count, dtype=jnp.int32)[None, :]).astype(
        jnp.float32
    )


def local(
    hidden,
    down_matrix,
    first_factor_table,
    second_factor_table,
    adapter_storage_index,
    request_adapter,
):
    steps_n, rows_n, ff_local = hidden.shape
    per_shard, rank_count, hidden_full = first_factor_table.shape
    model_width_full = second_factor_table.shape[2]
    adapters_n = adapter_storage_index.shape[0]
    flat = hidden.reshape(steps_n * rows_n, ff_local)
    partial_value = jnp.dot(flat, down_matrix, preferred_element_type=jnp.float32).reshape(
        steps_n, rows_n, model_width_full
    )
    table = jnp.arange(adapters_n, dtype=jnp.int32)
    slot_row = jnp.sum(
        jnp.where(request_adapter[:, None] == table[None, :], adapter_storage_index[None, :], 0),
        axis=1,
    )
    blocks_a, blocks_b = (
        lax.all_to_all(first_factor_table, "tensor", split_axis=2, concat_axis=0, tiled=True),
        lax.all_to_all(second_factor_table, "tensor", split_axis=2, concat_axis=0, tiled=True),
    )
    d_local = blocks_b.shape[2]
    widened = lax.dot_general(
        flat,
        blocks_a.reshape(adapters_n * rank_count, ff_local),
        (((1,), (1,)), ((), ())),
        preferred_element_type=jnp.float32,
    )
    chosen = (slot_row[:, None] == table[None, :]).astype(jnp.float32)
    column_mask = jnp.repeat(chosen, rank_count, axis=1)
    masked = widened.reshape(steps_n, rows_n, adapters_n * rank_count) * column_mask[None, :, :]
    folding = fold_table(adapters_n * rank_count, rank_count)
    lowpart = jnp.einsum("src,ck->srk", masked, folding, precision=lax.Precision.HIGHEST)
    low_sum = lax.psum(lowpart, "tensor")
    low_half = low_sum.astype(jnp.bfloat16)
    spread = (
        column_mask.astype(jnp.bfloat16)[None, :, :] * jnp.tile(low_half, (1, 1, adapters_n))
    ).reshape(steps_n * rows_n, adapters_n * rank_count)
    adapter_out = jnp.dot(
        spread,
        blocks_b.reshape(adapters_n * rank_count, d_local),
        preferred_element_type=jnp.float32,
    )
    addition = adapter_out.reshape(steps_n, rows_n, d_local)
    summed = lax.psum_scatter(partial_value, "tensor", scatter_dimension=2, tiled=True)
    return (summed + addition).astype(jnp.bfloat16)


def solution(mesh):
    in_specs = (
        P(None, "groups", "tensor"),
        P("tensor", None),
        P(("groups", "tensor"), None, None),
        P(("groups", "tensor"), None, None),
        P("groups"),
        P("groups"),
    )
    out_specs = P(None, "groups", "tensor")
    return jax.shard_map(local, mesh=mesh, in_specs=in_specs, out_specs=out_specs, check_vma=False)
```

profile of v0, /device:TPU:0, one launch (start us, length us, event | category | flops | bytes accessed | tf_op | source)
XLA Modules:
  0.0 438.3 jit_solution(4424443397395054595)
XLA Ops:
  6.5 0.0 copy-start
  6.5 0.0 reduce-scatter.2.cloned.1.call-start
  6.5 1.2 copy-done
  7.8 15.6 %fusion = f32[4,128,8192]{2,1,0:T(8,128)} fusion(bf16[4,128,1024]{2,1,0:T(8,128)(2,1)S(1)} %copy-done, bf16[1024,8192]{1,0:T(8,128)(2,1)} %param.7), kind=kOutput, calls=%fused_computation | convolution fusion | flops 8589934592 | bytes 34603008 | tf_op jit(solution)/shard_map/dot_general | solution.py:27
  23.4 0.0 copy-start.2
  23.4 0.0 reduce-scatter.2.cloned.1.call-update
  23.4 1.6 copy-done.2
  25.0 13.1 %copy.27 = bf16[8,16,8192]{1,0,2:T(8,128)(2,1)} copy(bf16[8,16,8192]{2,1,0:T(8,128)(2,1)S(1)} %copy-done.2) | data formatting | bytes 4194304 | tf_op args[3]
  38.1 22.0 %reshape.70 = bf16[16,2,32768]{2,1,0:T(2,128)(2,1)} reshape(bf16[8192,8,16]{2,1,0:T(8,128)(2,1)} %bitcast.33) | data formatting | bytes 4194304
  60.0 7.3 %all-to-all-start.1 = ((bf16[16,2,32768]{2,1,0:T(2,128)(2,1)}), bf16[16,2,32768]{2,1,0:T(2,128)(2,1)S(1)}, u32[]{:S(2)}, u32[]{:S(2)}) async-start(bf16[16,2,32768]{2,1,0:T(2,128)(2,1)} %reshape.70), calls=%async_computation.2 | async-start | bytes 4194304 | tf_op jit(solution)/shard_map/all_to_all | solution.py:37
  67.3 27.2 %copy.23 = bf16[8,16,16384]{1,0,2:T(8,128)(2,1)} copy(bf16[8,16,16384]{2,1,0:T(8,128)(2,1)} %param.8) | data formatting | bytes 8388608 | tf_op args[2]
  94.5 36.8 %reshape.68 = bf16[16,2,65536]{2,1,0:T(2,128)(2,1)} reshape(bf16[16384,8,16]{2,1,0:T(8,128)(2,1)} %bitcast.31) | data formatting | bytes 8388608
  131.3 0.0 copy-start.3
  131.3 0.0 copy-start.4
  131.3 9.6 %all-to-all-done.1 = bf16[16,2,32768]{2,1,0:T(2,128)(2,1)S(1)} async-done(((bf16[16,2,32768]{2,1,0:T(2,128)(2,1)}), bf16[16,2,32768]{2,1,0:T(2,128)(2,1)S(1)}, u32[]{:S(2)}, u32[]{:S(2)}) %all-to-all-start.1) | async-done | bytes 2097184 | tf_op jit(solution)/shard_map/all_to_all | solution.py:37
  140.9 27.4 %all-to-all-start = ((bf16[16,2,65536]{2,1,0:T(2,128)(2,1)}), bf16[16,2,65536]{2,1,0:T(2,128)(2,1)}, u32[]{:S(2)}, u32[]{:S(2)}) async-start(bf16[16,2,65536]{2,1,0:T(2,128)(2,1)} %reshape.68), calls=%async_computation.1 | async-start | bytes 8388608 | tf_op jit(solution)/shard_map/all_to_all | solution.py:36
  168.3 0.0 copy-done.3
  168.3 0.0 copy-done.4
  168.3 0.2 select_reduce_fusion
  168.5 1.0 broadcast_in_dim.16
  169.5 2.6 copy.26
  172.2 14.3 %reshape.71 = bf16[8192,8,16]{2,1,0:T(8,128)(2,1)} reshape(bf16[16,2,32768]{2,1,0:T(2,128)(2,1)S(1)} %all-to-all-done.1) | data formatting | bytes 4194304
  186.4 16.0 %copy.28 = bf16[8,16,16,512]{3,1,0,2:T(8,128)(2,1)S(1)} copy(bf16[8,16,16,512]{1,0,3,2:T(8,128)(2,1)} %bitcast.32) | data formatting | bytes 4194304 | tf_op jit(solution)/shard_map/all_to_all | solution.py:37
  202.5 50.1 %all-to-all-done = bf16[16,2,65536]{2,1,0:T(2,128)(2,1)} async-done(((bf16[16,2,65536]{2,1,0:T(2,128)(2,1)}), bf16[16,2,65536]{2,1,0:T(2,128)(2,1)}, u32[]{:S(2)}, u32[]{:S(2)}) %all-to-all-start) | async-done | bytes 4194336 | tf_op jit(solution)/shard_map/all_to_all | solution.py:36
  252.6 25.6 %reshape.69 = bf16[16384,8,16]{2,1,0:T(8,128)(2,1)} reshape(bf16[16,2,65536]{2,1,0:T(2,128)(2,1)} %all-to-all-done) | data formatting | bytes 8388608
  278.2 33.1 %copy.25 = bf16[16,8,16,1024]{3,2,1,0:T(8,128)(2,1)} copy(bf16[16,8,16,1024]{2,1,3,0:T(8,128)(2,1)} %bitcast.30) | data formatting | bytes 8388608 | tf_op jit(solution)/shard_map/all_to_all | solution.py:36
  311.2 0.0 copy-start.1
  311.2 4.6 %fusion.14 = f32[4,128,2048]{2,1,0:T(8,128)S(1)} fusion(bf16[4,128,1024]{2,1,0:T(8,128)(2,1)S(1)} %copy-done, bf16[2048,1024,1]{1,0,2:T(8,128)(2,1)} %bitcast.36), kind=kOutput, calls=%fused_computation.21 | convolution fusion | flops 2147483648 | bytes 9437184 | tf_op jit(solution)/shard_map/dot_general | solution.py:40
  315.9 0.0 copy-done.1
  315.9 2.1 fusion.2
  318.0 108.0 %psum.7 = bf16[4,128,16]{1,2,0:T(8,128)(2,1)S(1)} all-reduce(f32[4,128,16]{1,2,0:T(8,128)S(1)} %fusion.2), channel_id=1, replica_groups=mesh['groups'=2,'tensor'=16] {'tensor'}, use_global_device_ids=true, to_apply=%region_2.3 | all-reduce | flops 8192 | bytes 49152 | tf_op jit(solution)/shard_map/psum | solution.py:51
  426.0 1.5 broadcast_multiply_fusion
  427.5 0.0 reduce-scatter.2.cloned.1.call-done
  427.5 3.9 fusion.5
  (2 shorter events, 0.0 us)
Async XLA Ops:
  6.5 1.2 copy-start
  6.5 421.0 %reduce-scatter.2.cloned.1.call-start = ((), (), s32[]{:S(2)}) async-start(), calls=%async_computation.3 | async-start | bytes 17825792 | tf_op jit(solution)/shard_map/reduce_scatter | solution.py:62
  23.4 1.6 copy-start.2
  60.0 80.8 %all-to-all-start.1 = ((bf16[16,2,32768]{2,1,0:T(2,128)(2,1)}), bf16[16,2,32768]{2,1,0:T(2,128)(2,1)S(1)}, u32[]{:S(2)}, u32[]{:S(2)}) async-start(bf16[16,2,32768]{2,1,0:T(2,128)(2,1)} %reshape.70), calls=%async_computation.2 | async-start | bytes 4194304 | tf_op jit(solution)/shard_map/all_to_all | solution.py:37
  131.3 37.0 %copy-start.3 = (s32[128]{0:T(128)S(1)}, s32[128]{0:T(128)}, u32[]{:S(2)}) copy-start(s32[128]{0:T(128)} %param.10) | copy-start | bytes 1540
  131.3 37.0 %copy-start.4 = (s32[128]{0:T(128)S(1)}, s32[128]{0:T(128)}, u32[]{:S(2)}) copy-start(s32[128]{0:T(128)} %param.11) | copy-start | bytes 1540
  140.9 111.7 %all-to-all-start = ((bf16[16,2,65536]{2,1,0:T(2,128)(2,1)}), bf16[16,2,65536]{2,1,0:T(2,128)(2,1)}, u32[]{:S(2)}, u32[]{:S(2)}) async-start(bf16[16,2,65536]{2,1,0:T(2,128)(2,1)} %reshape.68), calls=%async_computation.1 | async-start | bytes 8388608 | tf_op jit(solution)/shard_map/all_to_all | solution.py:36
  311.2 4.7 %copy-start.1 = (f32[128,2048]{1,0:T(8,128)S(1)}, f32[128,2048]{1,0:T(8,128)}, u32[]{:S(2)}) copy-start(f32[128,2048]{1,0:T(8,128)} %copy.26) | copy-start | bytes 3145732
Sparse Core Ops, SparseCore 0:
  23.5 280.0 reduce-scatter.1
where the time goes:
time: 441 us; the launch traced here: 438 us
  local copies, waits for them, and re-layouts  194 us (44%)
  blocking collectives  108 us (24%)
  waiting for transfers between devices  59.7 us (14%)
  starting transfers between devices  34.6 us (8%)
  matrix products  26.3 us (6%)
  between operations  13.5 us (3%)
    unnamed x16, local copies, waits for them, and re-layouts  142 us
    psum x1, blocking collectives, local(): low_sum = lax.psum(lowpart, 'tensor')  108 us
    all_to_all x1, waiting for transfers between devices, local(): lax.all_to_all(first_factor_table, 'tensor', split_axis=2, concat_axis=0,...  50.1 us
    all_to_all x1, local copies, waits for them, and re-layouts, local(): lax.all_to_all(first_factor_table, 'tensor', split_axis=2, concat_axis=0,...  33.1 us
    all_to_all x1, starting transfers between devices, local(): lax.all_to_all(first_factor_table, 'tensor', split_axis=2, concat_axis=0,...  27.4 us
    all_to_all x1, local copies, waits for them, and re-layouts, local(): lax.all_to_all(second_factor_table, 'tensor', split_axis=2, concat_axis=0...  16 us
    dot_general x1, matrix products, local(): jnp.dot(flat, down_matrix, preferred_element_type=jnp.float32)  15.6 us
    all_to_all x1, waiting for transfers between devices, local(): lax.all_to_all(second_factor_table, 'tensor', split_axis=2, concat_axis=0...  9.55 us
  transfers between devices with their start and end apart: 3, of which 2 were waited for; matrix products, arithmetic and copies ran while one was open for 46% of the time, Pallas kernels for 0%

commit v1 on v0

v1 whole, which is shorter than its diff:
```python
import jax
import jax.numpy as jnp
from jax import lax
from jax.experimental import pallas as pl
from jax.experimental.pallas import tpu as pltpu
from jax.sharding import PartitionSpec as P

PLANE = 4
F32 = jnp.float32
BF16 = jnp.bfloat16
VMEM_BYTES = 48 * 1024 * 1024
LOW_CHUNKS = ((0, 2), (2, 4))
SUM_CHUNKS = ((0, 1), (1, 2), (2, 3), (3, 4))


def params():
    return pltpu.CompilerParams(vmem_limit_bytes=VMEM_BYTES)


def pack_factors(place, table, planes, width):
    rows = table.shape[0]

    def body(place_ref, *refs):
        for i in range(PLANE - 1):
            refs[PLANE - 1 + i][0] = refs[i][...]

    def columns(other):
        return lambda i, place_ref: (0, i * PLANE + (place_ref[1] ^ other))

    return pl.pallas_call(
        body,
        grid_spec=pltpu.PrefetchScalarGridSpec(
            num_scalar_prefetch=1,
            grid=(planes,),
            in_specs=[pl.BlockSpec((rows, width), columns(o)) for o in range(1, PLANE)],
            out_specs=[pl.BlockSpec((1, rows, width), lambda i, p: (i, 0, 0))] * (PLANE - 1),
        ),
        out_shape=[jax.ShapeDtypeStruct((planes, rows, width), BF16)] * (PLANE - 1),
        compiler_params=params(),
        name="pack_factors",
    )(place, table, table, table)


def base_blocks(place, hidden, down, planes, width):
    steps, rows, units = hidden.shape

    def body(place_ref, hidden_ref, d0, d1, d2, d3, send_ref, keep_ref):
        flat = hidden_ref[...].reshape(steps * rows, units)
        for i, ref in enumerate((d0, d1, d2, d3)):
            value = jnp.dot(flat, ref[...], preferred_element_type=F32).reshape(steps, rows, width)
            if i & 1:
                send_ref[i >> 1, 0] = value.astype(BF16)
            else:
                keep_ref[i >> 1, 0] = value

    def columns(other):
        return lambda i, p: (0, (p[0] ^ i) * PLANE + (p[1] ^ other))

    shape = (2, planes, steps, rows, width)
    return pl.pallas_call(
        body,
        grid_spec=pltpu.PrefetchScalarGridSpec(
            num_scalar_prefetch=1,
            grid=(planes,),
            in_specs=[pl.BlockSpec((steps, rows, units), lambda i, p: (0, 0, 0))]
            + [pl.BlockSpec((units, width), columns(o)) for o in range(PLANE)],
            out_specs=[pl.BlockSpec((2, 1, steps, rows, width), lambda i, p: (0, i, 0, 0, 0))] * 2,
        ),
        out_shape=[jax.ShapeDtypeStruct(shape, BF16), jax.ShapeDtypeStruct(shape, F32)],
        compiler_params=params(),
        name="base_blocks",
    )(place, hidden, down, down, down, down)


def low_part(place, order, slots, table, received, gathered, per_shard, rank):
    planes = len(gathered)
    rows, width = table.shape[0], gathered[0].shape[-1]
    steps, requests = gathered[0].shape[:2]
    lanes = steps * requests

    def body(place_ref, order_ref, slots_ref, a0, a1, a2, a3, *refs):
        hidden_refs, (out_ref, held, total) = refs[:planes], refs[planes:]
        j = pl.program_id(0)
        for i, ref in enumerate(hidden_refs):

            @pl.when(j == i)
            def _():
                held[...] = ref[...].reshape(lanes, width)

        @pl.when(j == 0)
        def _():
            total[...] = jnp.zeros_like(total)

        block = held[...]
        for i, ref in enumerate((a0, a1, a2, a3)):
            factors = ref[...] if i == 0 else ref[0]
            total[i] += lax.dot_general(
                factors, block, (((1,), (1,)), ((), ())), preferred_element_type=F32
            )

        @pl.when(j == planes - 1)
        def _():
            low = jnp.zeros((rank, lanes), F32)
            wanted = slots_ref[...]
            for i in range(PLANE):
                first = (place_ref[0] * PLANE + (place_ref[1] ^ i)) * per_shard
                for a in range(per_shard):
                    part = total[i, a * rank : (a + 1) * rank, :]
                    low += jnp.where(wanted == first + a, part, 0.0)
            out_ref[...] = low

    return pl.pallas_call(
        body,
        grid_spec=pltpu.PrefetchScalarGridSpec(
            num_scalar_prefetch=2,
            grid=(planes,),
            in_specs=[
                pl.BlockSpec((1, lanes), lambda j, p, o: (0, 0)),
                pl.BlockSpec((rows, width), lambda j, p, o: (0, o[j] * PLANE + p[1])),
            ]
            + [pl.BlockSpec((1, rows, width), lambda j, p, o: (o[j], 0, 0))] * (PLANE - 1)
            + [pl.BlockSpec((steps, requests, width), lambda j, p, o: (0, 0, 0))] * planes,
            out_specs=pl.BlockSpec((rank, lanes), lambda j, p, o: (0, 0)),
            scratch_shapes=[pltpu.VMEM((lanes, width), BF16), pltpu.VMEM((PLANE, rows, lanes), F32)],
        ),
        out_shape=jax.ShapeDtypeStruct((rank, lanes), F32),
        compiler_params=params(),
        name="low_part",
    )(place, order, slots, table, *received, *gathered)


def add_extra(place, low, slots, table, send, keep, chunk, per_shard, rank):
    _, planes, _, requests, width = send.shape
    first_step, last_step = chunk
    steps = last_step - first_step
    lanes = steps * requests
    rows = table.shape[0]

    def body(place_ref, low_ref, slots_ref, b0, b1, b2, b3, s_ref, k_ref, so_ref, ko_ref, spread):
        @pl.when(pl.program_id(0) == 0)
        def _():
            rounded = low_ref[...].astype(BF16).astype(F32)
            wanted = slots_ref[...]
            first = (place_ref[0] * PLANE + place_ref[1]) * per_shard
            parts = [jnp.where(wanted == first + a, rounded, 0.0) for a in range(per_shard)]
            spread[...] = jnp.concatenate(parts, axis=0).T.astype(BF16)

        rows_of = spread[...]
        for i, ref in enumerate((b0, b1, b2, b3)):
            extra = jnp.dot(rows_of, ref[...], preferred_element_type=F32)
            if i & 1:
                value = s_ref[i >> 1, 0].reshape(lanes, width).astype(F32) + extra
                so_ref[i >> 1, 0] = value.astype(BF16)
            else:
                ko_ref[i >> 1, 0] = k_ref[i >> 1, 0].reshape(lanes, width) + extra

    def columns(other):
        return lambda i, p: (0, (p[0] ^ i) * PLANE + (p[1] ^ other))

    base = pl.BlockSpec((2, 1, steps, requests, width), lambda i, p: (0, i, first_step // steps, 0, 0))
    shape = (2, planes, lanes, width)
    return pl.pallas_call(
        body,
        grid_spec=pltpu.PrefetchScalarGridSpec(
            num_scalar_prefetch=1,
            grid=(planes,),
            in_specs=[
                pl.BlockSpec((rank, lanes), lambda i, p: (0, 0)),
                pl.BlockSpec((1, lanes), lambda i, p: (0, 0)),
            ]
            + [pl.BlockSpec((rows, width), columns(o)) for o in range(PLANE)]
            + [base, base],
            out_specs=[pl.BlockSpec((2, 1, lanes, width), lambda i, p: (0, i, 0, 0))] * 2,
            scratch_shapes=[pltpu.VMEM((lanes, rows), BF16)],
        ),
        out_shape=[jax.ShapeDtypeStruct(shape, BF16), jax.ShapeDtypeStruct(shape, F32)],
        compiler_params=params(),
        name="add_extra",
    )(place, low, slots, table, table, table, table, send, keep)


def local(hidden, down_matrix, first_table, second_table, storage_index, request_adapter):
    steps, requests, units = hidden.shape
    per_shard, rank, all_units = first_table.shape
    features = second_table.shape[2]
    adapters = storage_index.shape[0]
    devices = all_units // units
    planes = devices // PLANE
    width = features // devices
    me = lax.axis_index("tensor").astype(jnp.int32)
    z, w = me // PLANE, me % PLANE
    place = jnp.stack([z, w])

    def in_plane(value, other):
        return lax.ppermute(value, "tensor", [(t, t ^ other) for t in range(devices)])

    def along(value, other):
        return lax.ppermute(value, "tensor", [(t, t ^ (other * PLANE)) for t in range(devices)])

    def hop(value, moves):
        pairs = [(a * PLANE + v, b * PLANE + v) for a, b in moves for v in range(PLANE)]
        return lax.ppermute(value, "tensor", pairs)

    table = jnp.arange(adapters, dtype=jnp.int32)
    slot_row = jnp.sum(
        jnp.where(request_adapter[:, None] == table[None, :], storage_index[None, :], 0), axis=1
    ).astype(jnp.int32)

    first = first_table.reshape(per_shard * rank, all_units)
    second = second_table.reshape(per_shard * rank, features)

    packed = pack_factors(place, first, planes, units)
    received = [in_plane(packed[o - 1], o) for o in range(1, PLANE)]

    if planes == 4:
        inner = (z == 1) | (z == 2)
        near = along(hidden, 1)
        middle = hop(hidden, ((1, 2), (2, 1)))
        order = jnp.stack([z, z ^ 1, jnp.where(z < 2, 2, 1), jnp.where(z < 2, 3, 0)])
        gathered = []
        for a, b in LOW_CHUNKS:
            outer_one = hop(middle[a:b], ((1, 0), (2, 3)))
            middle_two = hop(near[a:b], ((1, 2), (2, 1)))
            outer_two = hop(middle_two, ((1, 0), (2, 3)))
            gathered.append(
                [
                    hidden[a:b],
                    near[a:b],
                    jnp.where(inner, middle[a:b], outer_one),
                    jnp.where(inner, middle_two, outer_two),
                ]
            )
    else:
        order = jnp.stack([z ^ o for o in range(planes)])
        blocks = [hidden] + [along(hidden, o) for o in range(1, planes)]
        gathered = [[block[a:b] for block in blocks] for a, b in LOW_CHUNKS]

    send, keep = base_blocks(place, hidden, down_matrix, planes, width)

    lows = []
    for (a, b), blocks in zip(LOW_CHUNKS, gathered):
        slots = jnp.tile(slot_row[None, :], (1, b - a))
        low = low_part(place, order, slots, first, received, blocks, per_shard, rank)
        low = low + in_plane(low, 1)
        low = low + in_plane(low, 2)
        lows.append(low)

    outputs = []
    for a, b in SUM_CHUNKS:
        for (la, lb), low in zip(LOW_CHUNKS, lows):
            if la <= a and b <= lb:
                part = low[:, (a - la) * requests : (b - la) * requests]
        slots = jnp.tile(slot_row[None, :], (1, b - a))
        sent, kept = add_extra(place, part, slots, second, send, keep, (a, b), per_shard, rank)
        total = kept + in_plane(sent, 1).astype(F32)
        half = total[0] + in_plane(total[1].astype(BF16), 2).astype(F32)
        value = half[0]
        for o in range(1, planes):
            value = value + along(half[o].astype(BF16), o).astype(F32)
        outputs.append(value.astype(BF16).reshape(b - a, requests, width))
    return jnp.concatenate(outputs, axis=0)


def solution(mesh):
    in_specs = (
        P(None, "groups", "tensor"),
        P("tensor", None),
        P(("groups", "tensor"), None, None),
        P(("groups", "tensor"), None, None),
        P("groups"),
        P("groups"),
    )
    out_specs = P(None, "groups", "tensor")
    return jax.shard_map(local, mesh=mesh, in_specs=in_specs, out_specs=out_specs, check_vma=False)
```

time: 441 us -> 237 us (0.54)
  local copies, waits for them, and re-layouts: 194 us -> 5.44 us
  blocking collectives: 108 us -> 0 us
  waiting for transfers between devices: 59.7 us -> 140 us
  Pallas kernels: 0 us -> 48.3 us
  matrix products: 26.3 us -> 0 us
  between operations: 13.5 us -> 0.49 us
  other arithmetic: 1.69 us -> 6.65 us
    ppermute x0 -> x35, waiting for transfers between devices: none -> 140 us  [the longest x15 57.3 us: in_plane(): lax.ppermute(value, 'tensor', [(t, t ^ other) for t in range(devices)])]
    unnamed x16, local copies, waits for them, and re-layouts: 142 us -> 3.1 us
    psum x1 -> x0, blocking collectives: 108 us -> none  [local(): low_sum = lax.psum(lowpart, 'tensor')]
    all_to_all x2 -> x0, waiting for transfers between devices: 59.7 us -> none  [the longest x1 50.1 us: local(): lax.all_to_all(first_factor_table, 'tensor', split_axis=2, concat_axis=0,...]
    all_to_all x2 -> x0, local copies, waits for them, and re-layouts: 49.1 us -> none  [the longest x1 33.1 us: local(): lax.all_to_all(first_factor_table, 'tensor', split_axis=2, concat_axis=0,...]
    pallas_call x0 -> x8, Pallas kernels: none -> 48.3 us  [the longest x4 17.9 us: add_extra(): pl.pallas_call(body, grid_spec=pltpu.PrefetchScalarGridSpec(num_scalar_pr...]
    ppermute x0 -> x35, starting transfers between devices: none -> 35.6 us  [the longest x13 17.4 us: along(): lax.ppermute(value, 'tensor', [(t, t ^ other * PLANE) for t in range(devi...]
    all_to_all x2 -> x0, starting transfers between devices: 34.6 us -> none  [the longest x1 27.4 us: local(): lax.all_to_all(first_factor_table, 'tensor', split_axis=2, concat_axis=0,...]
  transfers between devices with their start and end apart: 3 -> 35, of which waited for: 2 -> 17; matrix products, arithmetic and copies ran while one was open for 46% -> 3% of each run, Pallas kernels for 0% -> 20%
where the time goes in v1:
time: 237 us; the launch traced here: 236 us
  waiting for transfers between devices  140 us (59%)
  Pallas kernels  48.3 us (20%)
  starting transfers between devices  35.6 us (15%)
  other arithmetic  6.65 us (3%)
  local copies, waits for them, and re-layouts  5.44 us (2%)
    ppermute x15, waiting for transfers between devices, in_plane(): lax.ppermute(value, 'tensor', [(t, t ^ other) for t in range(devices)])  57.3 us
    ppermute x13, waiting for transfers between devices, along(): lax.ppermute(value, 'tensor', [(t, t ^ other * PLANE) for t in range(devi...  46.1 us
    ppermute x7, waiting for transfers between devices, hop(): return lax.ppermute(value, 'tensor', pairs)  36.4 us
    pallas_call x4, Pallas kernels, add_extra(): pl.pallas_call(body, grid_spec=pltpu.PrefetchScalarGridSpec(num_scalar_pr...  17.9 us
    ppermute x13, starting transfers between devices, along(): lax.ppermute(value, 'tensor', [(t, t ^ other * PLANE) for t in range(devi...  17.4 us
    pallas_call x1, Pallas kernels, base_blocks(): pl.pallas_call(body, grid_spec=pltpu.PrefetchScalarGridSpec(num_scalar_pr...  14.5 us
    pallas_call x2, Pallas kernels, low_part(): pl.pallas_call(body, grid_spec=pltpu.PrefetchScalarGridSpec(num_scalar_pr...  11.1 us
    ppermute x15, starting transfers between devices, in_plane(): lax.ppermute(value, 'tensor', [(t, t ^ other) for t in range(devices)])  9.89 us
  transfers between devices with their start and end apart: 35, of which 17 were waited for; matrix products, arithmetic and copies ran while one was open for 3% of the time, Pallas kernels for 20%

profile of v1, /device:TPU:0, one launch (start us, length us, event | category | flops | bytes accessed | tf_op | source)
XLA Modules:
  0.0 236.2 jit_solution(17940369652200016389)
XLA Ops:
  0.0 3.0 %collective-permute-start.3 = (bf16[4,128,1024]{2,1,0:T(8,128)(2,1)}, bf16[4,128,1024]{2,1,0:T(8,128)(2,1)S(1)}, u32[]{:S(2)}, u32[]{:S(2)}) collective-permute-start(bf16[4,128,1024]{2,1,0:T(8,128)(2,1)} %hidden_ref.1), channel_id=1, source_target_pairs={{0,4},{1,5},{2,6},{3,7},{4,0},{5,1},{6,2},{7,3},{8,12},{9,13},{10,... | collective-permute-start | bytes 3145736 | tf_op jit(solution)/shard_map/ppermute | solution.py:198
  3.7 22.6 %collective-permute-done.3 = bf16[4,128,1024]{2,1,0:T(8,128)(2,1)S(1)} collective-permute-done((bf16[4,128,1024]{2,1,0:T(8,128)(2,1)}, bf16[4,128,1024]{2,1,0:T(8,128)(2,1)S(1)}, u32[]{:S(2)}, u32[]{:S(2)}) %collective-permute-start.3) | collective-permute-done | bytes 1048608 | tf_op jit(solution)/shard_map/ppermute | solution.py:198
  26.4 1.0 fusion.36
  27.4 1.5 collective-permute-start.21
  28.9 1.0 copy-done.4
  29.9 0.8 slice.157
  30.7 1.3 collective-permute-start.5
  32.1 4.7 %pack_factors.1 = (bf16[4,128,1024]{2,1,0:T(8,128)(2,1)}, bf16[4,128,1024]{2,1,0:T(8,128)(2,1)}, bf16[4,128,1024]{2,1,0:T(8,128)(2,1)}) custom-call(s32[2]{0:T(128)S(1)} %pad_add_fusion.place_ref, bf16[128,16384]{1,0:T(8,128)(2,1)} %bitcast.139, bf16[128,16384]{1,0:T(8,128)(2,1)} %bitcast.140, bf16[128,16384]{1,0:T(8,128)(2,1)} %bitcast.141), custom_call_target="tpu_custom_call" | custom-call | tf_op jit(solution)/shard_map/pack_factors/pallas_call | solution.py:30
  36.9 1.8 collective-permute-start.1
  39.0 1.4 collective-permute-start.22
  40.5 6.7 %collective-permute-done.5 = bf16[2,128,1024]{2,1,0:T(8,128)(2,1)} collective-permute-done((bf16[2,128,1024]{2,1,0:T(8,128)(2,1)}, bf16[2,128,1024]{2,1,0:T(8,128)(2,1)}, u32[]{:S(2)}, u32[]{:S(2)}) %collective-permute-start.5) | collective-permute-done | bytes 524320 | tf_op jit(solution)/shard_map/ppermute | solution.py:202
  47.2 1.4 broadcast_select_fusion.3
  48.6 1.4 collective-permute-start.20
  50.2 8.2 %collective-permute-done.22 = bf16[2,128,1024]{2,1,0:T(8,128)(2,1)S(1)} collective-permute-done((bf16[2,128,1024]{2,1,0:T(8,128)(2,1)}, bf16[2,128,1024]{2,1,0:T(8,128)(2,1)S(1)}, u32[]{:S(2)}, u32[]{:S(2)}) %collective-permute-start.22) | collective-permute-done | bytes 524320 | tf_op jit(solution)/shard_map/ppermute | solution.py:202
  59.2 10.1 %collective-permute-done.20 = bf16[2,128,1024]{2,1,0:T(8,128)(2,1)S(1)} collective-permute-done((bf16[2,128,1024]{2,1,0:T(8,128)(2,1)S(1)}, bf16[2,128,1024]{2,1,0:T(8,128)(2,1)S(1)}, u32[]{:S(2)}, u32[]{:S(2)}) %collective-permute-start.20) | collective-permute-done | bytes 524320 | tf_op jit(solution)/shard_map/ppermute | solution.py:202
  69.3 15.4 %collective-permute-done.2.a3 = bf16[4,128,1024]{2,1,0:T(8,128)(2,1)} collective-permute-done((bf16[4,128,1024]{2,1,0:T(8,128)(2,1)}, bf16[4,128,1024]{2,1,0:T(8,128)(2,1)}, u32[]{:S(2)}, u32[]{:S(2)}) %collective-permute-start.2) | collective-permute-done | bytes 1048608 | tf_op jit(solution)/shard_map/ppermute | solution.py:195
  84.8 5.6 %low_part.3 = f32[16,256]{1,0:T(8,128)S(1)} custom-call(s32[2]{0:T(128)S(1)} %pad_add_fusion.place_ref, s32[4]{0:T(128)S(1)} %pad_add_fusion.1.order_ref, s32[1,256]{1,0:T(1,128)S(1)} %bitcast.137, bf16[128,16384]{1,0:T(8,128)(2,1)} %bitcast.142, bf16[4,128,1024]{2,1,0:T(8,128)(2,1)S(1)} %collective-permute-done.a1, ...), custom_call_target="tpu_custom_call" | custom-call | tf_op jit(solution)/shard_map/low_part/pallas_call | solution.py:112
  90.8 0.9 collective-permute-done.23
  91.7 1.7 collective-permute-start.24
  93.4 14.5 %base_blocks.1 = (bf16[2,4,4,128,512]{4,3,2,1,0:T(8,128)(2,1)S(1)}, f32[2,4,4,128,512]{4,3,2,1,0:T(8,128)}) custom-call(s32[2]{0:T(128)S(1)} %pad_add_fusion.place_ref, bf16[4,128,1024]{2,1,0:T(8,128)(2,1)S(1)} %copy-done.2, bf16[1024,8192]{1,0:T(8,128)(2,1)} %d3.1, bf16[1024,8192]{1,0:T(8,128)(2,1)} %d3.1, bf16[1024,8192]{1,0:T(8,128)(2,1)} %d3.1, ...), custom_call_target="tpu_custom_call" | custom-call | tf_op jit(solution)/shard_map/base_blocks/pallas_call | solution.py:60
  107.9 2.1 copy-done.1
  110.0 4.3 %add_extra.7 = (bf16[2,4,128,512]{3,2,1,0:T(8,128)(2,1)S(1)}, f32[2,4,128,512]{3,2,1,0:T(8,128)S(1)}) custom-call(s32[2]{0:T(128)S(1)} %pad_add_fusion.place_ref, f32[16,128]{1,0:T(8,128)S(1)} %get-tuple-element.60.low_ref, s32[1,128]{1,0:T(1,128)S(1)} %bitcast.133, bf16[128,8192]{1,0:T(8,128)(2,1)S(1)} %bitcast.117, bf16[128,8192]{1,0:T(8,128)(2,1)S(1)} %bitcast.118, ...), custom_call_target="tpu_custom_call" | custom-call | tf_op jit(solution)/shard_map/add_extra/pallas_call | solution.py:162
  114.4 1.3 collective-permute-start.7
  115.7 5.1 %add_extra.6 = (bf16[2,4,128,512]{3,2,1,0:T(8,128)(2,1)}, f32[2,4,128,512]{3,2,1,0:T(8,128)S(1)}) custom-call(s32[2]{0:T(128)S(1)} %pad_add_fusion.place_ref, f32[16,128]{1,0:T(8,128)S(1)} %get-tuple-element.59.low_ref, s32[1,128]{1,0:T(1,128)S(1)} %bitcast.134, bf16[128,8192]{1,0:T(8,128)(2,1)S(1)} %bitcast.121, bf16[128,8192]{1,0:T(8,128)(2,1)S(1)} %bitcast.122, ...), custom_call_target="tpu_custom_call" | custom-call | tf_op jit(solution)/shard_map/add_extra/pallas_call | solution.py:162
  121.2 11.4 %collective-permute-done.7 = bf16[2,128,1024]{2,1,0:T(8,128)(2,1)S(1)} collective-permute-done((bf16[2,128,1024]{2,1,0:T(8,128)(2,1)S(1)}, bf16[2,128,1024]{2,1,0:T(8,128)(2,1)S(1)}, u32[]{:S(2)}, u32[]{:S(2)}) %collective-permute-start.7) | collective-permute-done | bytes 524320 | tf_op jit(solution)/shard_map/ppermute | solution.py:202
  132.7 5.4 %low_part.2 = f32[16,256]{1,0:T(8,128)S(1)} custom-call(s32[2]{0:T(128)S(1)} %pad_add_fusion.place_ref, s32[4]{0:T(128)S(1)} %pad_add_fusion.1.order_ref, s32[1,256]{1,0:T(1,128)S(1)} %bitcast.138, bf16[128,16384]{1,0:T(8,128)(2,1)} %bitcast.143, bf16[4,128,1024]{2,1,0:T(8,128)(2,1)S(1)} %collective-permute-done.a1, ...), custom_call_target="tpu_custom_call" | custom-call | tf_op jit(solution)/shard_map/low_part/pallas_call | solution.py:112
  138.2 1.2 collective-permute-done.8
  139.8 3.2 %collective-permute-done.9 = f32[16,256]{1,0:T(8,128)S(1)} collective-permute-done((f32[16,256]{1,0:T(8,128)S(1)}, f32[16,256]{1,0:T(8,128)S(1)}, u32[]{:S(2)}, u32[]{:S(2)}) %collective-permute-start.9) | collective-permute-done | bytes 16416 | tf_op jit(solution)/shard_map/ppermute | solution.py:195
  143.1 4.3 %add_extra.5 = (bf16[2,4,128,512]{3,2,1,0:T(8,128)(2,1)S(1)}, f32[2,4,128,512]{3,2,1,0:T(8,128)S(1)}) custom-call(s32[2]{0:T(128)S(1)} %pad_add_fusion.place_ref, f32[16,128]{1,0:T(8,128)S(1)} %get-tuple-element.58.low_ref, s32[1,128]{1,0:T(1,128)S(1)} %bitcast.135, bf16[128,8192]{1,0:T(8,128)(2,1)S(1)} %bitcast.125, bf16[128,8192]{1,0:T(8,128)(2,1)S(1)} %bitcast.126, ...), custom_call_target="tpu_custom_call" | custom-call | tf_op jit(solution)/shard_map/add_extra/pallas_call | solution.py:162
  147.4 4.3 %add_extra.4 = (bf16[2,4,128,512]{3,2,1,0:T(8,128)(2,1)S(1)}, f32[2,4,128,512]{3,2,1,0:T(8,128)S(1)}) custom-call(s32[2]{0:T(128)S(1)} %pad_add_fusion.place_ref, f32[16,128]{1,0:T(8,128)S(1)} %get-tuple-element.57.low_ref, s32[1,128]{1,0:T(1,128)S(1)} %bitcast.136, bf16[128,8192]{1,0:T(8,128)(2,1)S(1)} %bitcast.129, bf16[128,8192]{1,0:T(8,128)(2,1)S(1)} %bitcast.130, ...), custom_call_target="tpu_custom_call" | custom-call | tf_op jit(solution)/shard_map/add_extra/pallas_call | solution.py:162
  153.3 1.6 convert_add_fusion.1
  155.0 1.6 collective-permute-start.26
  158.0 1.6 collective-permute-start.11
  159.6 7.9 %collective-permute-done.31 = bf16[4,128,512]{2,1,0:T(8,128)(2,1)S(1)} collective-permute-done((bf16[4,128,512]{2,1,0:T(8,128)(2,1)S(1)}, bf16[4,128,512]{2,1,0:T(8,128)(2,1)S(1)}, u32[]{:S(2)}, u32[]{:S(2)}) %collective-permute-start.31) | collective-permute-done | bytes 524320 | tf_op jit(solution)/shard_map/ppermute | solution.py:195
  167.9 2.7 %collective-permute-start.34 = (bf16[128,512]{1,0:T(8,128)(2,1)S(1)}, bf16[128,512]{1,0:T(8,128)(2,1)S(1)}, u32[]{:S(2)}, u32[]{:S(2)}) collective-permute-start(bf16[128,512]{1,0:T(8,128)(2,1)S(1)} %get-tuple-element.55), channel_id=1, source_target_pairs={{0,12},{1,13},{2,14},{3,15},{4,8},{5,9},{6,10},{7,11},{8,4},{9,5},... | collective-permute-start | bytes 393224 | tf_op jit(solution)/shard_map/ppermute | solution.py:198
  170.6 8.2 %collective-permute-done.26 = bf16[4,128,512]{2,1,0:T(8,128)(2,1)S(1)} collective-permute-done((bf16[4,128,512]{2,1,0:T(8,128)(2,1)S(1)}, bf16[4,128,512]{2,1,0:T(8,128)(2,1)S(1)}, u32[]{:S(2)}, u32[]{:S(2)}) %collective-permute-start.26) | collective-permute-done | bytes 524320 | tf_op jit(solution)/shard_map/ppermute | solution.py:195
  179.8 10.3 %collective-permute-done.16 = bf16[4,128,512]{2,1,0:T(8,128)(2,1)S(1)} collective-permute-done((bf16[4,128,512]{2,1,0:T(8,128)(2,1)S(1)}, bf16[4,128,512]{2,1,0:T(8,128)(2,1)S(1)}, u32[]{:S(2)}, u32[]{:S(2)}) %collective-permute-start.16) | collective-permute-done | bytes 524320 | tf_op jit(solution)/shard_map/ppermute | solution.py:195
  190.3 10.1 %collective-permute-done.11 = bf16[4,128,512]{2,1,0:T(8,128)(2,1)S(1)} collective-permute-done((bf16[4,128,512]{2,1,0:T(8,128)(2,1)S(1)}, bf16[4,128,512]{2,1,0:T(8,128)(2,1)S(1)}, u32[]{:S(2)}, u32[]{:S(2)}) %collective-permute-start.11) | collective-permute-done | bytes 524320 | tf_op jit(solution)/shard_map/ppermute | solution.py:195
  200.4 2.6 %collective-permute-start.29 = (bf16[128,512]{1,0:T(8,128)(2,1)S(1)}, bf16[128,512]{1,0:T(8,128)(2,1)S(1)}, u32[]{:S(2)}, u32[]{:S(2)}) collective-permute-start(bf16[128,512]{1,0:T(8,128)(2,1)S(1)} %get-tuple-element.52), channel_id=1, source_target_pairs={{0,12},{1,13},{2,14},{3,15},{4,8},{5,9},{6,10},{7,11},{8,4},{9,5},... | collective-permute-start | bytes 393224 | tf_op jit(solution)/shard_map/ppermute | solution.py:198
  203.4 1.7 collective-permute-start.17
  205.1 2.6 %collective-permute-start.19 = (bf16[128,512]{1,0:T(8,128)(2,1)S(1)}, bf16[128,512]{1,0:T(8,128)(2,1)S(1)}, u32[]{:S(2)}, u32[]{:S(2)}) collective-permute-start(bf16[128,512]{1,0:T(8,128)(2,1)S(1)} %get-tuple-element.49), channel_id=1, source_target_pairs={{0,12},{1,13},{2,14},{3,15},{4,8},{5,9},{6,10},{7,11},{8,4},{9,5},... | collective-permute-start | bytes 393224 | tf_op jit(solution)/shard_map/ppermute | solution.py:198
  207.9 0.7 collective-permute-done.29
  208.6 1.0 collective-permute-start.12
  209.6 7.6 %collective-permute-done.28 = bf16[128,512]{1,0:T(8,128)(2,1)S(1)} collective-permute-done((bf16[128,512]{1,0:T(8,128)(2,1)S(1)}, bf16[128,512]{1,0:T(8,128)(2,1)S(1)}, u32[]{:S(2)}, u32[]{:S(2)}) %collective-permute-start.28) | collective-permute-done | bytes 131104 | tf_op jit(solution)/shard_map/ppermute | solution.py:198
  217.2 2.7 %collective-permute-start.14 = (bf16[128,512]{1,0:T(8,128)(2,1)S(1)}, bf16[128,512]{1,0:T(8,128)(2,1)S(1)}, u32[]{:S(2)}, u32[]{:S(2)}) collective-permute-start(bf16[128,512]{1,0:T(8,128)(2,1)S(1)} %get-tuple-element.46), channel_id=1, source_target_pairs={{0,12},{1,13},{2,14},{3,15},{4,8},{5,9},{6,10},{7,11},{8,4},{9,5},... | collective-permute-start | bytes 393224 | tf_op jit(solution)/shard_map/ppermute | solution.py:198
  220.0 9.7 %collective-permute-done.18 = bf16[128,512]{1,0:T(8,128)(2,1)S(1)} collective-permute-done((bf16[128,512]{1,0:T(8,128)(2,1)S(1)}, bf16[128,512]{1,0:T(8,128)(2,1)S(1)}, u32[]{:S(2)}, u32[]{:S(2)}) %collective-permute-start.18) | collective-permute-done | bytes 131104 | tf_op jit(solution)/shard_map/ppermute | solution.py:198
  229.9 5.4 %collective-permute-done.13 = bf16[128,512]{1,0:T(8,128)(2,1)S(1)} collective-permute-done((bf16[128,512]{1,0:T(8,128)(2,1)S(1)}, bf16[128,512]{1,0:T(8,128)(2,1)S(1)}, u32[]{:S(2)}, u32[]{:S(2)}) %collective-permute-start.13) | collective-permute-done | bytes 131104 | tf_op jit(solution)/shard_map/ppermute | solution.py:198
  235.3 0.9 pad_maximum_fusion
  (84 shorter events, 8.9 us)
Async XLA Ops:
  0.0 26.4 %collective-permute-start.3 = (bf16[4,128,1024]{2,1,0:T(8,128)(2,1)}, bf16[4,128,1024]{2,1,0:T(8,128)(2,1)S(1)}, u32[]{:S(2)}, u32[]{:S(2)}) collective-permute-start(bf16[4,128,1024]{2,1,0:T(8,128)(2,1)} %hidden_ref.1), channel_id=1, source_target_pairs={{0,4},{1,5},{2,6},{3,7},{4,0},{5,1},{6,2},{7,3},{8,12},{9,13},{10,... | collective-permute-start | bytes 3145736 | tf_op jit(solution)/shard_map/ppermute | solution.py:198
  3.0 25.9 %collective-permute-start.4 = (bf16[4,128,1024]{2,1,0:T(8,128)(2,1)}, bf16[4,128,1024]{2,1,0:T(8,128)(2,1)S(1)}, u32[]{:S(2)}, u32[]{:S(2)}) collective-permute-start(bf16[4,128,1024]{2,1,0:T(8,128)(2,1)} %hidden_ref.1), channel_id=1, source_target_pairs={{4,8},{5,9},{6,10},{7,11},{8,4},{9,5},{10,6},{11,7},{20,24},{21,25... | collective-permute-start | bytes 3145736 | tf_op jit(solution)/shard_map/ppermute | solution.py:202
  27.4 11.6 %collective-permute-start.21 = (bf16[2,128,1024]{2,1,0:T(8,128)(2,1)}, bf16[2,128,1024]{2,1,0:T(8,128)(2,1)}, u32[]{:S(2)}, u32[]{:S(2)}) collective-permute-start(bf16[2,128,1024]{2,1,0:T(8,128)(2,1)} %get-tuple-element.42.refs_1_), channel_id=1, source_target_pairs={{4,8},{5,9},{6,10},{7,11},{8,4},{9,5},{10,6},{11,7},{20,24},{21,25... | collective-permute-start | bytes 1572872 | tf_op jit(solution)/shard_map/ppermute | solution.py:202
  28.9 1.0 copy-start.4
  30.7 16.4 %collective-permute-start.5 = (bf16[2,128,1024]{2,1,0:T(8,128)(2,1)}, bf16[2,128,1024]{2,1,0:T(8,128)(2,1)}, u32[]{:S(2)}, u32[]{:S(2)}) collective-permute-start(bf16[2,128,1024]{2,1,0:T(8,128)(2,1)} %slice.157), channel_id=1, source_target_pairs={{4,0},{5,1},{6,2},{7,3},{8,12},{9,13},{10,14},{11,15},{20,16},{21,... | collective-permute-start | bytes 1572872 | tf_op jit(solution)/shard_map/ppermute | solution.py:202
  32.1 6.7 %copy-start.6 = (s32[128]{0:T(128)S(1)}, s32[128]{0:T(128)}, u32[]{:S(2)}) copy-start(s32[128]{0:T(128)} %param.10) | copy-start | bytes 1540
  32.1 6.7 %copy-start.7 = (s32[128]{0:T(128)S(1)}, s32[128]{0:T(128)}, u32[]{:S(2)}) copy-start(s32[128]{0:T(128)} %param.11) | copy-start | bytes 1540
  36.9 13.2 %copy-start.2 = (bf16[4,128,1024]{2,1,0:T(8,128)(2,1)S(1)}, bf16[4,128,1024]{2,1,0:T(8,128)(2,1)}, u32[]{:S(2)}) copy-start(bf16[4,128,1024]{2,1,0:T(8,128)(2,1)} %hidden_ref.1) | copy-start | bytes 3145732
  36.9 32.4 %collective-permute-start = (bf16[4,128,1024]{2,1,0:T(8,128)(2,1)}, bf16[4,128,1024]{2,1,0:T(8,128)(2,1)S(1)}, u32[]{:S(2)}, u32[]{:S(2)}) collective-permute-start(bf16[4,128,1024]{2,1,0:T(8,128)(2,1)} %get-tuple-element.18), channel_id=1, source_target_pairs={{0,1},{1,0},{2,3},{3,2},{4,5},{5,4},{6,7},{7,6},{8,9},{9,8},{10,11... | collective-permute-start | bytes 3145736 | tf_op jit(solution)/shard_map/ppermute | solution.py:195
  36.9 32.4 %collective-permute-start.1 = (bf16[4,128,1024]{2,1,0:T(8,128)(2,1)}, bf16[4,128,1024]{2,1,0:T(8,128)(2,1)S(1)}, u32[]{:S(2)}, u32[]{:S(2)}) collective-permute-start(bf16[4,128,1024]{2,1,0:T(8,128)(2,1)} %get-tuple-element.19), channel_id=1, source_target_pairs={{0,2},{1,3},{2,0},{3,1},{4,6},{5,7},{6,4},{7,5},{8,10},{9,11},{10,... | collective-permute-start | bytes 3145736 | tf_op jit(solution)/shard_map/ppermute | solution.py:195
  38.6 46.1 %collective-permute-start.2 = (bf16[4,128,1024]{2,1,0:T(8,128)(2,1)}, bf16[4,128,1024]{2,1,0:T(8,128)(2,1)}, u32[]{:S(2)}, u32[]{:S(2)}) collective-permute-start(bf16[4,128,1024]{2,1,0:T(8,128)(2,1)} %get-tuple-element.20), channel_id=1, source_target_pairs={{0,3},{1,2},{2,1},{3,0},{4,7},{5,6},{6,5},{7,4},{8,11},{9,10},{10,... | collective-permute-start | bytes 3145736 | tf_op jit(solution)/shard_map/ppermute | solution.py:195
  39.0 19.4 %copy-start.3 = (bf16[2,128,1024]{2,1,0:T(8,128)(2,1)S(1)}, bf16[2,128,1024]{2,1,0:T(8,128)(2,1)}, u32[]{:S(2)}) copy-start(bf16[2,128,1024]{2,1,0:T(8,128)(2,1)} %get-tuple-element.41.refs_1_) | copy-start | bytes 1572868
  39.0 19.4 %collective-permute-start.22 = (bf16[2,128,1024]{2,1,0:T(8,128)(2,1)}, bf16[2,128,1024]{2,1,0:T(8,128)(2,1)S(1)}, u32[]{:S(2)}, u32[]{:S(2)}) collective-permute-start(bf16[2,128,1024]{2,1,0:T(8,128)(2,1)} %collective-permute-done.21), channel_id=1, source_target_pairs={{4,0},{5,1},{6,2},{7,3},{8,12},{9,13},{10,14},{11,15},{20,16},{21,... | collective-permute-start | bytes 1572872 | tf_op jit(solution)/shard_map/ppermute | solution.py:202
  48.6 20.6 %copy-start.5 = (bf16[4,128,1024]{2,1,0:T(8,128)(2,1)S(1)}, bf16[4,128,1024]{2,1,0:T(8,128)(2,1)}, u32[]{:S(2)}) copy-start(bf16[4,128,1024]{2,1,0:T(8,128)(2,1)} %copy-done.4) | copy-start | bytes 3145732
  48.6 20.6 %collective-permute-start.20 = (bf16[2,128,1024]{2,1,0:T(8,128)(2,1)S(1)}, bf16[2,128,1024]{2,1,0:T(8,128)(2,1)S(1)}, u32[]{:S(2)}, u32[]{:S(2)}) collective-permute-start(bf16[2,128,1024]{2,1,0:T(8,128)(2,1)S(1)} %get-tuple-element.40), channel_id=1, source_target_pairs={{4,0},{5,1},{6,2},{7,3},{8,12},{9,13},{10,14},{11,15},{20,16},{21,... | collective-permute-start | bytes 1572872 | tf_op jit(solution)/shard_map/ppermute | solution.py:202
  58.4 56.0 %collective-permute-start.6 = (bf16[2,128,1024]{2,1,0:T(8,128)(2,1)S(1)}, bf16[2,128,1024]{2,1,0:T(8,128)(2,1)S(1)}, u32[]{:S(2)}, u32[]{:S(2)}) collective-permute-start(bf16[2,128,1024]{2,1,0:T(8,128)(2,1)S(1)} %copy-done.3), channel_id=1, source_target_pairs={{4,8},{5,9},{6,10},{7,11},{8,4},{9,5},{10,6},{11,7},{20,24},{21,25... | collective-permute-start | bytes 1572872 | tf_op jit(solution)/shard_map/ppermute | solution.py:202
  90.4 1.2 collective-permute-start.23
  91.7 18.3 %copy-start = (bf16[8,16,8192]{2,1,0:T(8,128)(2,1)S(1)}, bf16[8,16,8192]{2,1,0:T(8,128)(2,1)}, u32[]{:S(2)}) copy-start(bf16[8,16,8192]{2,1,0:T(8,128)(2,1)} %param.9) | copy-start | bytes 6291460
  91.7 18.3 %collective-permute-start.24 = (f32[16,256]{1,0:T(8,128)S(1)}, f32[16,256]{1,0:T(8,128)S(1)}, u32[]{:S(2)}, u32[]{:S(2)}) collective-permute-start(f32[16,256]{1,0:T(8,128)S(1)} %add.90), channel_id=1, source_target_pairs={{0,2},{1,3},{2,0},{3,1},{4,6},{5,7},{6,4},{7,5},{8,10},{9,11},{10,... | collective-permute-start | bytes 49160 | tf_op jit(solution)/shard_map/ppermute | solution.py:195
  107.9 2.1 copy-start.1
  114.3 38.0 %collective-permute-start.30 = (bf16[2,4,128,512]{3,2,1,0:T(8,128)(2,1)S(1)}, bf16[2,4,128,512]{3,2,1,0:T(8,128)(2,1)S(1)}, u32[]{:S(2)}, u32[]{:S(2)}) collective-permute-start(bf16[2,4,128,512]{3,2,1,0:T(8,128)(2,1)S(1)} %get-tuple-element.30), channel_id=1, source_target_pairs={{0,1},{1,0},{2,3},{3,2},{4,5},{5,4},{6,7},{7,6},{8,9},{9,8},{10,11... | collective-permute-start | bytes 3145736 | tf_op jit(solution)/shard_map/ppermute | solution.py:195
  114.4 18.2 %collective-permute-start.7 = (bf16[2,128,1024]{2,1,0:T(8,128)(2,1)S(1)}, bf16[2,128,1024]{2,1,0:T(8,128)(2,1)S(1)}, u32[]{:S(2)}, u32[]{:S(2)}) collective-permute-start(bf16[2,128,1024]{2,1,0:T(8,128)(2,1)S(1)} %collective-permute-done.6), channel_id=1, source_target_pairs={{4,0},{5,1},{6,2},{7,3},{8,12},{9,13},{10,14},{11,15},{20,16},{21,... | collective-permute-start | bytes 1572872 | tf_op jit(solution)/shard_map/ppermute | solution.py:202
  120.7 32.6 %collective-permute-start.25 = (bf16[2,4,128,512]{3,2,1,0:T(8,128)(2,1)}, bf16[2,4,128,512]{3,2,1,0:T(8,128)(2,1)}, u32[]{:S(2)}, u32[]{:S(2)}) collective-permute-start(bf16[2,4,128,512]{3,2,1,0:T(8,128)(2,1)} %get-tuple-element.28), channel_id=1, source_target_pairs={{0,1},{1,0},{2,3},{3,2},{4,5},{5,4},{6,7},{7,6},{8,9},{9,8},{10,11... | collective-permute-start | bytes 3145736 | tf_op jit(solution)/shard_map/ppermute | solution.py:195
  138.1 1.2 collective-permute-start.8
  139.3 3.7 %collective-permute-start.9 = (f32[16,256]{1,0:T(8,128)S(1)}, f32[16,256]{1,0:T(8,128)S(1)}, u32[]{:S(2)}, u32[]{:S(2)}) collective-permute-start(f32[16,256]{1,0:T(8,128)S(1)} %add.78), channel_id=1, source_target_pairs={{0,2},{1,3},{2,0},{3,1},{4,6},{5,7},{6,4},{7,5},{8,10},{9,11},{10,... | collective-permute-start | bytes 49160 | tf_op jit(solution)/shard_map/ppermute | solution.py:195
  151.7 4.9 %collective-permute-start.15 = (bf16[2,4,128,512]{3,2,1,0:T(8,128)(2,1)S(1)}, bf16[2,4,128,512]{3,2,1,0:T(8,128)(2,1)S(1)}, u32[]{:S(2)}, u32[]{:S(2)}) collective-permute-start(bf16[2,4,128,512]{3,2,1,0:T(8,128)(2,1)S(1)} %get-tuple-element.26), channel_id=1, source_target_pairs={{0,1},{1,0},{2,3},{3,2},{4,5},{5,4},{6,7},{7,6},{8,9},{9,8},{10,11... | collective-permute-start | bytes 3145736 | tf_op jit(solution)/shard_map/ppermute | solution.py:195
  151.8 5.9 %collective-permute-start.10 = (bf16[2,4,128,512]{3,2,1,0:T(8,128)(2,1)S(1)}, bf16[2,4,128,512]{3,2,1,0:T(8,128)(2,1)S(1)}, u32[]{:S(2)}, u32[]{:S(2)}) collective-permute-start(bf16[2,4,128,512]{3,2,1,0:T(8,128)(2,1)S(1)} %get-tuple-element.24), channel_id=1, source_target_pairs={{0,1},{1,0},{2,3},{3,2},{4,5},{5,4},{6,7},{7,6},{8,9},{9,8},{10,11... | collective-permute-start | bytes 3145736 | tf_op jit(solution)/shard_map/ppermute | solution.py:195
  152.7 14.8 %collective-permute-start.31 = (bf16[4,128,512]{2,1,0:T(8,128)(2,1)S(1)}, bf16[4,128,512]{2,1,0:T(8,128)(2,1)S(1)}, u32[]{:S(2)}, u32[]{:S(2)}) collective-permute-start(bf16[4,128,512]{2,1,0:T(8,128)(2,1)S(1)} %fusion.7), channel_id=1, source_target_pairs={{0,2},{1,3},{2,0},{3,1},{4,6},{5,7},{6,4},{7,5},{8,10},{9,11},{10,... | collective-permute-start | bytes 1572872 | tf_op jit(solution)/shard_map/ppermute | solution.py:195
  155.0 23.8 %collective-permute-start.26 = (bf16[4,128,512]{2,1,0:T(8,128)(2,1)S(1)}, bf16[4,128,512]{2,1,0:T(8,128)(2,1)S(1)}, u32[]{:S(2)}, u32[]{:S(2)}) collective-permute-start(bf16[4,128,512]{2,1,0:T(8,128)(2,1)S(1)} %fusion.6), channel_id=1, source_target_pairs={{0,2},{1,3},{2,0},{3,1},{4,6},{5,7},{6,4},{7,5},{8,10},{9,11},{10,... | collective-permute-start | bytes 1572872 | tf_op jit(solution)/shard_map/ppermute | solution.py:195
  157.1 33.0 %collective-permute-start.16 = (bf16[4,128,512]{2,1,0:T(8,128)(2,1)S(1)}, bf16[4,128,512]{2,1,0:T(8,128)(2,1)S(1)}, u32[]{:S(2)}, u32[]{:S(2)}) collective-permute-start(bf16[4,128,512]{2,1,0:T(8,128)(2,1)S(1)} %fusion.5), channel_id=1, source_target_pairs={{0,2},{1,3},{2,0},{3,1},{4,6},{5,7},{6,4},{7,5},{8,10},{9,11},{10,... | collective-permute-start | bytes 1572872 | tf_op jit(solution)/shard_map/ppermute | solution.py:195
  158.0 42.4 %collective-permute-start.11 = (bf16[4,128,512]{2,1,0:T(8,128)(2,1)S(1)}, bf16[4,128,512]{2,1,0:T(8,128)(2,1)S(1)}, u32[]{:S(2)}, u32[]{:S(2)}) collective-permute-start(bf16[4,128,512]{2,1,0:T(8,128)(2,1)S(1)} %fusion.4), channel_id=1, source_target_pairs={{0,2},{1,3},{2,0},{3,1},{4,6},{5,7},{6,4},{7,5},{8,10},{9,11},{10,... | collective-permute-start | bytes 1572872 | tf_op jit(solution)/shard_map/ppermute | solution.py:195
  167.8 35.5 %collective-permute-start.32 = (bf16[128,512]{1,0:T(8,128)(2,1)S(1)}, bf16[128,512]{1,0:T(8,128)(2,1)S(1)}, u32[]{:S(2)}, u32[]{:S(2)}) collective-permute-start(bf16[128,512]{1,0:T(8,128)(2,1)S(1)} %get-tuple-element.54), channel_id=1, source_target_pairs={{0,4},{1,5},{2,6},{3,7},{4,0},{5,1},{6,2},{7,3},{8,12},{9,13},{10,... | collective-permute-start | bytes 393224 | tf_op jit(solution)/shard_map/ppermute | solution.py:198
  167.9 35.5 %collective-permute-start.34 = (bf16[128,512]{1,0:T(8,128)(2,1)S(1)}, bf16[128,512]{1,0:T(8,128)(2,1)S(1)}, u32[]{:S(2)}, u32[]{:S(2)}) collective-permute-start(bf16[128,512]{1,0:T(8,128)(2,1)S(1)} %get-tuple-element.55), channel_id=1, source_target_pairs={{0,12},{1,13},{2,14},{3,15},{4,8},{5,9},{6,10},{7,11},{8,4},{9,5},... | collective-permute-start | bytes 393224 | tf_op jit(solution)/shard_map/ppermute | solution.py:198
  178.8 26.3 %collective-permute-start.33 = (bf16[128,512]{1,0:T(8,128)(2,1)S(1)}, bf16[128,512]{1,0:T(8,128)(2,1)S(1)}, u32[]{:S(2)}, u32[]{:S(2)}) collective-permute-start(bf16[128,512]{1,0:T(8,128)(2,1)S(1)} %get-tuple-element.56), channel_id=1, source_target_pairs={{0,8},{1,9},{2,10},{3,11},{4,12},{5,13},{6,14},{7,15},{8,0},{9,1},... | collective-permute-start | bytes 393224 | tf_op jit(solution)/shard_map/ppermute | solution.py:198
  190.0 17.8 %collective-permute-start.27 = (bf16[128,512]{1,0:T(8,128)(2,1)S(1)}, bf16[128,512]{1,0:T(8,128)(2,1)S(1)}, u32[]{:S(2)}, u32[]{:S(2)}) collective-permute-start(bf16[128,512]{1,0:T(8,128)(2,1)S(1)} %get-tuple-element.51), channel_id=1, source_target_pairs={{0,4},{1,5},{2,6},{3,7},{4,0},{5,1},{6,2},{7,3},{8,12},{9,13},{10,... | collective-permute-start | bytes 393224 | tf_op jit(solution)/shard_map/ppermute | solution.py:198
  200.4 8.2 %collective-permute-start.29 = (bf16[128,512]{1,0:T(8,128)(2,1)S(1)}, bf16[128,512]{1,0:T(8,128)(2,1)S(1)}, u32[]{:S(2)}, u32[]{:S(2)}) collective-permute-start(bf16[128,512]{1,0:T(8,128)(2,1)S(1)} %get-tuple-element.52), channel_id=1, source_target_pairs={{0,12},{1,13},{2,14},{3,15},{4,8},{5,9},{6,10},{7,11},{8,4},{9,5},... | collective-permute-start | bytes 393224 | tf_op jit(solution)/shard_map/ppermute | solution.py:198
  203.3 13.9 %collective-permute-start.28 = (bf16[128,512]{1,0:T(8,128)(2,1)S(1)}, bf16[128,512]{1,0:T(8,128)(2,1)S(1)}, u32[]{:S(2)}, u32[]{:S(2)}) collective-permute-start(bf16[128,512]{1,0:T(8,128)(2,1)S(1)} %get-tuple-element.53), channel_id=1, source_target_pairs={{0,8},{1,9},{2,10},{3,11},{4,12},{5,13},{6,14},{7,15},{8,0},{9,1},... | collective-permute-start | bytes 393224 | tf_op jit(solution)/shard_map/ppermute | solution.py:198
  203.4 16.6 %collective-permute-start.17 = (bf16[128,512]{1,0:T(8,128)(2,1)S(1)}, bf16[128,512]{1,0:T(8,128)(2,1)S(1)}, u32[]{:S(2)}, u32[]{:S(2)}) collective-permute-start(bf16[128,512]{1,0:T(8,128)(2,1)S(1)} %get-tuple-element.48), channel_id=1, source_target_pairs={{0,4},{1,5},{2,6},{3,7},{4,0},{5,1},{6,2},{7,3},{8,12},{9,13},{10,... | collective-permute-start | bytes 393224 | tf_op jit(solution)/shard_map/ppermute | solution.py:198
  205.1 14.9 %collective-permute-start.19 = (bf16[128,512]{1,0:T(8,128)(2,1)S(1)}, bf16[128,512]{1,0:T(8,128)(2,1)S(1)}, u32[]{:S(2)}, u32[]{:S(2)}) collective-permute-start(bf16[128,512]{1,0:T(8,128)(2,1)S(1)} %get-tuple-element.49), channel_id=1, source_target_pairs={{0,12},{1,13},{2,14},{3,15},{4,8},{5,9},{6,10},{7,11},{8,4},{9,5},... | collective-permute-start | bytes 393224 | tf_op jit(solution)/shard_map/ppermute | solution.py:198
  207.8 21.9 %collective-permute-start.18 = (bf16[128,512]{1,0:T(8,128)(2,1)S(1)}, bf16[128,512]{1,0:T(8,128)(2,1)S(1)}, u32[]{:S(2)}, u32[]{:S(2)}) collective-permute-start(bf16[128,512]{1,0:T(8,128)(2,1)S(1)} %get-tuple-element.50), channel_id=1, source_target_pairs={{0,8},{1,9},{2,10},{3,11},{4,12},{5,13},{6,14},{7,15},{8,0},{9,1},... | collective-permute-start | bytes 393224 | tf_op jit(solution)/shard_map/ppermute | solution.py:198
  208.6 21.2 %collective-permute-start.12 = (bf16[128,512]{1,0:T(8,128)(2,1)S(1)}, bf16[128,512]{1,0:T(8,128)(2,1)S(1)}, u32[]{:S(2)}, u32[]{:S(2)}) collective-permute-start(bf16[128,512]{1,0:T(8,128)(2,1)S(1)} %get-tuple-element.45), channel_id=1, source_target_pairs={{0,4},{1,5},{2,6},{3,7},{4,0},{5,1},{6,2},{7,3},{8,12},{9,13},{10,... | collective-permute-start | bytes 393224 | tf_op jit(solution)/shard_map/ppermute | solution.py:198
  217.2 12.7 %collective-permute-start.14 = (bf16[128,512]{1,0:T(8,128)(2,1)S(1)}, bf16[128,512]{1,0:T(8,128)(2,1)S(1)}, u32[]{:S(2)}, u32[]{:S(2)}) collective-permute-start(bf16[128,512]{1,0:T(8,128)(2,1)S(1)} %get-tuple-element.46), channel_id=1, source_target_pairs={{0,12},{1,13},{2,14},{3,15},{4,8},{5,9},{6,10},{7,11},{8,4},{9,5},... | collective-permute-start | bytes 393224 | tf_op jit(solution)/shard_map/ppermute | solution.py:198
  220.0 15.3 %collective-permute-start.13 = (bf16[128,512]{1,0:T(8,128)(2,1)S(1)}, bf16[128,512]{1,0:T(8,128)(2,1)S(1)}, u32[]{:S(2)}, u32[]{:S(2)}) collective-permute-start(bf16[128,512]{1,0:T(8,128)(2,1)S(1)} %get-tuple-element.47), channel_id=1, source_target_pairs={{0,8},{1,9},{2,10},{3,11},{4,12},{5,13},{6,14},{7,15},{8,0},{9,1},... | collective-permute-start | bytes 393224 | tf_op jit(solution)/shard_map/ppermute | solution.py:198

commit v2 on v1

v2 whole, which is shorter than its diff:
```python
import jax
import jax.numpy as jnp
from jax import lax
from jax.experimental import pallas as pl
from jax.experimental.pallas import tpu as pltpu
from jax.sharding import PartitionSpec as P

PLANE = 4
F32 = jnp.float32
BF16 = jnp.bfloat16
VMEM_BYTES = 48 * 1024 * 1024
LOW_CHUNKS = ((0, 2), (2, 4))
SUM_CHUNKS = ((0, 2), (2, 3), (3, 4))


def halving(i, planes):
    out, bit = 0, 1
    while bit < planes:
        out = out * 2 + ((i // bit) % 2)
        bit *= 2
    return out


def after(value, *others):
    return lax.optimization_barrier((value, *others))[0]


def cost(flops, moved):
    return pl.CostEstimate(flops=int(flops) // 1000, bytes_accessed=int(moved) // 1000, transcendentals=0)


def hbm(*values):
    return [pltpu.with_memory_space_constraint(value, pltpu.HBM) for value in values]


def params():
    return pltpu.CompilerParams(vmem_limit_bytes=VMEM_BYTES)


def pack_factors(place, order, table, width, others, first, last):
    rows = table.shape[0]
    count = len(others)
    planes = last - first

    def body(place_ref, order_ref, *refs):
        for i in range(count):
            refs[count + i][0] = refs[i][...]

    def columns(other):
        return lambda i, p, o: (0, o[first + i] * PLANE + (p[1] ^ other))

    return pl.pallas_call(
        body,
        grid_spec=pltpu.PrefetchScalarGridSpec(
            num_scalar_prefetch=2,
            grid=(planes,),
            in_specs=[pl.BlockSpec((rows, width), columns(o)) for o in others],
            out_specs=[pl.BlockSpec((1, rows, width), lambda i, p, o: (i, 0, 0))] * count,
        ),
        out_shape=[jax.ShapeDtypeStruct((planes, rows, width), BF16)] * count,
        cost_estimate=cost(0, 4 * count * planes * rows * width),
        compiler_params=params(),
        name="pack_factors",
    )(place, order, *hbm(*([table] * count)))


def pack_core(place, order, first, second, width):
    rows, units = first.shape[0], 2 * width
    planes = first.shape[1] // (PLANE * units)

    def body(place_ref, order_ref, a_ref, s0_ref, s1_ref, out_ref):
        out_ref[0, 0] = a_ref[...]
        out_ref[1, 0, :, :width] = s0_ref[...]
        out_ref[1, 0, :, width:] = s1_ref[...]

    def columns(side):
        return lambda i, p, o: (
            0,
            (p[0] ^ halving(i, planes)) * PLANE + (p[1] ^ 1 ^ (2 * side)),
        )

    return pl.pallas_call(
        body,
        grid_spec=pltpu.PrefetchScalarGridSpec(
            num_scalar_prefetch=2,
            grid=(planes,),
            in_specs=[pl.BlockSpec((rows, units), lambda i, p, o: (0, o[i] * PLANE + (p[1] ^ 1)))]
            + [pl.BlockSpec((rows, width), columns(side)) for side in (0, 1)],
            out_specs=pl.BlockSpec((2, 1, rows, units), lambda i, p, o: (0, i, 0, 0)),
        ),
        out_shape=jax.ShapeDtypeStruct((2, planes, rows, units), BF16),
        cost_estimate=cost(0, 8 * planes * rows * units),
        compiler_params=params(),
        name="pack_core",
    )(place, order, *hbm(first, second, second))


def base_blocks(place, hidden, down, planes, width):
    steps, rows, units = hidden.shape

    def body(place_ref, hidden_ref, d0, d1, d2, d3, send_ref, keep_ref):
        flat = hidden_ref[...].reshape(steps * rows, units)
        for i, ref in enumerate((d0, d1, d2, d3)):
            value = jnp.dot(flat, ref[...], preferred_element_type=F32).reshape(steps, rows, width)
            if i & 1:
                send_ref[i >> 1, 0] = value.astype(BF16)
            else:
                keep_ref[i >> 1, 0] = value

    def columns(other):
        return lambda i, p: (0, (p[0] ^ halving(i, planes)) * PLANE + (p[1] ^ other))

    shape = (2, planes, steps, rows, width)
    return pl.pallas_call(
        body,
        grid_spec=pltpu.PrefetchScalarGridSpec(
            num_scalar_prefetch=1,
            grid=(planes,),
            in_specs=[pl.BlockSpec((steps, rows, units), lambda i, p: (0, 0, 0))]
            + [pl.BlockSpec((units, width), columns(o)) for o in range(PLANE)],
            out_specs=[pl.BlockSpec((2, 1, steps, rows, width), lambda i, p: (0, i, 0, 0, 0))] * 2,
        ),
        out_shape=[jax.ShapeDtypeStruct(shape, BF16), jax.ShapeDtypeStruct(shape, F32)],
        cost_estimate=cost(
            2 * steps * rows * units * down.shape[1], (2 * units + 3 * steps * rows) * down.shape[1]
        ),
        compiler_params=params(),
        name="base_blocks",
    )(place, *hbm(hidden, down, down, down, down))


def low_part(place, order, slots, tables, sources, first_plane, chunk, per_shard, rank):
    planes = len(sources)
    first_step, last_step = chunk
    steps = last_step - first_step
    rows, (_, requests, width) = tables[-1].shape[-2], sources[0][0].shape
    lanes = steps * requests
    hidden = [array for source in sources for array in source]

    def body(place_ref, order_ref, slots_ref, *refs):
        factor_refs, hidden_refs = refs[:PLANE], refs[PLANE : PLANE + len(hidden)]
        out_ref, held, factors, total = refs[PLANE + len(hidden) :]
        j = pl.program_id(0)
        at = 0
        for i, source in enumerate(sources):
            for inner in range(len(source)):
                chosen = j == i
                if len(source) > 1:
                    chosen &= place_ref[2] == 1 - inner

                @pl.when(chosen)
                def _(ref=hidden_refs[at]):
                    held[...] = ref[...].reshape(lanes, width)

                at += 1

        @pl.when(j == 0)
        def _():
            total[...] = jnp.zeros_like(total)

        for i, ref in enumerate(factor_refs):
            factors[i * rows : (i + 1) * rows, :] = ref[...].reshape(rows, width)
        total[...] += lax.dot_general(
            factors[...], held[...], (((1,), (1,)), ((), ())), preferred_element_type=F32
        )

        @pl.when(j == planes - 1)
        def _():
            low = jnp.zeros((rank, lanes), F32)
            wanted = slots_ref[...]
            for i in range(PLANE):
                first = (place_ref[0] * PLANE + (place_ref[1] ^ i)) * per_shard
                for a in range(per_shard):
                    at = (i * per_shard + a) * rank
                    low += jnp.where(wanted == first + a, total[at : at + rank, :], 0.0)
            out_ref[...] = low

    def hidden_spec(array):
        block = first_step // steps if array.shape[0] > steps else 0
        return pl.BlockSpec((steps, requests, width), lambda j, p, o: (block, 0, 0))

    return pl.pallas_call(
        body,
        grid_spec=pltpu.PrefetchScalarGridSpec(
            num_scalar_prefetch=2,
            grid=(planes,),
            in_specs=[
                pl.BlockSpec((1, lanes), lambda j, p, o: (0, 0)),
                pl.BlockSpec((rows, width), lambda j, p, o: (0, o[first_plane + j] * PLANE + p[1])),
                pl.BlockSpec((1, 1, rows, width), lambda j, p, o: (0, first_plane + j, 0, 0)),
                pl.BlockSpec((1, rows, width), lambda j, p, o: (j, 0, 0)),
                pl.BlockSpec((1, rows, width), lambda j, p, o: (j, 0, 0)),
                *[hidden_spec(array) for array in hidden],
            ],
            out_specs=pl.BlockSpec((rank, lanes), lambda j, p, o: (0, 0)),
            scratch_shapes=[
                pltpu.VMEM((lanes, width), BF16),
                pltpu.VMEM((PLANE * rows, width), BF16),
                pltpu.VMEM((PLANE * rows, lanes), F32),
            ],
        ),
        out_shape=jax.ShapeDtypeStruct((rank, lanes), F32),
        cost_estimate=cost(
            2 * lanes * PLANE * rows * planes * width, 2 * (lanes + PLANE * rows) * planes * width
        ),
        compiler_params=params(),
        name="low_part",
    )(place, order, slots, *hbm(*tables, *hidden))


def add_extra(place, low, slots, mine, other, keep, recv, chunk, side, per_shard, rank):
    _, planes, _, requests, width = keep.shape
    first_step, last_step = chunk
    steps = last_step - first_step
    lanes = steps * requests
    rows = mine.shape[0]
    kind = BF16 if side else F32

    def body(place_ref, low_ref, slots_ref, *refs):
        tables, (t_ref, k_ref, r_ref, out_ref) = refs[:planes], refs[planes:]
        rounded = low_ref[...].astype(BF16).astype(F32)
        wanted = slots_ref[...]
        spread = []
        for i in range(2):
            first = (place_ref[0] * PLANE + (place_ref[1] ^ i)) * per_shard
            parts = [jnp.where(wanted == first + a, rounded, 0.0) for a in range(per_shard)]
            spread.append(jnp.concatenate(parts, axis=0).T.astype(BF16))
        for i in range(planes):
            extra = jnp.dot(spread[0], tables[i][...], preferred_element_type=F32)
            extra += jnp.dot(spread[1], t_ref[0, i], preferred_element_type=F32)
            base = k_ref[0, i] + r_ref[0, i].astype(F32)
            out_ref[i] = (base.reshape(lanes, width) + extra).astype(kind)

    def columns(i):
        return lambda j, p: (0, (p[0] ^ halving(i, planes)) * PLANE + (p[1] ^ (2 * side)))

    blocks = [pl.BlockSpec((rows, width), columns(i)) for i in range(planes)]
    base = pl.BlockSpec(
        (1, planes, steps, requests, width), lambda i, p: (side, 0, first_step // steps, 0, 0)
    )
    return pl.pallas_call(
        body,
        grid_spec=pltpu.PrefetchScalarGridSpec(
            num_scalar_prefetch=1,
            grid=(1,),
            in_specs=[
                pl.BlockSpec((rank, lanes), lambda i, p: (0, 0)),
                pl.BlockSpec((1, lanes), lambda i, p: (0, 0)),
                *blocks,
                pl.BlockSpec((1, planes, rows, width), lambda i, p: (1, 0, 0, side)),
                base,
                base,
            ],
            out_specs=pl.BlockSpec((planes, lanes, width), lambda i, p: (0, 0, 0)),
        ),
        out_shape=jax.ShapeDtypeStruct((planes, lanes, width), kind),
        cost_estimate=cost(4 * lanes * rows * planes * width, 10 * lanes * planes * width),
        compiler_params=params(),
        name="add_extra",
    )(place, low, slots, *hbm(*([mine] * planes), other, keep, recv))


def local(hidden, down_matrix, first_table, second_table, storage_index, request_adapter):
    steps, requests, units = hidden.shape
    per_shard, rank, all_units = first_table.shape
    features = second_table.shape[2]
    adapters = storage_index.shape[0]
    devices = all_units // units
    planes = devices // PLANE
    width = features // devices
    me = lax.axis_index("tensor").astype(jnp.int32)
    z, w = me // PLANE, me % PLANE
    place = jnp.stack([z, w, ((z == 1) | (z == 2)).astype(jnp.int32)])

    def in_plane(value, other):
        return lax.ppermute(value, "tensor", [(t, t ^ other) for t in range(devices)])

    def along(value, other):
        return lax.ppermute(value, "tensor", [(t, t ^ (other * PLANE)) for t in range(devices)])

    def hop(value, moves):
        pairs = [(a * PLANE + v, b * PLANE + v) for a, b in moves for v in range(PLANE)]
        return lax.ppermute(value, "tensor", pairs)

    table = jnp.arange(adapters, dtype=jnp.int32)
    slot_row = jnp.sum(
        jnp.where(request_adapter[:, None] == table[None, :], storage_index[None, :], 0), axis=1
    ).astype(jnp.int32)

    first = first_table.reshape(per_shard * rank, all_units)
    second = second_table.reshape(per_shard * rank, features)

    if planes == 4:
        order = jnp.stack([z, z ^ 1, jnp.where(z < 2, 2, 1), jnp.where(z < 2, 3, 0)])
    else:
        order = jnp.stack([z ^ o for o in range(planes)])
    split = planes // 2

    for_y = pack_factors(place, order, first, units, (2, 3), 0, split)
    near_y = [in_plane(block, o) for block, o in zip(for_y, (2, 3))]
    hidden_z = after(hidden, *for_y)
    if planes == 4:
        near = along(hidden_z, 1)
        middle = hop(hidden_z, ((1, 2), (2, 1)))
    else:
        blocks = [hidden] + [along(hidden_z, o) for o in range(1, planes)]
        near = middle = blocks[1]
    for_far = pack_factors(place, order, after(first, *for_y), units, (2, 3), split, planes)
    for_core = pack_core(place, order, after(first, *for_far), second, width)
    send, keep = base_blocks(place, after(hidden, for_core), down_matrix, planes, width)
    near, middle, send, *near_y = lax.optimization_barrier((near, middle, send, *near_y))
    from_core = in_plane(after(for_core, near), 1)
    far_y = [in_plane(after(for_far[0], *near_y), 2)]
    far_y.append(in_plane(after(for_far[1], *far_y), 3))

    if planes == 4:
        gathered = []
        near_rest, middle_rest = near, middle
        for a, b in LOW_CHUNKS:
            outer_one = hop(middle_rest[a:b], ((1, 0), (2, 3)))
            middle_two = hop(near_rest[a:b], ((1, 2), (2, 1)))
            ready = after(middle_two, outer_one, far_y[0])
            if a == 0:
                recv = in_plane(after(send, outer_one, middle_two), 1)
            outer_two = hop(ready, ((1, 0), (2, 3)))
            near_rest = after(near, middle_two)
            middle_rest = after(middle, outer_two, *far_y)
            gathered.append([[middle, outer_one], [middle_two, outer_two]])
        second_wave = [source[1] for source in gathered[1]]
    else:
        gathered = [[[block] for block in blocks[split:]] for _ in LOW_CHUNKS]
        recv = in_plane(send, 1)
        second_wave = []
    at_hand = [[hidden], [near]] if planes == 4 else [[block] for block in blocks[:split]]
    slots = jnp.tile(slot_row[None, :], (1, steps))
    early = low_part(
        place, order, slots, (first, from_core, *near_y), at_hand, 0, (0, steps), per_shard, rank
    )

    def low_of(chunk, sources, token):
        a, b = chunk
        tables = (first, after(from_core, early, *token), *far_y)
        sources = [[after(array, *token) for array in source] for source in sources]
        low = low_part(
            place, order, slots[:, a * requests : b * requests], tables, sources, split, chunk, per_shard, rank
        )
        low = low + early[:, a * requests : b * requests]
        low = low + in_plane(low, 1)
        return low + in_plane(low, 2)

    def blocks_of(low, low_chunk, chunk, side):
        (a, _), (c, d) = low_chunk, chunk
        part = low[:, (c - a) * requests : (d - a) * requests]
        slots = jnp.tile(slot_row[None, :], (1, d - c))
        return add_extra(
            place, part, slots, second, from_core, keep, recv, chunk, side, per_shard, rank
        )

    def begin(low, low_chunk):
        begun = []
        for chunk in SUM_CHUNKS:
            if low_chunk[0] <= chunk[0] and chunk[1] <= low_chunk[1]:
                sent = blocks_of(low, low_chunk, chunk, 1)
                begun.append([low_chunk, chunk, low, in_plane(sent, 2)])
                low = after(low, sent)
        return begun

    def stay(low_chunk, chunk, low, token):
        return blocks_of(after(low, *token), low_chunk, chunk, 0)

    low = low_of(LOW_CHUNKS[0], gathered[0], ())
    begun = begin(after(low, *second_wave[:1]), LOW_CHUNKS[0])
    token = tuple(b[2] for b in begun)
    for chunk, sources in zip(LOW_CHUNKS[1:], gathered[1:]):
        low = low_of(chunk, sources, token)
        begun += begin(low, chunk)
    token = (begun[-1][2],)
    stages = planes.bit_length()
    events = sorted((3 * c + 2 * s, c, s) for c in range(len(SUM_CHUNKS)) for s in range(stages))
    state = []
    for _, c, stage in events:
        if stage == 0:
            low_chunk, chunk, low, received = begun[c]
            value = stay(low_chunk, chunk, low, token)
            token = (value,)
        else:
            value, received = state[c]
        half = value + after(received, *token).astype(F32)
        if stage == 0:
            state.append(None)
        if stage == stages - 1:
            state[c] = (half, None)
            token = (half,)
        else:
            count = half.shape[0] // 2
            moving = half[count:].astype(BF16)
            state[c] = (half[:count], along(moving, 1 << stage))
            token = (moving,)
    outputs = [
        value[0].astype(BF16).reshape(d - c, requests, width)
        for (value, _), (c, d) in zip(state, SUM_CHUNKS)
    ]
    return jnp.concatenate(outputs, axis=0)


def solution(mesh):
    in_specs = (
        P(None, "groups", "tensor"),
        P("tensor", None),
        P(("groups", "tensor"), None, None),
        P(("groups", "tensor"), None, None),
        P("groups"),
        P("groups"),
    )
    out_specs = P(None, "groups", "tensor")
    return jax.shard_map(local, mesh=mesh, in_specs=in_specs, out_specs=out_specs, check_vma=False)
```

time: 237 us -> 185 us (0.78)
  waiting for transfers between devices: 140 us -> 101 us
  starting transfers between devices: 35.6 us -> 24.2 us
  other arithmetic: 6.65 us -> 2.36 us
  Pallas kernels: 48.3 us -> 52.5 us
    ppermute x15 -> x13, waiting for transfers between devices: 57.3 us -> 36.4 us  [in_plane(): lax.ppermute(value, 'tensor', [(t, t ^ other) for t in range(devices)])]
    ppermute x13 -> x7, waiting for transfers between devices: 46.1 us -> 28.5 us  [along(): lax.ppermute(value, 'tensor', [(t, t ^ other * PLANE) for t in range(devi...]
    ppermute x13 -> x7, starting transfers between devices: 17.4 us -> 10.1 us  [along(): lax.ppermute(value, 'tensor', [(t, t ^ other * PLANE) for t in range(devi...]
    pallas_call x0 -> x1, Pallas kernels: none -> 3.15 us  [pack_core(): pl.pallas_call(body, grid_spec=pltpu.PrefetchScalarGridSpec(num_scalar_pr...]
    ppermute x15 -> x13, starting transfers between devices: 9.89 us -> 6.92 us  [in_plane(): lax.ppermute(value, 'tensor', [(t, t ^ other) for t in range(devices)])]
    pallas_call x2 -> x3, Pallas kernels: 11.1 us -> 12 us  [low_part(): pl.pallas_call(body, grid_spec=pltpu.PrefetchScalarGridSpec(num_scalar_pr...]
    pallas_call x4 -> x6, Pallas kernels: 17.9 us -> 18.4 us  [add_extra(): pl.pallas_call(body, grid_spec=pltpu.PrefetchScalarGridSpec(num_scalar_pr...]
  transfers between devices with their start and end apart: 35 -> 27, of which waited for: 17 -> 16; matrix products, arithmetic and copies ran while one was open for 3% -> 2% of each run, Pallas kernels for 20% -> 27%
where the time goes in v2:
time: 185 us
  waiting for transfers between devices  101 us (55%)
  Pallas kernels  52.5 us (28%)
  starting transfers between devices  24.2 us (13%)
  local copies, waits for them, and re-layouts  4.18 us (2%)
  other arithmetic  2.36 us (1%)
    ppermute x13, waiting for transfers between devices, in_plane(): lax.ppermute(value, 'tensor', [(t, t ^ other) for t in range(devices)])  36.4 us
    ppermute x7, waiting for transfers between devices, hop(): return lax.ppermute(value, 'tensor', pairs)  35.9 us
    ppermute x7, waiting for transfers between devices, along(): lax.ppermute(value, 'tensor', [(t, t ^ other * PLANE) for t in range(devi...  28.5 us
    pallas_call x6, Pallas kernels, add_extra(): pl.pallas_call(body, grid_spec=pltpu.PrefetchScalarGridSpec(num_scalar_pr...  18.4 us
    pallas_call x1, Pallas kernels, base_blocks(): pl.pallas_call(body, grid_spec=pltpu.PrefetchScalarGridSpec(num_scalar_pr...  15.2 us
    pallas_call x3, Pallas kernels, low_part(): pl.pallas_call(body, grid_spec=pltpu.PrefetchScalarGridSpec(num_scalar_pr...  12 us
    ppermute x7, starting transfers between devices, along(): lax.ppermute(value, 'tensor', [(t, t ^ other * PLANE) for t in range(devi...  10.1 us
    ppermute x7, starting transfers between devices, hop(): return lax.ppermute(value, 'tensor', pairs)  7.24 us
  transfers between devices with their start and end apart: 27, of which 16 were waited for; matrix products, arithmetic and copies ran while one was open for 2% of the time, Pallas kernels for 27%

profile of v2, /device:TPU:0, one launch (start us, length us, event | category | flops | bytes accessed | tf_op | source)
XLA Modules:
  0.0 184.6 jit_solution(13027160747403220317)
XLA Ops:
  0.2 1.8 pack_factors.2
  2.0 3.1 %collective-permute-start = (bf16[4,128,1024]{2,1,0:T(8,128)(2,1)S(1)}, bf16[4,128,1024]{2,1,0:T(8,128)(2,1)S(1)}, u32[]{:S(2)}, u32[]{:S(2)}) collective-permute-start(bf16[4,128,1024]{2,1,0:T(8,128)(2,1)S(1)} %copy-done.2), channel_id=1, source_target_pairs={{0,4},{1,5},{2,6},{3,7},{4,0},{5,1},{6,2},{7,3},{8,12},{9,13},{10,... | collective-permute-start | bytes 3145736 | tf_op jit(solution)/shard_map/ppermute | solution.py:279
  5.8 1.6 collective-permute-start.2
  7.4 1.8 pack_factors.3
  9.2 3.1 %pack_core.1 = bf16[2,4,128,1024]{3,2,1,0:T(8,128)(2,1)S(1)} custom-call(s32[3]{0:T(128)S(1)} %pad_add_fusion.place_ref, s32[4]{0:T(128)S(1)} %pad_add_fusion.1.order_ref, bf16[128,16384]{1,0:T(8,128)(2,1)} %bitcast.50, bf16[128,8192]{1,0:T(8,128)(2,1)} %bitcast.20, bf16[128,8192]{1,0:T(8,128)(2,1)} %bitcast.21), custom_call_target="tpu_custom_call" | custom-call | bytes 4194 | tf_op jit(solution)/shard_map/pack_core/pallas_call | solution.py:82
  12.4 15.2 %base_blocks.1 = (bf16[2,4,4,128,512]{4,3,2,1,0:T(8,128)(2,1)S(1)}, f32[2,4,4,128,512]{4,3,2,1,0:T(8,128)}) custom-call(s32[3]{0:T(128)S(1)} %pad_add_fusion.place_ref, bf16[4,128,1024]{2,1,0:T(8,128)(2,1)} %refs_4_.1, bf16[1024,8192]{1,0:T(8,128)(2,1)} %d3.1, bf16[1024,8192]{1,0:T(8,128)(2,1)} %d3.1, bf16[1024,8192]{1,0:T(8,128)(2,1)} %d3.1, ...), custom_call_target="tpu_custom_call" | custom-call | flops 8589934 | bytes 29360 | tf_op jit(solution)/shard_map/base_blocks/pallas_call | solution.py:114
  27.6 1.9 %collective-permute-done.3.refs_3_ = bf16[2,128,1024]{2,1,0:T(8,128)(2,1)S(1)} collective-permute-done((bf16[2,128,1024]{2,1,0:T(8,128)(2,1)S(1)}, bf16[2,128,1024]{2,1,0:T(8,128)(2,1)S(1)}, u32[]{:S(2)}, u32[]{:S(2)}) %collective-permute-start.3) | collective-permute-done | bytes 524320 | tf_op jit(solution)/shard_map/ppermute | solution.py:276
  29.6 1.3 collective-permute-start.7
  31.7 16.0 %collective-permute-done.7.refs_5_ = bf16[2,128,1024]{2,1,0:T(8,128)(2,1)S(1)} collective-permute-done((bf16[2,128,1024]{2,1,0:T(8,128)(2,1)S(1)}, bf16[2,128,1024]{2,1,0:T(8,128)(2,1)S(1)}, u32[]{:S(2)}, u32[]{:S(2)}) %collective-permute-start.7) | collective-permute-done | bytes 524320 | tf_op jit(solution)/shard_map/ppermute | solution.py:283
  48.6 13.5 %collective-permute-done.5.refs_2_ = bf16[2,128,1024]{2,1,0:T(8,128)(2,1)S(1)} collective-permute-done((bf16[2,128,1024]{2,1,0:T(8,128)(2,1)S(1)}, bf16[2,128,1024]{2,1,0:T(8,128)(2,1)S(1)}, u32[]{:S(2)}, u32[]{:S(2)}) %collective-permute-start.5) | collective-permute-done | bytes 524320 | tf_op jit(solution)/shard_map/ppermute | solution.py:276
  62.1 1.3 collective-permute-start.9
  63.4 12.4 %collective-permute-done.6.refs_3_ = bf16[2,128,1024]{2,1,0:T(8,128)(2,1)S(1)} collective-permute-done((bf16[2,128,1024]{2,1,0:T(8,128)(2,1)S(1)}, bf16[2,128,1024]{2,1,0:T(8,128)(2,1)S(1)}, u32[]{:S(2)}, u32[]{:S(2)}) %collective-permute-start.6) | collective-permute-done | bytes 524320 | tf_op jit(solution)/shard_map/ppermute | solution.py:276
  75.8 3.8 %collective-permute-done.9.refs_7_ = bf16[2,128,1024]{2,1,0:T(8,128)(2,1)S(1)} collective-permute-done((bf16[2,128,1024]{2,1,0:T(8,128)(2,1)S(1)}, bf16[2,128,1024]{2,1,0:T(8,128)(2,1)S(1)}, u32[]{:S(2)}, u32[]{:S(2)}) %collective-permute-start.9) | collective-permute-done | bytes 524320 | tf_op jit(solution)/shard_map/ppermute | solution.py:283
  79.6 0.9 slice.82
  80.5 1.3 collective-permute-start.12
  81.9 0.9 slice.84
  83.6 1.3 copy-done
  84.9 4.5 %low_part.3 = f32[16,512]{1,0:T(8,128)S(1)} custom-call(s32[3]{0:T(128)S(1)} %pad_add_fusion.place_ref, s32[4]{0:T(128)S(1)} %pad_add_fusion.1.order_ref, s32[1,512]{1,0:T(1,128)S(1)} %bitcast.13, bf16[128,16384]{1,0:T(8,128)(2,1)} %bitcast.51, bf16[2,4,128,1024]{3,2,1,0:T(8,128)(2,1)} %copy-done, bf16[2,128,1024]{2,1,0:T(8,128)(2,1)} %copy-done.6, ...), custom_call_target="tpu_custom_call" | custom-call | flops 1073741 | bytes 4194 | tf_op jit(solution)/shard_map/low_part/pallas_call | solution.py:182
  89.4 3.8 %low_part.4 = f32[16,256]{1,0:T(8,128)S(1)} custom-call(s32[3]{0:T(128)S(1)} %pad_add_fusion.place_ref, s32[4]{0:T(128)S(1)} %pad_add_fusion.1.order_ref, s32[1,256]{1,0:T(1,128)S(1)} %get-tuple-element.91.slots_ref, bf16[128,16384]{1,0:T(8,128)(2,1)} %bitcast.52, bf16[2,4,128,1024]{3,2,1,0:T(8,128)(2,1)} %copy-done, bf16[2,128,1024]{2,1,0:T(8,128)(2,1)} %copy-done.4, ...), custom_call_target="tpu_custom_call" | custom-call | flops 536870 | bytes 3145 | tf_op jit(solution)/shard_map/low_part/pallas_call | solution.py:182
  93.4 1.0 collective-permute-done.10
  94.4 0.8 collective-permute-start.11
  95.2 2.9 %collective-permute-done.11 = f32[16,256]{1,0:T(8,128)S(1)} collective-permute-done((f32[16,256]{1,0:T(8,128)S(1)}, f32[16,256]{1,0:T(8,128)S(1)}, u32[]{:S(2)}, u32[]{:S(2)}) %collective-permute-start.11) | collective-permute-done | bytes 16416 | tf_op jit(solution)/shard_map/ppermute | solution.py:276
  98.2 3.6 %add_extra.8 = bf16[4,256,512]{2,1,0:T(8,128)(2,1)S(1)} custom-call(s32[3]{0:T(128)S(1)} %pad_add_fusion.place_ref, f32[16,256]{1,0:T(8,128)S(1)} %add.53.low_ref, s32[1,256]{1,0:T(1,128)S(1)} %bitcast.18, bf16[128,8192]{1,0:T(8,128)(2,1)} %bitcast.22, bf16[128,8192]{1,0:T(8,128)(2,1)} %bitcast.23, bf16[128,8192]{1,0:T(8,128)(2,1)} %bitcast.24, ...), custom_call_target="tpu_custom_call" | custom-call | flops 268435 | bytes 5242 | tf_op jit(solution)/shard_map/add_extra/pallas_call | solution.py:241
  101.8 0.9 collective-permute-start.18
  102.7 1.3 collective-permute-start.14
  104.0 16.2 %collective-permute-done.14.refs_7_ = bf16[2,128,1024]{2,1,0:T(8,128)(2,1)S(1)} collective-permute-done((bf16[2,128,1024]{2,1,0:T(8,128)(2,1)S(1)}, bf16[2,128,1024]{2,1,0:T(8,128)(2,1)S(1)}, u32[]{:S(2)}, u32[]{:S(2)}) %collective-permute-start.14) | collective-permute-done | bytes 524320 | tf_op jit(solution)/shard_map/ppermute | solution.py:283
  120.2 0.8 copy-done.13
  121.0 3.8 %low_part.5 = f32[16,256]{1,0:T(8,128)S(1)} custom-call(s32[3]{0:T(128)S(1)} %pad_add_fusion.place_ref, s32[4]{0:T(128)S(1)} %pad_add_fusion.1.order_ref, s32[1,256]{1,0:T(1,128)S(1)} %get-tuple-element.92.slots_ref, bf16[128,16384]{1,0:T(8,128)(2,1)} %bitcast.53, bf16[2,4,128,1024]{3,2,1,0:T(8,128)(2,1)} %copy-done, bf16[2,128,1024]{2,1,0:T(8,128)(2,1)} %copy-done.4, ...), custom_call_target="tpu_custom_call" | custom-call | flops 536870 | bytes 3145 | tf_op jit(solution)/shard_map/low_part/pallas_call | solution.py:182
  124.8 1.2 collective-permute-done.15
  126.3 3.4 %collective-permute-done.16 = f32[16,256]{1,0:T(8,128)S(1)} collective-permute-done((f32[16,256]{1,0:T(8,128)S(1)}, f32[16,256]{1,0:T(8,128)S(1)}, u32[]{:S(2)}, u32[]{:S(2)}) %collective-permute-start.16) | collective-permute-done | bytes 16416 | tf_op jit(solution)/shard_map/ppermute | solution.py:276
  129.8 2.8 %add_extra.6 = bf16[4,128,512]{2,1,0:T(8,128)(2,1)S(1)} custom-call(s32[3]{0:T(128)S(1)} %pad_add_fusion.place_ref, f32[16,128]{1,0:T(8,128)S(1)} %slice.106.low_ref, s32[1,128]{1,0:T(1,128)S(1)} %bitcast.14, bf16[128,8192]{1,0:T(8,128)(2,1)} %bitcast.26, bf16[128,8192]{1,0:T(8,128)(2,1)} %bitcast.27, bf16[128,8192]{1,0:T(8,128)(2,1)} %bitcast.28, ...), custom_call_target="tpu_custom_call" | custom-call | flops 134217 | bytes 2621 | tf_op jit(solution)/shard_map/add_extra/pallas_call | solution.py:241
  132.6 3.6 %add_extra.7 = f32[4,256,512]{2,1,0:T(8,128)S(1)} custom-call(s32[3]{0:T(128)S(1)} %pad_add_fusion.place_ref, f32[16,256]{1,0:T(8,128)S(1)} %add.53.low_ref, s32[1,256]{1,0:T(1,128)S(1)} %bitcast.19, bf16[128,8192]{1,0:T(8,128)(2,1)} %bitcast.32, bf16[128,8192]{1,0:T(8,128)(2,1)} %bitcast.31, bf16[128,8192]{1,0:T(8,128)(2,1)} %bitcast.30, ...), custom_call_target="tpu_custom_call" | custom-call | flops 268435 | bytes 5242 | tf_op jit(solution)/shard_map/add_extra/pallas_call | solution.py:241
  136.6 1.1 collective-permute-start.19
  137.7 1.7 collective-permute-start.21
  139.4 2.8 %add_extra.11 = bf16[4,128,512]{2,1,0:T(8,128)(2,1)S(1)} custom-call(s32[3]{0:T(128)S(1)} %pad_add_fusion.place_ref, f32[16,128]{1,0:T(8,128)S(1)} %slice.97.low_ref, s32[1,128]{1,0:T(1,128)S(1)} %bitcast.15, bf16[128,8192]{1,0:T(8,128)(2,1)} %bitcast.34, bf16[128,8192]{1,0:T(8,128)(2,1)} %bitcast.35, bf16[128,8192]{1,0:T(8,128)(2,1)} %bitcast.36, ...), custom_call_target="tpu_custom_call" | custom-call | flops 134217 | bytes 2621 | tf_op jit(solution)/shard_map/add_extra/pallas_call | solution.py:241
  142.6 6.9 %collective-permute-done.19 = bf16[2,256,512]{2,1,0:T(8,128)(2,1)S(1)} collective-permute-done((bf16[2,256,512]{2,1,0:T(8,128)(2,1)S(1)}, bf16[2,256,512]{2,1,0:T(8,128)(2,1)S(1)}, u32[]{:S(2)}, u32[]{:S(2)}) %collective-permute-start.19) | collective-permute-done | bytes 524320 | tf_op jit(solution)/shard_map/ppermute | solution.py:279
  149.8 1.1 collective-permute-start.20
  150.8 2.8 %add_extra.9 = f32[4,128,512]{2,1,0:T(8,128)S(1)} custom-call(s32[3]{0:T(128)S(1)} %pad_add_fusion.place_ref, f32[16,128]{1,0:T(8,128)S(1)} %slice.91.low_ref, s32[1,128]{1,0:T(1,128)S(1)} %bitcast.16, bf16[128,8192]{1,0:T(8,128)(2,1)} %bitcast.38, bf16[128,8192]{1,0:T(8,128)(2,1)} %bitcast.39, bf16[128,8192]{1,0:T(8,128)(2,1)} %bitcast.40, ...), custom_call_target="tpu_custom_call" | custom-call | flops 134217 | bytes 2621 | tf_op jit(solution)/shard_map/add_extra/pallas_call | solution.py:241
  153.9 1.1 collective-permute-start.22
  155.0 6.8 %collective-permute-done.20 = bf16[1,256,512]{2,1,0:T(8,128)(2,1)S(1)} collective-permute-done((bf16[1,256,512]{2,1,0:T(8,128)(2,1)S(1)}, bf16[1,256,512]{2,1,0:T(8,128)(2,1)S(1)}, u32[]{:S(2)}, u32[]{:S(2)}) %collective-permute-start.20) | collective-permute-done | bytes 262176 | tf_op jit(solution)/shard_map/ppermute | solution.py:279
  161.9 2.6 %collective-permute-done.22 = bf16[2,128,512]{2,1,0:T(8,128)(2,1)S(1)} collective-permute-done((bf16[2,128,512]{2,1,0:T(8,128)(2,1)S(1)}, bf16[2,128,512]{2,1,0:T(8,128)(2,1)S(1)}, u32[]{:S(2)}, u32[]{:S(2)}) %collective-permute-start.22) | collective-permute-done | bytes 262176 | tf_op jit(solution)/shard_map/ppermute | solution.py:279
  164.9 2.8 %add_extra.10 = f32[4,128,512]{2,1,0:T(8,128)S(1)} custom-call(s32[3]{0:T(128)S(1)} %pad_add_fusion.place_ref, f32[16,128]{1,0:T(8,128)S(1)} %slice.96.low_ref, s32[1,128]{1,0:T(1,128)S(1)} %bitcast.17, bf16[128,8192]{1,0:T(8,128)(2,1)} %bitcast.42, bf16[128,8192]{1,0:T(8,128)(2,1)} %bitcast.43, bf16[128,8192]{1,0:T(8,128)(2,1)} %bitcast.44, ...), custom_call_target="tpu_custom_call" | custom-call | flops 134217 | bytes 2621 | tf_op jit(solution)/shard_map/add_extra/pallas_call | solution.py:241
  168.0 2.5 %collective-permute-start.25 = (bf16[2,128,512]{2,1,0:T(8,128)(2,1)S(1)}, bf16[2,128,512]{2,1,0:T(8,128)(2,1)S(1)}, u32[]{:S(2)}, u32[]{:S(2)}) collective-permute-start(bf16[2,128,512]{2,1,0:T(8,128)(2,1)S(1)} %slice.136), channel_id=1, source_target_pairs={{0,4},{1,5},{2,6},{3,7},{4,0},{5,1},{6,2},{7,3},{8,12},{9,13},{10,... | collective-permute-start | bytes 786440 | tf_op jit(solution)/shard_map/ppermute | solution.py:279
  170.5 0.8 collective-permute-done.23
  171.4 4.9 %collective-permute-done.25 = bf16[2,128,512]{2,1,0:T(8,128)(2,1)S(1)} collective-permute-done((bf16[2,128,512]{2,1,0:T(8,128)(2,1)S(1)}, bf16[2,128,512]{2,1,0:T(8,128)(2,1)S(1)}, u32[]{:S(2)}, u32[]{:S(2)}) %collective-permute-start.25) | collective-permute-done | bytes 262176 | tf_op jit(solution)/shard_map/ppermute | solution.py:279
  176.3 0.9 collective-permute-start.26
  177.3 6.4 %collective-permute-done.26 = bf16[1,128,512]{2,1,0:T(8,128)(2,1)S(1)} collective-permute-done((bf16[1,128,512]{2,1,0:T(8,128)(2,1)S(1)}, bf16[1,128,512]{2,1,0:T(8,128)(2,1)S(1)}, u32[]{:S(2)}, u32[]{:S(2)}) %collective-permute-start.26) | collective-permute-done | bytes 131104 | tf_op jit(solution)/shard_map/ppermute | solution.py:279
  183.7 0.9 pad_maximum_fusion
  (87 shorter events, 6.3 us)
Async XLA Ops:
  0.2 1.8 copy-start.2
  2.0 27.5 %collective-permute-start = (bf16[4,128,1024]{2,1,0:T(8,128)(2,1)S(1)}, bf16[4,128,1024]{2,1,0:T(8,128)(2,1)S(1)}, u32[]{:S(2)}, u32[]{:S(2)}) collective-permute-start(bf16[4,128,1024]{2,1,0:T(8,128)(2,1)S(1)} %copy-done.2), channel_id=1, source_target_pairs={{0,4},{1,5},{2,6},{3,7},{4,0},{5,1},{6,2},{7,3},{8,12},{9,13},{10,... | collective-permute-start | bytes 3145736 | tf_op jit(solution)/shard_map/ppermute | solution.py:279
  5.1 24.5 %collective-permute-start.1 = (bf16[4,128,1024]{2,1,0:T(8,128)(2,1)S(1)}, bf16[4,128,1024]{2,1,0:T(8,128)(2,1)S(1)}, u32[]{:S(2)}, u32[]{:S(2)}) collective-permute-start(bf16[4,128,1024]{2,1,0:T(8,128)(2,1)S(1)} %copy-done.2), channel_id=1, source_target_pairs={{4,8},{5,9},{6,10},{7,11},{8,4},{9,5},{10,6},{11,7},{20,24},{21,25... | collective-permute-start | bytes 3145736 | tf_op jit(solution)/shard_map/ppermute | solution.py:283
  5.8 21.8 %collective-permute-start.2 = (bf16[2,128,1024]{2,1,0:T(8,128)(2,1)S(1)}, bf16[2,128,1024]{2,1,0:T(8,128)(2,1)S(1)}, u32[]{:S(2)}, u32[]{:S(2)}) collective-permute-start(bf16[2,128,1024]{2,1,0:T(8,128)(2,1)S(1)} %get-tuple-element.48), channel_id=1, source_target_pairs={{0,2},{1,3},{2,0},{3,1},{4,6},{5,7},{6,4},{7,5},{8,10},{9,11},{10,... | collective-permute-start | bytes 1572872 | tf_op jit(solution)/shard_map/ppermute | solution.py:276
  7.4 22.1 %collective-permute-start.3 = (bf16[2,128,1024]{2,1,0:T(8,128)(2,1)S(1)}, bf16[2,128,1024]{2,1,0:T(8,128)(2,1)S(1)}, u32[]{:S(2)}, u32[]{:S(2)}) collective-permute-start(bf16[2,128,1024]{2,1,0:T(8,128)(2,1)S(1)} %get-tuple-element.49), channel_id=1, source_target_pairs={{0,3},{1,2},{2,1},{3,0},{4,7},{5,6},{6,5},{7,4},{8,11},{9,10},{10,... | collective-permute-start | bytes 1572872 | tf_op jit(solution)/shard_map/ppermute | solution.py:276
  27.6 54.1 %copy-start.14 = (s32[128]{0:T(128)S(1)}, s32[128]{0:T(128)}, u32[]{:S(2)}) copy-start(s32[128]{0:T(128)} %param.10) | copy-start | bytes 1540
  27.6 54.1 %copy-start.15 = (s32[128]{0:T(128)S(1)}, s32[128]{0:T(128)}, u32[]{:S(2)}) copy-start(s32[128]{0:T(128)} %param.11) | copy-start | bytes 1540
  27.6 55.2 %copy-start.6 = (bf16[2,128,1024]{2,1,0:T(8,128)(2,1)}, bf16[2,128,1024]{2,1,0:T(8,128)(2,1)S(1)}, u32[]{:S(2)}) copy-start(bf16[2,128,1024]{2,1,0:T(8,128)(2,1)S(1)} %collective-permute-done.2.refs_2_) | copy-start | bytes 1572868
  29.5 53.3 %copy-start.7 = (bf16[2,128,1024]{2,1,0:T(8,128)(2,1)}, bf16[2,128,1024]{2,1,0:T(8,128)(2,1)S(1)}, u32[]{:S(2)}) copy-start(bf16[2,128,1024]{2,1,0:T(8,128)(2,1)S(1)} %collective-permute-done.3.refs_3_) | copy-start | bytes 1572868
  29.5 53.3 %copy-start.3 = (bf16[4,128,1024]{2,1,0:T(8,128)(2,1)}, bf16[4,128,1024]{2,1,0:T(8,128)(2,1)S(1)}, u32[]{:S(2)}) copy-start(bf16[4,128,1024]{2,1,0:T(8,128)(2,1)S(1)} %collective-permute-done.refs_5_) | copy-start | bytes 3145732
  29.6 53.3 %copy-start.1 = (bf16[4,128,1024]{2,1,0:T(8,128)(2,1)}, bf16[4,128,1024]{2,1,0:T(8,128)(2,1)S(1)}, u32[]{:S(2)}) copy-start(bf16[4,128,1024]{2,1,0:T(8,128)(2,1)S(1)} %collective-permute-done.1.refs_4_) | copy-start | bytes 3145732
  29.6 18.0 %collective-permute-start.7 = (bf16[2,128,1024]{2,1,0:T(8,128)(2,1)S(1)}, bf16[2,128,1024]{2,1,0:T(8,128)(2,1)S(1)}, u32[]{:S(2)}, u32[]{:S(2)}) collective-permute-start(bf16[2,128,1024]{2,1,0:T(8,128)(2,1)S(1)} %slice.79), channel_id=1, source_target_pairs={{4,0},{5,1},{6,2},{7,3},{8,12},{9,13},{10,14},{11,15},{20,16},{21,... | collective-permute-start | bytes 1572872 | tf_op jit(solution)/shard_map/ppermute | solution.py:283
  30.9 16.7 %collective-permute-start.8 = (bf16[2,128,1024]{2,1,0:T(8,128)(2,1)S(1)}, bf16[2,128,1024]{2,1,0:T(8,128)(2,1)S(1)}, u32[]{:S(2)}, u32[]{:S(2)}) collective-permute-start(bf16[2,128,1024]{2,1,0:T(8,128)(2,1)S(1)} %slice.80), channel_id=1, source_target_pairs={{4,8},{5,9},{6,10},{7,11},{8,4},{9,5},{10,6},{11,7},{20,24},{21,25... | collective-permute-start | bytes 1572872 | tf_op jit(solution)/shard_map/ppermute | solution.py:283
  47.6 41.7 %copy-start.10 = (bf16[2,128,1024]{2,1,0:T(8,128)(2,1)}, bf16[2,128,1024]{2,1,0:T(8,128)(2,1)S(1)}, u32[]{:S(2)}) copy-start(bf16[2,128,1024]{2,1,0:T(8,128)(2,1)S(1)} %collective-permute-done.7.refs_5_) | copy-start | bytes 1572868
  47.6 41.7 %copy-start.11 = (bf16[2,128,1024]{2,1,0:T(8,128)(2,1)}, bf16[2,128,1024]{2,1,0:T(8,128)(2,1)S(1)}, u32[]{:S(2)}) copy-start(bf16[2,128,1024]{2,1,0:T(8,128)(2,1)S(1)} %collective-permute-done.8.refs_6_) | copy-start | bytes 1572868
  47.6 50.6 %collective-permute-start.17 = (bf16[2,4,4,128,512]{4,3,2,1,0:T(8,128)(2,1)S(1)}, bf16[2,4,4,128,512]{4,3,2,1,0:T(8,128)(2,1)}, u32[]{:S(2)}, u32[]{:S(2)}) collective-permute-start(bf16[2,4,4,128,512]{4,3,2,1,0:T(8,128)(2,1)S(1)} %get-tuple-element.77), channel_id=1, source_target_pairs={{0,1},{1,0},{2,3},{3,2},{4,5},{5,4},{6,7},{7,6},{8,9},{9,8},{10,11... | collective-permute-start | bytes 12582920 | tf_op jit(solution)/shard_map/ppermute | solution.py:276
  47.8 35.7 %collective-permute-start.4 = (bf16[2,4,128,1024]{3,2,1,0:T(8,128)(2,1)S(1)}, bf16[2,4,128,1024]{3,2,1,0:T(8,128)(2,1)S(1)}, u32[]{:S(2)}, u32[]{:S(2)}) collective-permute-start(bf16[2,4,128,1024]{3,2,1,0:T(8,128)(2,1)S(1)} %pack_core.1), channel_id=1, source_target_pairs={{0,1},{1,0},{2,3},{3,2},{4,5},{5,4},{6,7},{7,6},{8,9},{9,8},{10,11... | collective-permute-start | bytes 6291464 | tf_op jit(solution)/shard_map/ppermute | solution.py:276
  48.2 13.9 %collective-permute-start.5 = (bf16[2,128,1024]{2,1,0:T(8,128)(2,1)S(1)}, bf16[2,128,1024]{2,1,0:T(8,128)(2,1)S(1)}, u32[]{:S(2)}, u32[]{:S(2)}) collective-permute-start(bf16[2,128,1024]{2,1,0:T(8,128)(2,1)S(1)} %get-tuple-element.62), channel_id=1, source_target_pairs={{0,2},{1,3},{2,0},{3,1},{4,6},{5,7},{6,4},{7,5},{8,10},{9,11},{10,... | collective-permute-start | bytes 1572872 | tf_op jit(solution)/shard_map/ppermute | solution.py:276
  62.1 27.2 %copy-start.4 = (bf16[2,128,1024]{2,1,0:T(8,128)(2,1)}, bf16[2,128,1024]{2,1,0:T(8,128)(2,1)S(1)}, u32[]{:S(2)}) copy-start(bf16[2,128,1024]{2,1,0:T(8,128)(2,1)S(1)} %collective-permute-done.5.refs_2_) | copy-start | bytes 1572868
  62.1 13.7 %collective-permute-start.6 = (bf16[2,128,1024]{2,1,0:T(8,128)(2,1)S(1)}, bf16[2,128,1024]{2,1,0:T(8,128)(2,1)S(1)}, u32[]{:S(2)}, u32[]{:S(2)}) collective-permute-start(bf16[2,128,1024]{2,1,0:T(8,128)(2,1)S(1)} %get-tuple-element.63), channel_id=1, source_target_pairs={{0,3},{1,2},{2,1},{3,0},{4,7},{5,6},{6,5},{7,4},{8,11},{9,10},{10,... | collective-permute-start | bytes 1572872 | tf_op jit(solution)/shard_map/ppermute | solution.py:276
  62.1 17.4 %collective-permute-start.9 = (bf16[2,128,1024]{2,1,0:T(8,128)(2,1)S(1)}, bf16[2,128,1024]{2,1,0:T(8,128)(2,1)S(1)}, u32[]{:S(2)}, u32[]{:S(2)}) collective-permute-start(bf16[2,128,1024]{2,1,0:T(8,128)(2,1)S(1)} %collective-permute-done.8.refs_6_), channel_id=1, source_target_pairs={{4,0},{5,1},{6,2},{7,3},{8,12},{9,13},{10,14},{11,15},{20,16},{21,... | collective-permute-start | bytes 1572872 | tf_op jit(solution)/shard_map/ppermute | solution.py:283
  75.8 13.5 %copy-start.5 = (bf16[2,128,1024]{2,1,0:T(8,128)(2,1)}, bf16[2,128,1024]{2,1,0:T(8,128)(2,1)S(1)}, u32[]{:S(2)}) copy-start(bf16[2,128,1024]{2,1,0:T(8,128)(2,1)S(1)} %collective-permute-done.6.refs_3_) | copy-start | bytes 1572868
  79.6 9.8 %copy-start.12 = (bf16[2,128,1024]{2,1,0:T(8,128)(2,1)}, bf16[2,128,1024]{2,1,0:T(8,128)(2,1)S(1)}, u32[]{:S(2)}) copy-start(bf16[2,128,1024]{2,1,0:T(8,128)(2,1)S(1)} %collective-permute-done.9.refs_7_) | copy-start | bytes 1572868
  80.5 17.7 %collective-permute-start.12 = (bf16[2,128,1024]{2,1,0:T(8,128)(2,1)}, bf16[2,128,1024]{2,1,0:T(8,128)(2,1)S(1)}, u32[]{:S(2)}, u32[]{:S(2)}) collective-permute-start(bf16[2,128,1024]{2,1,0:T(8,128)(2,1)} %slice.82), channel_id=1, source_target_pairs={{4,0},{5,1},{6,2},{7,3},{8,12},{9,13},{10,14},{11,15},{20,16},{21,... | collective-permute-start | bytes 1572872 | tf_op jit(solution)/shard_map/ppermute | solution.py:283
  82.8 19.9 %collective-permute-start.13 = (bf16[2,128,1024]{2,1,0:T(8,128)(2,1)}, bf16[2,128,1024]{2,1,0:T(8,128)(2,1)S(1)}, u32[]{:S(2)}, u32[]{:S(2)}) collective-permute-start(bf16[2,128,1024]{2,1,0:T(8,128)(2,1)} %slice.84), channel_id=1, source_target_pairs={{4,8},{5,9},{6,10},{7,11},{8,4},{9,5},{10,6},{11,7},{20,24},{21,25... | collective-permute-start | bytes 1572872 | tf_op jit(solution)/shard_map/ppermute | solution.py:283
  83.6 1.3 copy-start
  93.2 1.2 collective-permute-start.10
  94.4 3.7 %collective-permute-start.11 = (f32[16,256]{1,0:T(8,128)S(1)}, f32[16,256]{1,0:T(8,128)S(1)}, u32[]{:S(2)}, u32[]{:S(2)}) collective-permute-start(f32[16,256]{1,0:T(8,128)S(1)} %add.52), channel_id=1, source_target_pairs={{0,2},{1,3},{2,0},{3,1},{4,6},{5,7},{6,4},{7,5},{8,10},{9,11},{10,... | collective-permute-start | bytes 49160 | tf_op jit(solution)/shard_map/ppermute | solution.py:276
  98.2 3.6 %copy-start.8 = (bf16[2,128,1024]{2,1,0:T(8,128)(2,1)}, bf16[2,128,1024]{2,1,0:T(8,128)(2,1)S(1)}, u32[]{:S(2)}) copy-start(bf16[2,128,1024]{2,1,0:T(8,128)(2,1)S(1)} %collective-permute-done.12.refs_5_) | copy-start | bytes 1572868
  101.8 34.4 %collective-permute-start.18 = (bf16[4,256,512]{2,1,0:T(8,128)(2,1)S(1)}, bf16[4,256,512]{2,1,0:T(8,128)(2,1)S(1)}, u32[]{:S(2)}, u32[]{:S(2)}) collective-permute-start(bf16[4,256,512]{2,1,0:T(8,128)(2,1)S(1)} %add_extra.8), channel_id=1, source_target_pairs={{0,2},{1,3},{2,0},{3,1},{4,6},{5,7},{6,4},{7,5},{8,10},{9,11},{10,... | collective-permute-start | bytes 3145736 | tf_op jit(solution)/shard_map/ppermute | solution.py:276
  102.7 17.5 %copy-start.9 = (bf16[2,128,1024]{2,1,0:T(8,128)(2,1)}, bf16[2,128,1024]{2,1,0:T(8,128)(2,1)S(1)}, u32[]{:S(2)}) copy-start(bf16[2,128,1024]{2,1,0:T(8,128)(2,1)S(1)} %collective-permute-done.13.refs_6_) | copy-start | bytes 1572868
  102.7 17.5 %collective-permute-start.14 = (bf16[2,128,1024]{2,1,0:T(8,128)(2,1)S(1)}, bf16[2,128,1024]{2,1,0:T(8,128)(2,1)S(1)}, u32[]{:S(2)}, u32[]{:S(2)}) collective-permute-start(bf16[2,128,1024]{2,1,0:T(8,128)(2,1)S(1)} %collective-permute-done.13.refs_6_), channel_id=1, source_target_pairs={{4,0},{5,1},{6,2},{7,3},{8,12},{9,13},{10,14},{11,15},{20,16},{21,... | collective-permute-start | bytes 1572872 | tf_op jit(solution)/shard_map/ppermute | solution.py:283
  120.2 0.8 copy-start.13
  124.8 1.2 collective-permute-start.15
  126.0 3.7 %collective-permute-start.16 = (f32[16,256]{1,0:T(8,128)S(1)}, f32[16,256]{1,0:T(8,128)S(1)}, u32[]{:S(2)}, u32[]{:S(2)}) collective-permute-start(f32[16,256]{1,0:T(8,128)S(1)} %add.55), channel_id=1, source_target_pairs={{0,2},{1,3},{2,0},{3,1},{4,6},{5,7},{6,4},{7,5},{8,10},{9,11},{10,... | collective-permute-start | bytes 49160 | tf_op jit(solution)/shard_map/ppermute | solution.py:276
  136.6 12.9 %collective-permute-start.19 = (bf16[2,256,512]{2,1,0:T(8,128)(2,1)S(1)}, bf16[2,256,512]{2,1,0:T(8,128)(2,1)S(1)}, u32[]{:S(2)}, u32[]{:S(2)}) collective-permute-start(bf16[2,256,512]{2,1,0:T(8,128)(2,1)S(1)} %slice.135), channel_id=1, source_target_pairs={{0,4},{1,5},{2,6},{3,7},{4,0},{5,1},{6,2},{7,3},{8,12},{9,13},{10,... | collective-permute-start | bytes 1572872 | tf_op jit(solution)/shard_map/ppermute | solution.py:279
  137.7 16.0 %collective-permute-start.21 = (bf16[4,128,512]{2,1,0:T(8,128)(2,1)S(1)}, bf16[4,128,512]{2,1,0:T(8,128)(2,1)S(1)}, u32[]{:S(2)}, u32[]{:S(2)}) collective-permute-start(bf16[4,128,512]{2,1,0:T(8,128)(2,1)S(1)} %add_extra.6), channel_id=1, source_target_pairs={{0,2},{1,3},{2,0},{3,1},{4,6},{5,7},{6,4},{7,5},{8,10},{9,11},{10,... | collective-permute-start | bytes 1572872 | tf_op jit(solution)/shard_map/ppermute | solution.py:276
  142.3 25.5 %collective-permute-start.24 = (bf16[4,128,512]{2,1,0:T(8,128)(2,1)S(1)}, bf16[4,128,512]{2,1,0:T(8,128)(2,1)S(1)}, u32[]{:S(2)}, u32[]{:S(2)}) collective-permute-start(bf16[4,128,512]{2,1,0:T(8,128)(2,1)S(1)} %add_extra.11), channel_id=1, source_target_pairs={{0,2},{1,3},{2,0},{3,1},{4,6},{5,7},{6,4},{7,5},{8,10},{9,11},{10,... | collective-permute-start | bytes 1572872 | tf_op jit(solution)/shard_map/ppermute | solution.py:276
  149.8 12.0 %collective-permute-start.20 = (bf16[1,256,512]{2,1,0:T(8,128)(2,1)S(1)}, bf16[1,256,512]{2,1,0:T(8,128)(2,1)S(1)}, u32[]{:S(2)}, u32[]{:S(2)}) collective-permute-start(bf16[1,256,512]{2,1,0:T(8,128)(2,1)S(1)} %slice.138), channel_id=1, source_target_pairs={{0,8},{1,9},{2,10},{3,11},{4,12},{5,13},{6,14},{7,15},{8,0},{9,1},... | collective-permute-start | bytes 786440 | tf_op jit(solution)/shard_map/ppermute | solution.py:279
  153.9 10.6 %collective-permute-start.22 = (bf16[2,128,512]{2,1,0:T(8,128)(2,1)S(1)}, bf16[2,128,512]{2,1,0:T(8,128)(2,1)S(1)}, u32[]{:S(2)}, u32[]{:S(2)}) collective-permute-start(bf16[2,128,512]{2,1,0:T(8,128)(2,1)S(1)} %slice.137), channel_id=1, source_target_pairs={{0,4},{1,5},{2,6},{3,7},{4,0},{5,1},{6,2},{7,3},{8,12},{9,13},{10,... | collective-permute-start | bytes 786440 | tf_op jit(solution)/shard_map/ppermute | solution.py:279
  164.6 6.7 %collective-permute-start.23 = (bf16[1,128,512]{2,1,0:T(8,128)(2,1)S(1)}, bf16[1,128,512]{2,1,0:T(8,128)(2,1)S(1)}, u32[]{:S(2)}, u32[]{:S(2)}) collective-permute-start(bf16[1,128,512]{2,1,0:T(8,128)(2,1)S(1)} %slice.140), channel_id=1, source_target_pairs={{0,8},{1,9},{2,10},{3,11},{4,12},{5,13},{6,14},{7,15},{8,0},{9,1},... | collective-permute-start | bytes 393224 | tf_op jit(solution)/shard_map/ppermute | solution.py:279
  168.0 8.2 %collective-permute-start.25 = (bf16[2,128,512]{2,1,0:T(8,128)(2,1)S(1)}, bf16[2,128,512]{2,1,0:T(8,128)(2,1)S(1)}, u32[]{:S(2)}, u32[]{:S(2)}) collective-permute-start(bf16[2,128,512]{2,1,0:T(8,128)(2,1)S(1)} %slice.136), channel_id=1, source_target_pairs={{0,4},{1,5},{2,6},{3,7},{4,0},{5,1},{6,2},{7,3},{8,12},{9,13},{10,... | collective-permute-start | bytes 786440 | tf_op jit(solution)/shard_map/ppermute | solution.py:279
  176.3 7.3 %collective-permute-start.26 = (bf16[1,128,512]{2,1,0:T(8,128)(2,1)S(1)}, bf16[1,128,512]{2,1,0:T(8,128)(2,1)S(1)}, u32[]{:S(2)}, u32[]{:S(2)}) collective-permute-start(bf16[1,128,512]{2,1,0:T(8,128)(2,1)S(1)} %slice.139), channel_id=1, source_target_pairs={{0,8},{1,9},{2,10},{3,11},{4,12},{5,13},{6,14},{7,15},{8,0},{9,1},... | collective-permute-start | bytes 393224 | tf_op jit(solution)/shard_map/ppermute | solution.py:279

commit v3 on v2

v3 whole, which is shorter than its diff:
```python
import jax
import jax.numpy as jnp
from jax import lax
from jax.experimental import pallas as pl
from jax.experimental.pallas import tpu as pltpu
from jax.sharding import PartitionSpec as P

PLANE = 4
F32 = jnp.float32
BF16 = jnp.bfloat16
VMEM_BYTES = 48 * 1024 * 1024
LOW_CHUNKS = ((0, 2), (2, 4))
KEEP_Y, SEND_Y, KEEP_Z, SEND_Z = range(4)


def halving(i, planes):
    out, bit = 0, 1
    while bit < planes:
        out = out * 2 + ((i // bit) % 2)
        bit *= 2
    return out


def after(value, *others):
    return lax.optimization_barrier((value, *others))[0]


def cost(flops, moved, share=1000):
    return pl.CostEstimate(
        flops=int(flops) // share, bytes_accessed=int(moved) // share, transcendentals=0
    )


def hbm(*values):
    return [pltpu.with_memory_space_constraint(value, pltpu.HBM) for value in values]


def params():
    return pltpu.CompilerParams(vmem_limit_bytes=VMEM_BYTES)


def pack_factors(place, order, table, width, other):
    rows = table.shape[0]
    planes = table.shape[1] // (PLANE * width)

    def body(place_ref, order_ref, *refs):
        for i in range(planes):
            refs[planes][i] = refs[i][...]

    def columns(i):
        return lambda j, p, o: (0, o[i] * PLANE + (p[1] ^ other))

    return pl.pallas_call(
        body,
        grid_spec=pltpu.PrefetchScalarGridSpec(
            num_scalar_prefetch=2,
            grid=(1,),
            in_specs=[pl.BlockSpec((rows, width), columns(i)) for i in range(planes)],
            out_specs=pl.BlockSpec((planes, rows, width), lambda i, p, o: (0, 0, 0)),
        ),
        out_shape=jax.ShapeDtypeStruct((planes, rows, width), BF16),
        cost_estimate=cost(0, 4 * planes * rows * width),
        compiler_params=params(),
        name="pack_factors",
    )(place, order, *hbm(*([table] * planes)))


def pack_core(place, order, first, second, width):
    rows, units = first.shape[0], 2 * width
    planes = first.shape[1] // (PLANE * units)

    def body(place_ref, order_ref, a_ref, s0_ref, s1_ref, out_ref):
        out_ref[0, 0] = a_ref[...]
        out_ref[1, 0, :, :width] = s0_ref[...]
        out_ref[1, 0, :, width:] = s1_ref[...]

    def columns(side):
        return lambda i, p, o: (
            0,
            (p[0] ^ halving(i, planes)) * PLANE + (p[1] ^ 1 ^ (2 * side)),
        )

    return pl.pallas_call(
        body,
        grid_spec=pltpu.PrefetchScalarGridSpec(
            num_scalar_prefetch=2,
            grid=(planes,),
            in_specs=[pl.BlockSpec((rows, units), lambda i, p, o: (0, o[i] * PLANE + (p[1] ^ 1)))]
            + [pl.BlockSpec((rows, width), columns(side)) for side in (0, 1)],
            out_specs=pl.BlockSpec((2, 1, rows, units), lambda i, p, o: (0, i, 0, 0)),
        ),
        out_shape=jax.ShapeDtypeStruct((2, planes, rows, units), BF16),
        cost_estimate=cost(0, 8 * planes * rows * units),
        compiler_params=params(),
        name="pack_core",
    )(place, order, *hbm(first, second, second))


def base_blocks(place, hidden, down, planes, width):
    steps, rows, units = hidden.shape

    def body(place_ref, hidden_ref, d0, d1, d2, d3, send_ref, keep_ref):
        flat = hidden_ref[...].reshape(steps * rows, units)
        for i, ref in enumerate((d0, d1, d2, d3)):
            value = jnp.dot(flat, ref[...], preferred_element_type=F32).reshape(steps, rows, width)
            if i & 1:
                send_ref[i >> 1, 0] = value.astype(BF16)
            else:
                keep_ref[i >> 1, 0] = value

    def columns(other):
        return lambda i, p: (0, (p[0] ^ halving(i, planes)) * PLANE + (p[1] ^ other))

    shape = (2, planes, steps, rows, width)
    return pl.pallas_call(
        body,
        grid_spec=pltpu.PrefetchScalarGridSpec(
            num_scalar_prefetch=1,
            grid=(planes,),
            in_specs=[pl.BlockSpec((steps, rows, units), lambda i, p: (0, 0, 0))]
            + [pl.BlockSpec((units, width), columns(o)) for o in range(PLANE)],
            out_specs=[pl.BlockSpec((2, 1, steps, rows, width), lambda i, p: (0, i, 0, 0, 0))] * 2,
        ),
        out_shape=[jax.ShapeDtypeStruct(shape, BF16), jax.ShapeDtypeStruct(shape, F32)],
        cost_estimate=cost(
            2 * steps * rows * units * down.shape[1], (2 * units + 3 * steps * rows) * down.shape[1]
        ),
        compiler_params=params(),
        name="base_blocks",
    )(place, *hbm(hidden, down, down, down, down))


def low_part(place, order, slots, owners, tables, sources, first_plane, chunk, per_shard, rank):
    planes = len(sources)
    first_step, last_step = chunk
    steps = last_step - first_step
    rows, (_, requests, width) = tables[-1].shape[-2], sources[0][0].shape
    lanes, count = steps * requests, len(owners)
    hidden = [array for source in sources for array in source]

    def body(place_ref, order_ref, slots_ref, *refs):
        factor_refs, hidden_refs = refs[:count], refs[count : count + len(hidden)]
        out_ref, held, factors, total = refs[count + len(hidden) :]
        j = pl.program_id(0)
        at = 0
        for i, source in enumerate(sources):
            for inner in range(len(source)):
                chosen = j == i
                if len(source) > 1:
                    chosen &= place_ref[2] == 1 - inner

                @pl.when(chosen)
                def _(ref=hidden_refs[at]):
                    held[...] = ref[...].reshape(lanes, width)

                at += 1

        @pl.when(j == 0)
        def _():
            total[...] = jnp.zeros_like(total)

        for i, ref in enumerate(factor_refs):
            factors[i * rows : (i + 1) * rows, :] = ref[...].reshape(rows, width)
        total[...] += lax.dot_general(
            factors[...], held[...], (((1,), (1,)), ((), ())), preferred_element_type=F32
        )

        @pl.when(j == planes - 1)
        def _():
            low = jnp.zeros((rank, lanes), F32)
            wanted = slots_ref[...]
            for i, owner in enumerate(owners):
                first = (place_ref[0] * PLANE + (place_ref[1] ^ owner)) * per_shard
                for a in range(per_shard):
                    at = (i * per_shard + a) * rank
                    low += jnp.where(wanted == first + a, total[at : at + rank, :], 0.0)
            out_ref[...] = low

    def factor_spec(owner):
        if owner == 0:
            return pl.BlockSpec(
                (rows, width), lambda j, p, o: (0, o[first_plane + j] * PLANE + p[1])
            )
        if owner == 1:
            return pl.BlockSpec((1, 1, rows, width), lambda j, p, o: (0, first_plane + j, 0, 0))
        return pl.BlockSpec((1, rows, width), lambda j, p, o: (first_plane + j, 0, 0))

    def hidden_spec(array):
        block = first_step // steps if array.shape[0] > steps else 0
        return pl.BlockSpec((steps, requests, width), lambda j, p, o: (block, 0, 0))

    return pl.pallas_call(
        body,
        grid_spec=pltpu.PrefetchScalarGridSpec(
            num_scalar_prefetch=2,
            grid=(planes,),
            in_specs=[
                pl.BlockSpec((1, lanes), lambda j, p, o: (0, 0)),
                *[factor_spec(owner) for owner in owners],
                *[hidden_spec(array) for array in hidden],
            ],
            out_specs=pl.BlockSpec((rank, lanes), lambda j, p, o: (0, 0)),
            scratch_shapes=[
                pltpu.VMEM((lanes, width), BF16),
                pltpu.VMEM((count * rows, width), BF16),
                pltpu.VMEM((count * rows, lanes), F32),
            ],
        ),
        out_shape=jax.ShapeDtypeStruct((rank, lanes), F32),
        cost_estimate=cost(
            2 * lanes * count * rows * planes * width, 2 * (lanes + count * rows) * planes * width, 1
        ),
        compiler_params=params(),
        name="low_part",
    )(place, order, slots, *hbm(*tables, *hidden))


def add_extra(place, low, slots, mine, other, keep, recv, first_step, pieces, per_shard, rank):
    _, planes, _, requests, width = keep.shape
    rows, lanes = mine.shape[0], low.shape[1]
    count, half = len(pieces), planes // 2
    parts = {
        KEEP_Y: ((0,), range(planes)),
        SEND_Y: ((1,), range(planes)),
        KEEP_Z: ((0, 1), range(half)),
        SEND_Z: ((0, 1), range(half, planes)),
    }
    sides = sorted({side for _, what in pieces for side in parts[what][0]})

    def body(place_ref, low_ref, slots_ref, *refs):
        tables, refs = refs[: len(sides) * planes], refs[len(sides) * planes :]
        others, refs = refs[: len(sides)], refs[len(sides) :]
        rounded = low_ref[...].astype(BF16).astype(F32)
        wanted = slots_ref[...]
        spread = []
        for i in range(2):
            first = (place_ref[0] * PLANE + (place_ref[1] ^ i)) * per_shard
            masked = [jnp.where(wanted == first + a, rounded, 0.0) for a in range(per_shard)]
            spread.append(jnp.concatenate(masked, axis=0).T.astype(BF16))
        for n, (step, what) in enumerate(pieces):
            k_ref, r_ref, out_ref = refs[n], refs[count + n], refs[2 * count + n]
            start = (step - first_step) * requests
            here = [value[start : start + requests] for value in spread]
            for side_at, side in enumerate(parts[what][0]):
                at = sides.index(side)
                for block_at, i in enumerate(parts[what][1]):
                    extra = jnp.dot(
                        here[0], tables[at * planes + i][...], preferred_element_type=F32
                    )
                    extra += jnp.dot(here[1], others[at][0, i], preferred_element_type=F32)
                    base = k_ref[side_at, block_at, 0] + r_ref[side_at, block_at, 0].astype(F32)
                    out_ref[side_at, block_at] = (base + extra).astype(out_ref.dtype)

    def columns(i, side):
        return lambda j, p: (0, (p[0] ^ halving(i, planes)) * PLANE + (p[1] ^ (2 * side)))

    def shape(what):
        return (len(parts[what][0]), len(parts[what][1]), requests, width)

    def base(step, what):
        side = 1 if what == SEND_Y else 0
        block = 1 if what == SEND_Z else 0
        n, m, _, _ = shape(what)
        return pl.BlockSpec((n, m, 1, requests, width), lambda i, p: (side, block, step, 0, 0))

    def other_spec(side):
        return pl.BlockSpec((1, planes, rows, width), lambda i, p: (1, 0, 0, side))

    bases = [base(*piece) for piece in pieces]
    return pl.pallas_call(
        body,
        grid_spec=pltpu.PrefetchScalarGridSpec(
            num_scalar_prefetch=1,
            grid=(1,),
            in_specs=[
                pl.BlockSpec((rank, lanes), lambda i, p: (0, 0)),
                pl.BlockSpec((1, lanes), lambda i, p: (0, 0)),
                *[
                    pl.BlockSpec((rows, width), columns(i, side))
                    for side in sides
                    for i in range(planes)
                ],
                *[other_spec(side) for side in sides],
                *bases,
                *bases,
            ],
            out_specs=[pl.BlockSpec(shape(what), lambda i, p: (0, 0, 0, 0)) for _, what in pieces],
        ),
        out_shape=[
            jax.ShapeDtypeStruct(shape(what), BF16 if what in (SEND_Y, SEND_Z) else F32)
            for _, what in pieces
        ],
        cost_estimate=cost(4 * lanes * rows * planes * width, 10 * lanes * planes * width),
        compiler_params=params(),
        name="add_extra",
    )(
        place,
        low,
        slots,
        *hbm(*([mine] * (planes * len(sides))), *([other] * len(sides))),
        *hbm(*([keep] * count), *([recv] * count)),
    )


def local(hidden, down_matrix, first_table, second_table, storage_index, request_adapter):
    steps, requests, units = hidden.shape
    per_shard, rank, all_units = first_table.shape
    features = second_table.shape[2]
    adapters = storage_index.shape[0]
    devices = all_units // units
    planes = devices // PLANE
    width = features // devices
    me = lax.axis_index("tensor").astype(jnp.int32)
    z, w = me // PLANE, me % PLANE
    place = jnp.stack([z, w, ((z == 1) | (z == 2)).astype(jnp.int32)])

    def in_plane(value, other):
        return lax.ppermute(value, "tensor", [(t, t ^ other) for t in range(devices)])

    def along(value, other):
        return lax.ppermute(value, "tensor", [(t, t ^ (other * PLANE)) for t in range(devices)])

    def hop(value, moves):
        pairs = [(a * PLANE + v, b * PLANE + v) for a, b in moves for v in range(PLANE)]
        return lax.ppermute(value, "tensor", pairs)

    table = jnp.arange(adapters, dtype=jnp.int32)
    slot_row = jnp.sum(
        jnp.where(request_adapter[:, None] == table[None, :], storage_index[None, :], 0), axis=1
    ).astype(jnp.int32)

    first = first_table.reshape(per_shard * rank, all_units)
    second = second_table.reshape(per_shard * rank, features)

    if planes == 4:
        order = jnp.stack([z, z ^ 1, jnp.where(z < 2, 2, 1), jnp.where(z < 2, 3, 0)])
    else:
        order = jnp.stack([z ^ o for o in range(planes)])
    split = planes // 2

    for_near = pack_factors(place, order, first, units, 2)
    near_y = in_plane(for_near, 2)
    hidden_z = hidden
    if planes == 4:
        near = along(hidden_z, 1)
        middle = hop(hidden_z, ((1, 2), (2, 1)))
    else:
        blocks = [hidden] + [along(hidden_z, o) for o in range(1, planes)]
        near = middle = blocks[1]
    for_far = pack_factors(place, order, after(first, for_near), units, 3)
    for_core = pack_core(place, order, after(first, for_far), second, width)
    send, keep = base_blocks(place, after(hidden, for_core), down_matrix, planes, width)
    near, middle, send, near_y = lax.optimization_barrier((near, middle, send, near_y))
    from_core = in_plane(after(for_core, near), 1)
    far_y = in_plane(after(for_far, near_y), 3)
    recv = in_plane(send, 1)

    at_hand = [[hidden], [near]] if planes == 4 else [[block] for block in blocks[:split]]
    slots = jnp.tile(slot_row[None, :], (1, steps))

    def low_at(chunk, owners, tables, sources, first_plane):
        lanes = slots[:, chunk[0] * requests : chunk[1] * requests]
        return low_part(
            place, order, lanes, owners, tables, sources, first_plane, chunk, per_shard, rank
        )

    def early_of(*ready):
        near_by = (first, after(from_core, *ready), near_y)
        part = low_at((0, steps), (0, 1, 2), near_by, at_hand, 0)
        return part, low_at((0, steps), (3,), (after(far_y, part),), at_hand, 0)

    def late_of(chunk, plane, source, *ready):
        tables = (first, after(from_core, *ready), near_y, far_y)
        return low_at(chunk, range(PLANE), tables, [source], plane)

    if planes == 4:
        outward, across = ((1, 0), (2, 3)), ((1, 2), (2, 1))
        (a, b), (c, d) = LOW_CHUNKS
        outer_one = hop(middle[a:b], outward)
        middle_two = hop(near[a:b], across)
        outer_two = hop(after(middle_two, outer_one), outward)
        early, early_far = early_of(outer_one, middle_two)
        part = late_of((a, b), 2, [middle, outer_one], early_far)
        late = [[part, [middle_two, outer_two]]]
        middle_two = hop(after(near[c:d], middle_two), across)
        outer_one = hop(after(middle[c:d], outer_one), outward)
        outer_two = hop(after(middle_two, outer_two, part), outward)
        late.append([[middle, outer_one], [middle_two, outer_two]])
        second_wave = [outer_one]
    else:
        early, early_far = early_of()
        late = [[[block] for block in blocks[split:]] for _ in LOW_CHUNKS]
        second_wave = []

    def core_sum(chunk, parts):
        low = (early + early_far)[:, chunk[0] * requests : chunk[1] * requests]
        for part in parts:
            low = low + part
        return low + in_plane(low, 1)

    def with_extra(low, first_step, pieces):
        lanes = slots[:, : low.shape[1]]
        return add_extra(
            place, low, lanes, second, from_core, keep, recv, first_step, pieces, per_shard, rank
        )

    along_z = [1 << bit for bit in range(planes.bit_length() - 1)]
    y_first, z_first = ["y", *along_z], [*along_z[:1], "y", *along_z[1:]]
    plans = [list(plan) for plan in (y_first, z_first, y_first, z_first)]
    state = [None] * steps

    def send(value, stage):
        return in_plane(value, 2) if stage == "y" else along(value, stage)

    def add(c, *ready):
        value, received = state[c]
        total = value + after(received, *ready).astype(F32)
        plans[c].pop(0)
        if not plans[c]:
            state[c] = (total, None)
            return total
        count = total.shape[0] // 2
        stays, goes = total[:count], total[count:].astype(BF16)
        if plans[c][0] == "y":
            stays, goes = stays[0], goes[0]
        state[c] = (stays, send(goes, plans[c][0]))
        return goes

    def begin(c, stays, goes):
        if plans[c][0] == "y":
            stays, goes = stays[0], goes[0]
        state[c] = (stays, send(goes, plans[c][0]))

    parts, ready = [], early_far
    for i, source in enumerate(late[0]):
        part = late_of(LOW_CHUNKS[0], split + i, source, ready) if isinstance(source, list) else source
        parts.append(part)
        ready = part
    low = core_sum(LOW_CHUNKS[0], parts)
    low = low + in_plane(low, 2)
    (goes,) = with_extra(low[:, :requests], 0, [(0, SEND_Y)])
    low = after(low, goes, *second_wave)
    moved = send(goes[0], "y")
    stays, goes, next_stays = with_extra(low, 0, [(0, KEEP_Y), (1, SEND_Z), (1, KEEP_Z)])
    state[0] = (stays[0], moved)
    parts, ready = [], (stays, goes, next_stays)
    for i, source in enumerate(late[1]):
        source = [after(array, *ready) for array in source]
        parts.append(late_of(LOW_CHUNKS[1], split + i, source, *ready))
        ready = (parts[-1],)
    begin(1, next_stays, after(goes, parts[0]))

    low = core_sum(LOW_CHUNKS[1], parts)
    across_y = in_plane(low, 2)
    done = add(0, low)
    low = low + after(across_y, done)
    moved, stays, goes, next_stays = with_extra(
        low, 2, [(2, SEND_Y), (2, KEEP_Y), (3, SEND_Z), (3, KEEP_Z)]
    )
    begin(2, stays, moved)
    begin(3, next_stays, goes)
    done = next_stays
    for c in (1, 0, 2, 1, 3, 0, 2, 3, 1, 2, 3):
        if plans[c]:
            done = add(c, done)
    for c in range(steps):
        while plans[c]:
            done = add(c, done)
    outputs = [value.astype(BF16) for value, _ in state]
    return jnp.concatenate(outputs, axis=0)


def solution(mesh):
    in_specs = (
        P(None, "groups", "tensor"),
        P("tensor", None),
        P(("groups", "tensor"), None, None),
        P(("groups", "tensor"), None, None),
        P("groups"),
        P("groups"),
    )
    out_specs = P(None, "groups", "tensor")
    return jax.shard_map(local, mesh=mesh, in_specs=in_specs, out_specs=out_specs, check_vma=False)
```

time: 185 us -> 146 us (0.79)
  waiting for transfers between devices: 101 us -> 54.4 us
  starting transfers between devices: 24.2 us -> 34.4 us
  local copies, waits for them, and re-layouts: 4.18 us -> 1.41 us
    ppermute x7, waiting for transfers between devices: 35.9 us -> 19.1 us  [hop(): return lax.ppermute(value, 'tensor', pairs)]
    ppermute x13 -> x12, waiting for transfers between devices: 36.4 us -> 20.6 us  [in_plane(): lax.ppermute(value, 'tensor', [(t, t ^ other) for t in range(devices)])]
    ppermute x7 -> x9, waiting for transfers between devices: 28.5 us -> 14.8 us  [along(): lax.ppermute(value, 'tensor', [(t, t ^ other * PLANE) for t in range(devi...]
    ppermute x7 -> x9, starting transfers between devices: 10.1 us -> 17.3 us  [along(): lax.ppermute(value, 'tensor', [(t, t ^ other * PLANE) for t in range(devi...]
    pallas_call x3 -> x6, Pallas kernels: 12 us -> 17.7 us  [low_part(): pl.pallas_call(body, grid_spec=pltpu.PrefetchScalarGridSpec(num_scalar_pr...]
    pallas_call x6 -> x3, Pallas kernels: 18.4 us -> 12.8 us  [add_extra(): pl.pallas_call(body, grid_spec=pltpu.PrefetchScalarGridSpec(num_scalar_pr...]
    ppermute x13 -> x12, starting transfers between devices: 6.92 us -> 9.92 us  [in_plane(): lax.ppermute(value, 'tensor', [(t, t ^ other) for t in range(devices)])]
  transfers between devices with their start and end apart: 27 -> 28, of which waited for: 16 -> 17; matrix products, arithmetic and copies ran while one was open for 2% -> 1% of each run, Pallas kernels for 27% -> 35%
where the time goes in v3:
time: 146 us
  waiting for transfers between devices  54.4 us (37%)
  Pallas kernels  52.4 us (36%)
  starting transfers between devices  34.4 us (24%)
  other arithmetic  2.35 us (2%)
    ppermute x12, waiting for transfers between devices, in_plane(): lax.ppermute(value, 'tensor', [(t, t ^ other) for t in range(devices)])  20.6 us
    ppermute x7, waiting for transfers between devices, hop(): return lax.ppermute(value, 'tensor', pairs)  19.1 us
    pallas_call x6, Pallas kernels, low_part(): pl.pallas_call(body, grid_spec=pltpu.PrefetchScalarGridSpec(num_scalar_pr...  17.7 us
    ppermute x9, starting transfers between devices, along(): lax.ppermute(value, 'tensor', [(t, t ^ other * PLANE) for t in range(devi...  17.3 us
    pallas_call x1, Pallas kernels, base_blocks(): pl.pallas_call(body, grid_spec=pltpu.PrefetchScalarGridSpec(num_scalar_pr...  15.2 us
    ppermute x9, waiting for transfers between devices, along(): lax.ppermute(value, 'tensor', [(t, t ^ other * PLANE) for t in range(devi...  14.8 us
    pallas_call x3, Pallas kernels, add_extra(): pl.pallas_call(body, grid_spec=pltpu.PrefetchScalarGridSpec(num_scalar_pr...  12.8 us
    ppermute x12, starting transfers between devices, in_plane(): lax.ppermute(value, 'tensor', [(t, t ^ other) for t in range(devices)])  9.92 us
  transfers between devices with their start and end apart: 28, of which 17 were waited for; matrix products, arithmetic and copies ran while one was open for 1% of the time, Pallas kernels for 35%

profile of v3, /device:TPU:0, one launch (start us, length us, event | category | flops | bytes accessed | tf_op | source)
XLA Modules:
  0.0 145.6 jit_solution(1804143591592190888)
XLA Ops:
  0.2 1.8 %pack_factors.2 = bf16[4,128,1024]{2,1,0:T(8,128)(2,1)S(1)} custom-call(s32[3]{0:T(128)S(1)} %pad_add_fusion.place_ref, s32[4]{0:T(128)S(1)} %pad_add_fusion.1.order_ref, bf16[128,16384]{1,0:T(8,128)(2,1)} %bitcast.55, bf16[128,16384]{1,0:T(8,128)(2,1)} %bitcast.56, bf16[128,16384]{1,0:T(8,128)(2,1)} %bitcast.57, bf16[128,16384]{1,0:T(8,128)(2,1)} %bitcast.58), custom_call_target="tpu_custom_call" | custom-call | bytes 2097 | tf_op jit(solution)/shard_map/pack_factors/pallas_call | solution.py:53
  2.0 3.0 %collective-permute-start.2 = (bf16[4,128,1024]{2,1,0:T(8,128)(2,1)S(1)}, bf16[4,128,1024]{2,1,0:T(8,128)(2,1)S(1)}, u32[]{:S(2)}, u32[]{:S(2)}) collective-permute-start(bf16[4,128,1024]{2,1,0:T(8,128)(2,1)S(1)} %pack_factors.2), channel_id=1, source_target_pairs={{0,2},{1,3},{2,0},{3,1},{4,6},{5,7},{6,4},{7,5},{8,10},{9,11},{10,... | collective-permute-start | bytes 3145736 | tf_op jit(solution)/shard_map/ppermute | solution.py:318
  5.0 0.7 collective-permute-start.1
  5.7 4.4 %collective-permute-start = (bf16[4,128,1024]{2,1,0:T(8,128)(2,1)S(1)}, bf16[4,128,1024]{2,1,0:T(8,128)(2,1)S(1)}, u32[]{:S(2)}, u32[]{:S(2)}) collective-permute-start(bf16[4,128,1024]{2,1,0:T(8,128)(2,1)S(1)} %copy-done.3), channel_id=1, source_target_pairs={{0,4},{1,5},{2,6},{3,7},{4,0},{5,1},{6,2},{7,3},{8,12},{9,13},{10,... | collective-permute-start | bytes 3145736 | tf_op jit(solution)/shard_map/ppermute | solution.py:321
  10.1 1.8 %pack_factors.3 = bf16[4,128,1024]{2,1,0:T(8,128)(2,1)S(1)} custom-call(s32[3]{0:T(128)S(1)} %pad_add_fusion.place_ref, s32[4]{0:T(128)S(1)} %pad_add_fusion.1.order_ref, bf16[128,16384]{1,0:T(8,128)(2,1)} %bitcast.59, bf16[128,16384]{1,0:T(8,128)(2,1)} %bitcast.60, bf16[128,16384]{1,0:T(8,128)(2,1)} %bitcast.61, bf16[128,16384]{1,0:T(8,128)(2,1)} %bitcast.62), custom_call_target="tpu_custom_call" | custom-call | bytes 2097 | tf_op jit(solution)/shard_map/pack_factors/pallas_call | solution.py:53
  11.9 3.1 %pack_core.1 = bf16[2,4,128,1024]{3,2,1,0:T(8,128)(2,1)S(1)} custom-call(s32[3]{0:T(128)S(1)} %pad_add_fusion.place_ref, s32[4]{0:T(128)S(1)} %pad_add_fusion.1.order_ref, bf16[128,16384]{1,0:T(8,128)(2,1)} %bitcast.63, bf16[128,8192]{1,0:T(8,128)(2,1)} %bitcast.33, bf16[128,8192]{1,0:T(8,128)(2,1)} %bitcast.34), custom_call_target="tpu_custom_call" | custom-call | bytes 4194 | tf_op jit(solution)/shard_map/pack_core/pallas_call | solution.py:83
  15.1 15.2 %base_blocks.1 = (bf16[2,4,4,128,512]{4,3,2,1,0:T(8,128)(2,1)S(1)}, f32[2,4,4,128,512]{4,3,2,1,0:T(8,128)}) custom-call(s32[3]{0:T(128)S(1)} %pad_add_fusion.place_ref, bf16[4,128,1024]{2,1,0:T(8,128)(2,1)} %refs_1_.1, bf16[1024,8192]{1,0:T(8,128)(2,1)} %d3.1, bf16[1024,8192]{1,0:T(8,128)(2,1)} %d3.1, bf16[1024,8192]{1,0:T(8,128)(2,1)} %d3.1, ...), custom_call_target="tpu_custom_call" | custom-call | flops 8589934 | bytes 29360 | tf_op jit(solution)/shard_map/base_blocks/pallas_call | solution.py:115
  30.4 2.4 %collective-permute-done.refs_4_.refs_2_ = bf16[4,128,1024]{2,1,0:T(8,128)(2,1)S(1)} collective-permute-done((bf16[4,128,1024]{2,1,0:T(8,128)(2,1)S(1)}, bf16[4,128,1024]{2,1,0:T(8,128)(2,1)S(1)}, u32[]{:S(2)}, u32[]{:S(2)}) %collective-permute-start) | collective-permute-done | bytes 1048608 | tf_op jit(solution)/shard_map/ppermute | solution.py:321
  34.3 1.3 collective-permute-start.4
  35.6 16.0 %collective-permute-done.4.refs_5_ = bf16[2,128,1024]{2,1,0:T(8,128)(2,1)S(1)} collective-permute-done((bf16[2,128,1024]{2,1,0:T(8,128)(2,1)S(1)}, bf16[2,128,1024]{2,1,0:T(8,128)(2,1)S(1)}, u32[]{:S(2)}, u32[]{:S(2)}) %collective-permute-start.4) | collective-permute-done | bytes 524320 | tf_op jit(solution)/shard_map/ppermute | solution.py:325
  51.6 1.3 collective-permute-start.7
  53.8 1.3 collective-permute-start.11
  55.1 4.0 %low_part.6 = f32[16,512]{1,0:T(8,128)S(1)} custom-call(s32[3]{0:T(128)S(1)} %pad_add_fusion.place_ref, s32[4]{0:T(128)S(1)} %pad_add_fusion.1.order_ref, s32[1,512]{1,0:T(1,128)S(1)} %bitcast.29, bf16[128,16384]{1,0:T(8,128)(2,1)} %bitcast.64, bf16[2,4,128,1024]{3,2,1,0:T(8,128)(2,1)} %copy-done, bf16[4,128,1024]{2,1,0:T(8,128)(2,1)} %copy-done.2, ...), custom_call_target="tpu_custom_call" | custom-call | flops 805306368 | bytes 3670016 | tf_op jit(solution)/shard_map/low_part/pallas_call | solution.py:192
  59.4 1.0 copy-done.1
  60.4 3.4 %low_part.7 = f32[16,512]{1,0:T(8,128)S(1)} custom-call(s32[3]{0:T(128)S(1)} %pad_add_fusion.place_ref, s32[4]{0:T(128)S(1)} %pad_add_fusion.1.order_ref, s32[1,512]{1,0:T(1,128)S(1)} %bitcast.30, bf16[4,128,1024]{2,1,0:T(8,128)(2,1)} %copy-done.1, bf16[4,128,1024]{2,1,0:T(8,128)(2,1)} %refs_1_.1, bf16[4,128,1024]{2,1,0:T(8,128)(2,1)} %copy-done.4), custom_call_target="tpu_custom_call" | custom-call | flops 268435456 | bytes 2621440 | tf_op jit(solution)/shard_map/low_part/pallas_call | solution.py:192
  63.7 2.6 %low_part.8 = f32[16,256]{1,0:T(8,128)S(1)} custom-call(s32[3]{0:T(128)S(1)} %pad_add_fusion.place_ref, s32[4]{0:T(128)S(1)} %pad_add_fusion.1.order_ref, s32[1,256]{1,0:T(1,128)S(1)} %get-tuple-element.103.slots_ref, bf16[128,16384]{1,0:T(8,128)(2,1)} %bitcast.65, bf16[2,4,128,1024]{3,2,1,0:T(8,128)(2,1)} %copy-done, bf16[4,128,1024]{2,1,0:T(8,128)(2,1)} %copy-done.2, ...), custom_call_target="tpu_custom_call" | custom-call | flops 268435456 | bytes 1572864 | tf_op jit(solution)/shard_map/low_part/pallas_call | solution.py:192
  66.3 2.0 %collective-permute-done.7.refs_5_ = bf16[2,128,1024]{2,1,0:T(8,128)(2,1)} collective-permute-done((bf16[2,128,1024]{2,1,0:T(8,128)(2,1)S(1)}, bf16[2,128,1024]{2,1,0:T(8,128)(2,1)}, u32[]{:S(2)}, u32[]{:S(2)}) %collective-permute-start.7) | collective-permute-done | bytes 524320 | tf_op jit(solution)/shard_map/ppermute | solution.py:325
  68.3 1.3 collective-permute-start.14
  69.6 2.6 %low_part.9 = f32[16,256]{1,0:T(8,128)S(1)} custom-call(s32[3]{0:T(128)S(1)} %pad_add_fusion.place_ref, s32[4]{0:T(128)S(1)} %pad_add_fusion.1.order_ref, s32[1,256]{1,0:T(1,128)S(1)} %get-tuple-element.103.slots_ref, bf16[128,16384]{1,0:T(8,128)(2,1)} %bitcast.66, bf16[2,4,128,1024]{3,2,1,0:T(8,128)(2,1)} %copy-done, bf16[4,128,1024]{2,1,0:T(8,128)(2,1)} %copy-done.2, ...), custom_call_target="tpu_custom_call" | custom-call | flops 268435456 | bytes 1572864 | tf_op jit(solution)/shard_map/low_part/pallas_call | solution.py:192
  72.3 1.2 collective-permute-done.8
  73.5 1.3 collective-permute-start.9
  74.8 2.4 %collective-permute-done.9 = f32[16,256]{1,0:T(8,128)S(1)} collective-permute-done((f32[16,256]{1,0:T(8,128)S(1)}, f32[16,256]{1,0:T(8,128)S(1)}, u32[]{:S(2)}, u32[]{:S(2)}) %collective-permute-start.9) | collective-permute-done | bytes 16416 | tf_op jit(solution)/shard_map/ppermute | solution.py:318
  77.3 2.8 %add_extra.3 = bf16[1,4,128,512]{3,2,1,0:T(8,128)(2,1)S(1)} custom-call(s32[3]{0:T(128)S(1)} %pad_add_fusion.place_ref, f32[16,128]{1,0:T(8,128)S(1)} %slice.118.low_ref, s32[1,128]{1,0:T(1,128)S(1)} %slice.119.slots_ref, bf16[128,8192]{1,0:T(8,128)(2,1)} %bitcast.35, bf16[128,8192]{1,0:T(8,128)(2,1)} %bitcast.36, bf16[128,8192]{1,0:T(8,128)(2,1)} %bitcast.37, ...), custom_call_target="tpu_custom_call" | custom-call | flops 134217 | bytes 2621 | tf_op jit(solution)/shard_map/add_extra/pallas_call | solution.py:270
  80.1 1.4 collective-permute-start.12
  81.5 4.6 %add_extra.4 = (f32[1,4,128,512]{3,2,1,0:T(8,128)S(1)}, bf16[2,2,128,512]{3,2,1,0:T(8,128)(2,1)S(1)}, f32[2,2,128,512]{3,2,1,0:T(8,128)S(1)}) custom-call(s32[3]{0:T(128)S(1)} %pad_add_fusion.place_ref, f32[16,256]{1,0:T(8,128)S(1)} %add.74.low_ref, s32[1,256]{1,0:T(1,128)S(1)} %get-tuple-element.103.slots_ref, bf16[128,8192]{1,0:T(8,128)(2,1)} %bitcast.39, ...), custom_call_target="tpu_custom_call" | custom-call | flops 268435 | bytes 5242 | tf_op jit(solution)/shard_map/add_extra/pallas_call | solution.py:270
  86.1 2.6 %low_part.10 = f32[16,256]{1,0:T(8,128)S(1)} custom-call(s32[3]{0:T(128)S(1)} %pad_add_fusion.place_ref, s32[4]{0:T(128)S(1)} %pad_add_fusion.1.order_ref, s32[1,256]{1,0:T(1,128)S(1)} %get-tuple-element.104.slots_ref, bf16[128,16384]{1,0:T(8,128)(2,1)} %bitcast.67, bf16[2,4,128,1024]{3,2,1,0:T(8,128)(2,1)} %copy-done, bf16[4,128,1024]{2,1,0:T(8,128)(2,1)} %copy-done.2, ...), custom_call_target="tpu_custom_call" | custom-call | flops 268435456 | bytes 1572864 | tf_op jit(solution)/shard_map/low_part/pallas_call | solution.py:192
  88.7 1.1 collective-permute-done.14.refs_5_
  89.8 3.2 %collective-permute-start.17 = (bf16[2,2,128,512]{3,2,1,0:T(8,128)(2,1)S(1)}, bf16[2,2,128,512]{3,2,1,0:T(8,128)(2,1)S(1)}, u32[]{:S(2)}, u32[]{:S(2)}) collective-permute-start(bf16[2,2,128,512]{3,2,1,0:T(8,128)(2,1)S(1)} %get-tuple-element.82), channel_id=1, source_target_pairs={{0,4},{1,5},{2,6},{3,7},{4,0},{5,1},{6,2},{7,3},{8,12},{9,13},{10,... | collective-permute-start | bytes 1572872 | tf_op jit(solution)/shard_map/ppermute | solution.py:321
  92.9 2.6 %low_part.11 = f32[16,256]{1,0:T(8,128)S(1)} custom-call(s32[3]{0:T(128)S(1)} %pad_add_fusion.place_ref, s32[4]{0:T(128)S(1)} %pad_add_fusion.1.order_ref, s32[1,256]{1,0:T(1,128)S(1)} %get-tuple-element.104.slots_ref, bf16[128,16384]{1,0:T(8,128)(2,1)} %bitcast.68, bf16[2,4,128,1024]{3,2,1,0:T(8,128)(2,1)} %copy-done, bf16[4,128,1024]{2,1,0:T(8,128)(2,1)} %copy-done.2, ...), custom_call_target="tpu_custom_call" | custom-call | flops 268435456 | bytes 1572864 | tf_op jit(solution)/shard_map/low_part/pallas_call | solution.py:192
  95.6 1.2 collective-permute-done.15
  97.8 2.8 %collective-permute-done.18 = f32[16,256]{1,0:T(8,128)S(1)} collective-permute-done((f32[16,256]{1,0:T(8,128)S(1)}, f32[16,256]{1,0:T(8,128)S(1)}, u32[]{:S(2)}, u32[]{:S(2)}) %collective-permute-start.18) | collective-permute-done | bytes 16416 | tf_op jit(solution)/shard_map/ppermute | solution.py:318
  100.5 0.7 collective-permute-start.16
  101.3 5.3 %add_extra.5 = (bf16[1,4,128,512]{3,2,1,0:T(8,128)(2,1)S(1)}, f32[1,4,128,512]{3,2,1,0:T(8,128)S(1)}, bf16[2,2,128,512]{3,2,1,0:T(8,128)(2,1)S(1)}, f32[2,2,128,512]{3,2,1,0:T(8,128)S(1)}) custom-call(s32[3]{0:T(128)S(1)} %pad_add_fusion.place_ref, f32[16,256]{1,0:T(8,128)S(1)} %add.79.low_ref, s32[1,256]{1,0:T(1,128)S(1)} %get-tuple-element.103.slots_ref, ...), custom_call_target="tpu_custom_call" | custom-call | flops 268435 | bytes 5242 | tf_op jit(solution)/shard_map/add_extra/pallas_call | solution.py:270
  106.6 1.4 collective-permute-start.20
  108.9 1.4 collective-permute-start.21
  110.5 2.8 %collective-permute-start.19 = (bf16[1,128,512]{2,1,0:T(8,128)(2,1)S(1)}, bf16[1,128,512]{2,1,0:T(8,128)(2,1)S(1)}, u32[]{:S(2)}, u32[]{:S(2)}) collective-permute-start(bf16[1,128,512]{2,1,0:T(8,128)(2,1)S(1)} %slice.175), channel_id=1, source_target_pairs={{0,8},{1,9},{2,10},{3,11},{4,12},{5,13},{6,14},{7,15},{8,0},{9,1},... | collective-permute-start | bytes 393224 | tf_op jit(solution)/shard_map/ppermute | solution.py:321
  113.3 9.6 %collective-permute-done.22 = bf16[4,128,512]{2,1,0:T(8,128)(2,1)S(1)} collective-permute-done((bf16[4,128,512]{2,1,0:T(8,128)(2,1)S(1)}, bf16[4,128,512]{2,1,0:T(8,128)(2,1)S(1)}, u32[]{:S(2)}, u32[]{:S(2)}) %collective-permute-start.22) | collective-permute-done | bytes 524320 | tf_op jit(solution)/shard_map/ppermute | solution.py:318
  123.1 0.8 collective-permute-start.25
  123.9 2.3 %collective-permute-done.21 = bf16[2,128,512]{2,1,0:T(8,128)(2,1)S(1)} collective-permute-done((bf16[2,128,512]{2,1,0:T(8,128)(2,1)S(1)}, bf16[2,128,512]{2,1,0:T(8,128)(2,1)S(1)}, u32[]{:S(2)}, u32[]{:S(2)}) %collective-permute-start.21) | collective-permute-done | bytes 262176 | tf_op jit(solution)/shard_map/ppermute | solution.py:318
  126.3 1.3 collective-permute-start.23
  128.5 3.8 %collective-permute-done.25 = bf16[2,128,512]{2,1,0:T(8,128)(2,1)S(1)} collective-permute-done((bf16[2,128,512]{2,1,0:T(8,128)(2,1)S(1)}, bf16[2,128,512]{2,1,0:T(8,128)(2,1)S(1)}, u32[]{:S(2)}, u32[]{:S(2)}) %collective-permute-start.25) | collective-permute-done | bytes 262176 | tf_op jit(solution)/shard_map/ppermute | solution.py:321
  132.3 1.0 collective-permute-start.26
  133.3 1.0 collective-permute-done.24
  134.4 1.7 %collective-permute-start.27 = (bf16[1,128,512]{2,1,0:T(8,128)(2,1)S(1)}, bf16[1,128,512]{2,1,0:T(8,128)(2,1)S(1)}, u32[]{:S(2)}, u32[]{:S(2)}) collective-permute-start(bf16[1,128,512]{2,1,0:T(8,128)(2,1)S(1)} %slice.172), channel_id=1, source_target_pairs={{0,8},{1,9},{2,10},{3,11},{4,12},{5,13},{6,14},{7,15},{8,0},{9,1},... | collective-permute-start | bytes 393224 | tf_op jit(solution)/shard_map/ppermute | solution.py:321
  136.1 3.3 %collective-permute-done.23 = bf16[1,128,512]{2,1,0:T(8,128)(2,1)S(1)} collective-permute-done((bf16[1,128,512]{2,1,0:T(8,128)(2,1)S(1)}, bf16[1,128,512]{2,1,0:T(8,128)(2,1)S(1)}, u32[]{:S(2)}, u32[]{:S(2)}) %collective-permute-start.23) | collective-permute-done | bytes 131104 | tf_op jit(solution)/shard_map/ppermute | solution.py:321
  139.5 3.8 %collective-permute-done.26 = bf16[1,128,512]{2,1,0:T(8,128)(2,1)S(1)} collective-permute-done((bf16[1,128,512]{2,1,0:T(8,128)(2,1)S(1)}, bf16[1,128,512]{2,1,0:T(8,128)(2,1)S(1)}, u32[]{:S(2)}, u32[]{:S(2)}) %collective-permute-start.26) | collective-permute-done | bytes 131104 | tf_op jit(solution)/shard_map/ppermute | solution.py:321
  143.4 1.4 collective-permute-done.27
  144.8 0.9 pad_maximum_fusion
  (84 shorter events, 6.5 us)
Async XLA Ops:
  0.2 4.8 %copy-start.3 = (bf16[4,128,1024]{2,1,0:T(8,128)(2,1)S(1)}, bf16[4,128,1024]{2,1,0:T(8,128)(2,1)}, u32[]{:S(2)}) copy-start(bf16[4,128,1024]{2,1,0:T(8,128)(2,1)} %refs_1_.1) | copy-start | bytes 3145732
  2.0 28.4 %collective-permute-start.2 = (bf16[4,128,1024]{2,1,0:T(8,128)(2,1)S(1)}, bf16[4,128,1024]{2,1,0:T(8,128)(2,1)S(1)}, u32[]{:S(2)}, u32[]{:S(2)}) collective-permute-start(bf16[4,128,1024]{2,1,0:T(8,128)(2,1)S(1)} %pack_factors.2), channel_id=1, source_target_pairs={{0,2},{1,3},{2,0},{3,1},{4,6},{5,7},{6,4},{7,5},{8,10},{9,11},{10,... | collective-permute-start | bytes 3145736 | tf_op jit(solution)/shard_map/ppermute | solution.py:318
  5.0 25.3 %collective-permute-start.1 = (bf16[4,128,1024]{2,1,0:T(8,128)(2,1)S(1)}, bf16[4,128,1024]{2,1,0:T(8,128)(2,1)S(1)}, u32[]{:S(2)}, u32[]{:S(2)}) collective-permute-start(bf16[4,128,1024]{2,1,0:T(8,128)(2,1)S(1)} %copy-done.3), channel_id=1, source_target_pairs={{4,8},{5,9},{6,10},{7,11},{8,4},{9,5},{10,6},{11,7},{20,24},{21,25... | collective-permute-start | bytes 3145736 | tf_op jit(solution)/shard_map/ppermute | solution.py:325
  5.7 27.0 %collective-permute-start = (bf16[4,128,1024]{2,1,0:T(8,128)(2,1)S(1)}, bf16[4,128,1024]{2,1,0:T(8,128)(2,1)S(1)}, u32[]{:S(2)}, u32[]{:S(2)}) collective-permute-start(bf16[4,128,1024]{2,1,0:T(8,128)(2,1)S(1)} %copy-done.3), channel_id=1, source_target_pairs={{0,4},{1,5},{2,6},{3,7},{4,0},{5,1},{6,2},{7,3},{8,12},{9,13},{10,... | collective-permute-start | bytes 3145736 | tf_op jit(solution)/shard_map/ppermute | solution.py:321
  30.3 23.2 %copy-start.11 = (s32[128]{0:T(128)S(1)}, s32[128]{0:T(128)}, u32[]{:S(2)}) copy-start(s32[128]{0:T(128)} %param.10) | copy-start | bytes 1540
  30.3 23.3 %copy-start.12 = (s32[128]{0:T(128)S(1)}, s32[128]{0:T(128)}, u32[]{:S(2)}) copy-start(s32[128]{0:T(128)} %param.11) | copy-start | bytes 1540
  30.3 24.8 %copy-start.2 = (bf16[4,128,1024]{2,1,0:T(8,128)(2,1)}, bf16[4,128,1024]{2,1,0:T(8,128)(2,1)S(1)}, u32[]{:S(2)}) copy-start(bf16[4,128,1024]{2,1,0:T(8,128)(2,1)S(1)} %collective-permute-done.2.refs_2_) | copy-start | bytes 3145732
  30.3 28.8 %copy-start.5 = (bf16[4,128,1024]{2,1,0:T(8,128)(2,1)}, bf16[4,128,1024]{2,1,0:T(8,128)(2,1)S(1)}, u32[]{:S(2)}) copy-start(bf16[4,128,1024]{2,1,0:T(8,128)(2,1)S(1)} %collective-permute-done.1.refs_4_) | copy-start | bytes 3145732
  32.7 22.4 %copy-start.4 = (bf16[4,128,1024]{2,1,0:T(8,128)(2,1)}, bf16[4,128,1024]{2,1,0:T(8,128)(2,1)S(1)}, u32[]{:S(2)}) copy-start(bf16[4,128,1024]{2,1,0:T(8,128)(2,1)S(1)} %collective-permute-done.refs_4_.refs_2_) | copy-start | bytes 3145732
  32.7 44.5 %collective-permute-start.10 = (bf16[2,4,4,128,512]{4,3,2,1,0:T(8,128)(2,1)S(1)}, bf16[2,4,4,128,512]{4,3,2,1,0:T(8,128)(2,1)}, u32[]{:S(2)}, u32[]{:S(2)}) collective-permute-start(bf16[2,4,4,128,512]{4,3,2,1,0:T(8,128)(2,1)S(1)} %get-tuple-element.67), channel_id=1, source_target_pairs={{0,1},{1,0},{2,3},{3,2},{4,5},{5,4},{6,7},{7,6},{8,9},{9,8},{10,11... | collective-permute-start | bytes 12582920 | tf_op jit(solution)/shard_map/ppermute | solution.py:318
  32.7 21.0 %collective-permute-start.3 = (bf16[2,4,128,1024]{3,2,1,0:T(8,128)(2,1)S(1)}, bf16[2,4,128,1024]{3,2,1,0:T(8,128)(2,1)S(1)}, u32[]{:S(2)}, u32[]{:S(2)}) collective-permute-start(bf16[2,4,128,1024]{3,2,1,0:T(8,128)(2,1)S(1)} %pack_core.1), channel_id=1, source_target_pairs={{0,1},{1,0},{2,3},{3,2},{4,5},{5,4},{6,7},{7,6},{8,9},{9,8},{10,11... | collective-permute-start | bytes 6291464 | tf_op jit(solution)/shard_map/ppermute | solution.py:318
  33.3 2.3 %collective-permute-start.5 = (bf16[2,128,1024]{2,1,0:T(8,128)(2,1)S(1)}, bf16[2,128,1024]{2,1,0:T(8,128)(2,1)S(1)}, u32[]{:S(2)}, u32[]{:S(2)}) collective-permute-start(bf16[2,128,1024]{2,1,0:T(8,128)(2,1)S(1)} %get-tuple-element.100), channel_id=1, source_target_pairs={{4,8},{5,9},{6,10},{7,11},{8,4},{9,5},{10,6},{11,7},{20,24},{21,25... | collective-permute-start | bytes 1572872 | tf_op jit(solution)/shard_map/ppermute | solution.py:325
  34.0 25.3 %collective-permute-start.6 = (bf16[4,128,1024]{2,1,0:T(8,128)(2,1)S(1)}, bf16[4,128,1024]{2,1,0:T(8,128)(2,1)S(1)}, u32[]{:S(2)}, u32[]{:S(2)}) collective-permute-start(bf16[4,128,1024]{2,1,0:T(8,128)(2,1)S(1)} %pack_factors.3), channel_id=1, source_target_pairs={{0,3},{1,2},{2,1},{3,0},{4,7},{5,6},{6,5},{7,4},{8,11},{9,10},{10,... | collective-permute-start | bytes 3145736 | tf_op jit(solution)/shard_map/ppermute | solution.py:318
  34.3 17.3 %collective-permute-start.4 = (bf16[2,128,1024]{2,1,0:T(8,128)(2,1)S(1)}, bf16[2,128,1024]{2,1,0:T(8,128)(2,1)S(1)}, u32[]{:S(2)}, u32[]{:S(2)}) collective-permute-start(bf16[2,128,1024]{2,1,0:T(8,128)(2,1)S(1)} %get-tuple-element.102), channel_id=1, source_target_pairs={{4,0},{5,1},{6,2},{7,3},{8,12},{9,13},{10,14},{11,15},{20,16},{21,... | collective-permute-start | bytes 1572872 | tf_op jit(solution)/shard_map/ppermute | solution.py:325
  35.6 34.0 %copy-start.10 = (bf16[2,128,1024]{2,1,0:T(8,128)(2,1)}, bf16[2,128,1024]{2,1,0:T(8,128)(2,1)S(1)}, u32[]{:S(2)}) copy-start(bf16[2,128,1024]{2,1,0:T(8,128)(2,1)S(1)} %collective-permute-done.5.refs_4_) | copy-start | bytes 1572868
  51.6 12.2 %copy-start.7 = (bf16[2,128,1024]{2,1,0:T(8,128)(2,1)}, bf16[2,128,1024]{2,1,0:T(8,128)(2,1)S(1)}, u32[]{:S(2)}) copy-start(bf16[2,128,1024]{2,1,0:T(8,128)(2,1)S(1)} %collective-permute-done.4.refs_5_) | copy-start | bytes 1572868
  51.6 16.8 %collective-permute-start.7 = (bf16[2,128,1024]{2,1,0:T(8,128)(2,1)S(1)}, bf16[2,128,1024]{2,1,0:T(8,128)(2,1)}, u32[]{:S(2)}, u32[]{:S(2)}) collective-permute-start(bf16[2,128,1024]{2,1,0:T(8,128)(2,1)S(1)} %collective-permute-done.5.refs_4_), channel_id=1, source_target_pairs={{4,0},{5,1},{6,2},{7,3},{8,12},{9,13},{10,14},{11,15},{20,16},{21,... | collective-permute-start | bytes 1572872 | tf_op jit(solution)/shard_map/ppermute | solution.py:325
  52.9 15.5 %collective-permute-start.13 = (bf16[2,128,1024]{2,1,0:T(8,128)(2,1)S(1)}, bf16[2,128,1024]{2,1,0:T(8,128)(2,1)S(1)}, u32[]{:S(2)}, u32[]{:S(2)}) collective-permute-start(bf16[2,128,1024]{2,1,0:T(8,128)(2,1)S(1)} %get-tuple-element.77), channel_id=1, source_target_pairs={{4,8},{5,9},{6,10},{7,11},{8,4},{9,5},{10,6},{11,7},{20,24},{21,25... | collective-permute-start | bytes 1572872 | tf_op jit(solution)/shard_map/ppermute | solution.py:325
  53.8 1.3 copy-start
  53.8 27.7 %collective-permute-start.11 = (bf16[2,128,1024]{2,1,0:T(8,128)(2,1)S(1)}, bf16[2,128,1024]{2,1,0:T(8,128)(2,1)S(1)}, u32[]{:S(2)}, u32[]{:S(2)}) collective-permute-start(bf16[2,128,1024]{2,1,0:T(8,128)(2,1)S(1)} %get-tuple-element.68), channel_id=1, source_target_pairs={{4,0},{5,1},{6,2},{7,3},{8,12},{9,13},{10,14},{11,15},{20,16},{21,... | collective-permute-start | bytes 1572872 | tf_op jit(solution)/shard_map/ppermute | solution.py:325
  59.4 1.0 copy-start.1
  68.3 3.9 %copy-start.8 = (bf16[2,128,1024]{2,1,0:T(8,128)(2,1)}, bf16[2,128,1024]{2,1,0:T(8,128)(2,1)S(1)}, u32[]{:S(2)}) copy-start(bf16[2,128,1024]{2,1,0:T(8,128)(2,1)S(1)} %collective-permute-done.13.refs_4_) | copy-start | bytes 1572868
  68.3 21.4 %collective-permute-start.14 = (bf16[2,128,1024]{2,1,0:T(8,128)(2,1)S(1)}, bf16[2,128,1024]{2,1,0:T(8,128)(2,1)S(1)}, u32[]{:S(2)}, u32[]{:S(2)}) collective-permute-start(bf16[2,128,1024]{2,1,0:T(8,128)(2,1)S(1)} %collective-permute-done.13.refs_4_), channel_id=1, source_target_pairs={{4,0},{5,1},{6,2},{7,3},{8,12},{9,13},{10,14},{11,15},{20,16},{21,... | collective-permute-start | bytes 1572872 | tf_op jit(solution)/shard_map/ppermute | solution.py:325
  72.3 1.2 collective-permute-start.8
  73.5 3.7 %collective-permute-start.9 = (f32[16,256]{1,0:T(8,128)S(1)}, f32[16,256]{1,0:T(8,128)S(1)}, u32[]{:S(2)}, u32[]{:S(2)}) collective-permute-start(f32[16,256]{1,0:T(8,128)S(1)} %add.73), channel_id=1, source_target_pairs={{0,2},{1,3},{2,0},{3,1},{4,6},{5,7},{6,4},{7,5},{8,10},{9,11},{10,... | collective-permute-start | bytes 49160 | tf_op jit(solution)/shard_map/ppermute | solution.py:318
  80.1 17.4 %collective-permute-start.12 = (bf16[4,128,512]{2,1,0:T(8,128)(2,1)S(1)}, bf16[4,128,512]{2,1,0:T(8,128)(2,1)S(1)}, u32[]{:S(2)}, u32[]{:S(2)}) collective-permute-start(bf16[4,128,512]{2,1,0:T(8,128)(2,1)S(1)} %bitcast.27), channel_id=1, source_target_pairs={{0,2},{1,3},{2,0},{3,1},{4,6},{5,7},{6,4},{7,5},{8,10},{9,11},{10,... | collective-permute-start | bytes 1572872 | tf_op jit(solution)/shard_map/ppermute | solution.py:318
  81.5 4.6 %copy-start.6 = (bf16[2,128,1024]{2,1,0:T(8,128)(2,1)}, bf16[2,128,1024]{2,1,0:T(8,128)(2,1)S(1)}, u32[]{:S(2)}) copy-start(bf16[2,128,1024]{2,1,0:T(8,128)(2,1)S(1)} %collective-permute-done.11.refs_5_) | copy-start | bytes 1572868
  89.8 3.2 %copy-start.9 = (bf16[2,128,1024]{2,1,0:T(8,128)(2,1)}, bf16[2,128,1024]{2,1,0:T(8,128)(2,1)S(1)}, u32[]{:S(2)}) copy-start(bf16[2,128,1024]{2,1,0:T(8,128)(2,1)S(1)} %collective-permute-done.14.refs_5_) | copy-start | bytes 1572868
  89.8 18.9 %collective-permute-start.17 = (bf16[2,2,128,512]{3,2,1,0:T(8,128)(2,1)S(1)}, bf16[2,2,128,512]{3,2,1,0:T(8,128)(2,1)S(1)}, u32[]{:S(2)}, u32[]{:S(2)}) collective-permute-start(bf16[2,2,128,512]{3,2,1,0:T(8,128)(2,1)S(1)} %get-tuple-element.82), channel_id=1, source_target_pairs={{0,4},{1,5},{2,6},{3,7},{4,0},{5,1},{6,2},{7,3},{8,12},{9,13},{10,... | collective-permute-start | bytes 1572872 | tf_op jit(solution)/shard_map/ppermute | solution.py:321
  95.5 1.2 collective-permute-start.15
  96.8 3.7 %collective-permute-start.18 = (f32[16,256]{1,0:T(8,128)S(1)}, f32[16,256]{1,0:T(8,128)S(1)}, u32[]{:S(2)}, u32[]{:S(2)}) collective-permute-start(f32[16,256]{1,0:T(8,128)S(1)} %add.77), channel_id=1, source_target_pairs={{0,2},{1,3},{2,0},{3,1},{4,6},{5,7},{6,4},{7,5},{8,10},{9,11},{10,... | collective-permute-start | bytes 49160 | tf_op jit(solution)/shard_map/ppermute | solution.py:318
  100.5 9.9 %collective-permute-start.16 = (bf16[2,128,512]{2,1,0:T(8,128)(2,1)S(1)}, bf16[2,128,512]{2,1,0:T(8,128)(2,1)S(1)}, u32[]{:S(2)}, u32[]{:S(2)}) collective-permute-start(bf16[2,128,512]{2,1,0:T(8,128)(2,1)S(1)} %slice.171), channel_id=1, source_target_pairs={{0,4},{1,5},{2,6},{3,7},{4,0},{5,1},{6,2},{7,3},{8,12},{9,13},{10,... | collective-permute-start | bytes 786440 | tf_op jit(solution)/shard_map/ppermute | solution.py:321
  106.6 21.0 %collective-permute-start.20 = (bf16[2,2,128,512]{3,2,1,0:T(8,128)(2,1)S(1)}, bf16[2,2,128,512]{3,2,1,0:T(8,128)(2,1)S(1)}, u32[]{:S(2)}, u32[]{:S(2)}) collective-permute-start(bf16[2,2,128,512]{3,2,1,0:T(8,128)(2,1)S(1)} %get-tuple-element.87), channel_id=1, source_target_pairs={{0,4},{1,5},{2,6},{3,7},{4,0},{5,1},{6,2},{7,3},{8,12},{9,13},{10,... | collective-permute-start | bytes 1572872 | tf_op jit(solution)/shard_map/ppermute | solution.py:321
  108.0 14.9 %collective-permute-start.22 = (bf16[4,128,512]{2,1,0:T(8,128)(2,1)S(1)}, bf16[4,128,512]{2,1,0:T(8,128)(2,1)S(1)}, u32[]{:S(2)}, u32[]{:S(2)}) collective-permute-start(bf16[4,128,512]{2,1,0:T(8,128)(2,1)S(1)} %bitcast.32), channel_id=1, source_target_pairs={{0,2},{1,3},{2,0},{3,1},{4,6},{5,7},{6,4},{7,5},{8,10},{9,11},{10,... | collective-permute-start | bytes 1572872 | tf_op jit(solution)/shard_map/ppermute | solution.py:318
  108.9 17.3 %collective-permute-start.21 = (bf16[2,128,512]{2,1,0:T(8,128)(2,1)S(1)}, bf16[2,128,512]{2,1,0:T(8,128)(2,1)S(1)}, u32[]{:S(2)}, u32[]{:S(2)}) collective-permute-start(bf16[2,128,512]{2,1,0:T(8,128)(2,1)S(1)} %fusion.2), channel_id=1, source_target_pairs={{0,2},{1,3},{2,0},{3,1},{4,6},{5,7},{6,4},{7,5},{8,10},{9,11},{10,... | collective-permute-start | bytes 786440 | tf_op jit(solution)/shard_map/ppermute | solution.py:318
  110.5 17.9 %collective-permute-start.19 = (bf16[1,128,512]{2,1,0:T(8,128)(2,1)S(1)}, bf16[1,128,512]{2,1,0:T(8,128)(2,1)S(1)}, u32[]{:S(2)}, u32[]{:S(2)}) collective-permute-start(bf16[1,128,512]{2,1,0:T(8,128)(2,1)S(1)} %slice.175), channel_id=1, source_target_pairs={{0,8},{1,9},{2,10},{3,11},{4,12},{5,13},{6,14},{7,15},{8,0},{9,1},... | collective-permute-start | bytes 393224 | tf_op jit(solution)/shard_map/ppermute | solution.py:321
  123.1 9.1 %collective-permute-start.25 = (bf16[2,128,512]{2,1,0:T(8,128)(2,1)S(1)}, bf16[2,128,512]{2,1,0:T(8,128)(2,1)S(1)}, u32[]{:S(2)}, u32[]{:S(2)}) collective-permute-start(bf16[2,128,512]{2,1,0:T(8,128)(2,1)S(1)} %slice.170), channel_id=1, source_target_pairs={{0,4},{1,5},{2,6},{3,7},{4,0},{5,1},{6,2},{7,3},{8,12},{9,13},{10,... | collective-permute-start | bytes 786440 | tf_op jit(solution)/shard_map/ppermute | solution.py:321
  126.3 13.2 %collective-permute-start.23 = (bf16[1,128,512]{2,1,0:T(8,128)(2,1)S(1)}, bf16[1,128,512]{2,1,0:T(8,128)(2,1)S(1)}, u32[]{:S(2)}, u32[]{:S(2)}) collective-permute-start(bf16[1,128,512]{2,1,0:T(8,128)(2,1)S(1)} %slice.174), channel_id=1, source_target_pairs={{0,8},{1,9},{2,10},{3,11},{4,12},{5,13},{6,14},{7,15},{8,0},{9,1},... | collective-permute-start | bytes 393224 | tf_op jit(solution)/shard_map/ppermute | solution.py:321
  127.8 6.4 %collective-permute-start.24 = (bf16[2,128,512]{2,1,0:T(8,128)(2,1)S(1)}, bf16[2,128,512]{2,1,0:T(8,128)(2,1)S(1)}, u32[]{:S(2)}, u32[]{:S(2)}) collective-permute-start(bf16[2,128,512]{2,1,0:T(8,128)(2,1)S(1)} %fusion.3), channel_id=1, source_target_pairs={{0,2},{1,3},{2,0},{3,1},{4,6},{5,7},{6,4},{7,5},{8,10},{9,11},{10,... | collective-permute-start | bytes 786440 | tf_op jit(solution)/shard_map/ppermute | solution.py:318
  132.3 11.0 %collective-permute-start.26 = (bf16[1,128,512]{2,1,0:T(8,128)(2,1)S(1)}, bf16[1,128,512]{2,1,0:T(8,128)(2,1)S(1)}, u32[]{:S(2)}, u32[]{:S(2)}) collective-permute-start(bf16[1,128,512]{2,1,0:T(8,128)(2,1)S(1)} %slice.173), channel_id=1, source_target_pairs={{0,8},{1,9},{2,10},{3,11},{4,12},{5,13},{6,14},{7,15},{8,0},{9,1},... | collective-permute-start | bytes 393224 | tf_op jit(solution)/shard_map/ppermute | solution.py:321
  134.4 10.3 %collective-permute-start.27 = (bf16[1,128,512]{2,1,0:T(8,128)(2,1)S(1)}, bf16[1,128,512]{2,1,0:T(8,128)(2,1)S(1)}, u32[]{:S(2)}, u32[]{:S(2)}) collective-permute-start(bf16[1,128,512]{2,1,0:T(8,128)(2,1)S(1)} %slice.172), channel_id=1, source_target_pairs={{0,8},{1,9},{2,10},{3,11},{4,12},{5,13},{6,14},{7,15},{8,0},{9,1},... | collective-permute-start | bytes 393224 | tf_op jit(solution)/shard_map/ppermute | solution.py:321

commit v4 on v3

--- a/solution.py
+++ b/solution.py
@@ -8,7 +8,6 @@
 PLANE = 4
 F32 = jnp.float32
 BF16 = jnp.bfloat16
-VMEM_BYTES = 48 * 1024 * 1024
 LOW_CHUNKS = ((0, 2), (2, 4))
 KEEP_Y, SEND_Y, KEEP_Z, SEND_Z = range(4)
 
@@ -35,8 +34,8 @@
     return [pltpu.with_memory_space_constraint(value, pltpu.HBM) for value in values]
 
 
-def params():
-    return pltpu.CompilerParams(vmem_limit_bytes=VMEM_BYTES)
+def params(mebibytes):
+    return pltpu.CompilerParams(vmem_limit_bytes=mebibytes * 1024 * 1024)
 
 
 def pack_factors(place, order, table, width, other):
@@ -60,7 +59,7 @@
         ),
         out_shape=jax.ShapeDtypeStruct((planes, rows, width), BF16),
         cost_estimate=cost(0, 4 * planes * rows * width),
-        compiler_params=params(),
+        compiler_params=params(10),
         name="pack_factors",
     )(place, order, *hbm(*([table] * planes)))
 
@@ -91,7 +90,7 @@
         ),
         out_shape=jax.ShapeDtypeStruct((2, planes, rows, units), BF16),
         cost_estimate=cost(0, 8 * planes * rows * units),
-        compiler_params=params(),
+        compiler_params=params(10),
         name="pack_core",
     )(place, order, *hbm(first, second, second))
 
@@ -125,111 +124,89 @@
         cost_estimate=cost(
             2 * steps * rows * units * down.shape[1], (2 * units + 3 * steps * rows) * down.shape[1]
         ),
-        compiler_params=params(),
+        compiler_params=params(24),
         name="base_blocks",
     )(place, *hbm(hidden, down, down, down, down))
 
 
-def low_part(place, order, slots, owners, tables, sources, first_plane, chunk, per_shard, rank):
-    planes = len(sources)
+def low_part(place, slots, owners, tables, sources, first_plane, chunk, per_shard, rank, share):
     first_step, last_step = chunk
     steps = last_step - first_step
     rows, (_, requests, width) = tables[-1].shape[-2], sources[0][0].shape
     lanes, count = steps * requests, len(owners)
     hidden = [array for source in sources for array in source]
 
-    def body(place_ref, order_ref, slots_ref, *refs):
+    def body(place_ref, slots_ref, *refs):
         factor_refs, hidden_refs = refs[:count], refs[count : count + len(hidden)]
-        out_ref, held, factors, total = refs[count + len(hidden) :]
-        j = pl.program_id(0)
-        at = 0
-        for i, source in enumerate(sources):
+        out_ref, held, factors = refs[count + len(hidden) :]
+        total, at = None, 0
+        for j, source in enumerate(sources):
             for inner in range(len(source)):
-                chosen = j == i
-                if len(source) > 1:
-                    chosen &= place_ref[2] == 1 - inner
-
-                @pl.when(chosen)
-                def _(ref=hidden_refs[at]):
-                    held[...] = ref[...].reshape(lanes, width)
+                ref = hidden_refs[at]
+                start = first_step if ref.shape[0] > steps else 0
+                if len(source) == 1:
+                    held[...] = ref[start : start + steps].reshape(lanes, width)
+                else:
+
+                    @pl.when(place_ref[2] == 1 - inner)
+                    def _(ref=ref, start=start):
+                        held[...] = ref[start : start + steps].reshape(lanes, width)
 
                 at += 1
-
-        @pl.when(j == 0)
-        def _():
-            total[...] = jnp.zeros_like(total)
-
-        for i, ref in enumerate(factor_refs):
-            factors[i * rows : (i + 1) * rows, :] = ref[...].reshape(rows, width)
-        total[...] += lax.dot_general(
-            factors[...], held[...], (((1,), (1,)), ((), ())), preferred_element_type=F32
-        )
-
-        @pl.when(j == planes - 1)
-        def _():
-            low = jnp.zeros((rank, lanes), F32)
-            wanted = slots_ref[...]
-            for i, owner in enumerate(owners):
-                first = (place_ref[0] * PLANE + (place_ref[1] ^ owner)) * per_shard
-                for a in range(per_shard):
-                    at = (i * per_shard + a) * rank
-                    low += jnp.where(wanted == first + a, total[at : at + rank, :], 0.0)
-            out_ref[...] = low
-
-    def factor_spec(owner):
-        if owner == 0:
-            return pl.BlockSpec(
-                (rows, width), lambda j, p, o: (0, o[first_plane + j] * PLANE + p[1])
+            for i, ref in enumerate(factor_refs):
+                factors[i * rows : (i + 1) * rows, :] = (
+                    ref[0, first_plane + j] if ref.shape[0] == 2 else ref[first_plane + j]
+                )
+            product = lax.dot_general(
+                factors[...], held[...], (((1,), (1,)), ((), ())), preferred_element_type=F32
             )
-        if owner == 1:
-            return pl.BlockSpec((1, 1, rows, width), lambda j, p, o: (0, first_plane + j, 0, 0))
-        return pl.BlockSpec((1, rows, width), lambda j, p, o: (first_plane + j, 0, 0))
-
-    def hidden_spec(array):
-        block = first_step // steps if array.shape[0] > steps else 0
-        return pl.BlockSpec((steps, requests, width), lambda j, p, o: (block, 0, 0))
-
+            total = product if total is None else total + product
+        low = jnp.zeros((rank, lanes), F32)
+        wanted = slots_ref[...]
+        for i, owner in enumerate(owners):
+            first = (place_ref[0] * PLANE + (place_ref[1] ^ owner)) * per_shard
+            for a in range(per_shard):
+                at = (i * per_shard + a) * rank
+                low += jnp.where(wanted == first + a, total[at : at + rank, :], 0.0)
+        out_ref[...] = low
+
+    whole = pl.BlockSpec(memory_space=pltpu.VMEM)
+    held_in = [pltpu.with_memory_space_constraint(x, pltpu.VMEM) for x in (*tables, *hidden)]
     return pl.pallas_call(
         body,
         grid_spec=pltpu.PrefetchScalarGridSpec(
-            num_scalar_prefetch=2,
-            grid=(planes,),
-            in_specs=[
-                pl.BlockSpec((1, lanes), lambda j, p, o: (0, 0)),
-                *[factor_spec(owner) for owner in owners],
-                *[hidden_spec(array) for array in hidden],
-            ],
-            out_specs=pl.BlockSpec((rank, lanes), lambda j, p, o: (0, 0)),
+            num_scalar_prefetch=1,
+            grid=(1,),
+            in_specs=[whole] * (1 + len(held_in)),
+            out_specs=whole,
             scratch_shapes=[
                 pltpu.VMEM((lanes, width), BF16),
                 pltpu.VMEM((count * rows, width), BF16),
-                pltpu.VMEM((count * rows, lanes), F32),
             ],
         ),
         out_shape=jax.ShapeDtypeStruct((rank, lanes), F32),
         cost_estimate=cost(
-            2 * lanes * count * rows * planes * width, 2 * (lanes + count * rows) * planes * width, 1
-        ),
-        compiler_params=params(),
+            2 * lanes * count * rows * len(sources) * width,
+            2 * (lanes + count * rows) * len(sources) * width,
+            share,
+        ),
+        compiler_params=params(10),
         name="low_part",
-    )(place, order, slots, *hbm(*tables, *hidden))
+    )(place, slots, *held_in)
 
 
 def add_extra(place, low, slots, mine, other, keep, recv, first_step, pieces, per_shard, rank):
     _, planes, _, requests, width = keep.shape
     rows, lanes = mine.shape[0], low.shape[1]
-    count, half = len(pieces), planes // 2
+    half = planes // 2
     parts = {
         KEEP_Y: ((0,), range(planes)),
         SEND_Y: ((1,), range(planes)),
         KEEP_Z: ((0, 1), range(half)),
         SEND_Z: ((0, 1), range(half, planes)),
     }
-    sides = sorted({side for _, what in pieces for side in parts[what][0]})
-
-    def body(place_ref, low_ref, slots_ref, *refs):
-        tables, refs = refs[: len(sides) * planes], refs[len(sides) * planes :]
-        others, refs = refs[: len(sides)], refs[len(sides) :]
+
+    def body(place_ref, low_ref, slots_ref, m_ref, t_ref, k_ref, r_ref, *out_refs):
         rounded = low_ref[...].astype(BF16).astype(F32)
         wanted = slots_ref[...]
         spread = []
@@ -237,68 +214,45 @@
             first = (place_ref[0] * PLANE + (place_ref[1] ^ i)) * per_shard
             masked = [jnp.where(wanted == first + a, rounded, 0.0) for a in range(per_shard)]
             spread.append(jnp.concatenate(masked, axis=0).T.astype(BF16))
-        for n, (step, what) in enumerate(pieces):
-            k_ref, r_ref, out_ref = refs[n], refs[count + n], refs[2 * count + n]
-            start = (step - first_step) * requests
-            here = [value[start : start + requests] for value in spread]
+        for (step, what, part, share), out_ref in zip(pieces, out_refs):
+            size = requests // share
+            start = (step - first_step) * requests + part * size
+            here = [value[start : start + size] for value in spread]
+            rows_at = slice(part * size, (part + 1) * size)
             for side_at, side in enumerate(parts[what][0]):
-                at = sides.index(side)
                 for block_at, i in enumerate(parts[what][1]):
-                    extra = jnp.dot(
-                        here[0], tables[at * planes + i][...], preferred_element_type=F32
-                    )
-                    extra += jnp.dot(here[1], others[at][0, i], preferred_element_type=F32)
-                    base = k_ref[side_at, block_at, 0] + r_ref[side_at, block_at, 0].astype(F32)
+                    block = (place_ref[0] ^ halving(i, planes)) * PLANE + (place_ref[1] ^ (2 * side))
+                    columns = pl.ds(pl.multiple_of(block * width, width), width)
+                    own, other_own = m_ref[:, columns], t_ref[1, i, :, side * width : (side + 1) * width]
+                    extra = jnp.dot(here[0], own, preferred_element_type=F32)
+                    extra += jnp.dot(here[1], other_own, preferred_element_type=F32)
+                    base = k_ref[side, i, step, rows_at] + r_ref[side, i, step, rows_at].astype(F32)
                     out_ref[side_at, block_at] = (base + extra).astype(out_ref.dtype)
 
-    def columns(i, side):
-        return lambda j, p: (0, (p[0] ^ halving(i, planes)) * PLANE + (p[1] ^ (2 * side)))
-
-    def shape(what):
-        return (len(parts[what][0]), len(parts[what][1]), requests, width)
-
-    def base(step, what):
-        side = 1 if what == SEND_Y else 0
-        block = 1 if what == SEND_Z else 0
-        n, m, _, _ = shape(what)
-        return pl.BlockSpec((n, m, 1, requests, width), lambda i, p: (side, block, step, 0, 0))
-
-    def other_spec(side):
-        return pl.BlockSpec((1, planes, rows, width), lambda i, p: (1, 0, 0, side))
-
-    bases = [base(*piece) for piece in pieces]
+    def shape(step, what, part, share):
+        return (len(parts[what][0]), len(parts[what][1]), requests // share, width)
+
+    whole = pl.BlockSpec(memory_space=pltpu.VMEM)
     return pl.pallas_call(
         body,
         grid_spec=pltpu.PrefetchScalarGridSpec(
             num_scalar_prefetch=1,
             grid=(1,),
-            in_specs=[
-                pl.BlockSpec((rank, lanes), lambda i, p: (0, 0)),
-                pl.BlockSpec((1, lanes), lambda i, p: (0, 0)),
-                *[
-                    pl.BlockSpec((rows, width), columns(i, side))
-                    for side in sides
-                    for i in range(planes)
-                ],
-                *[other_spec(side) for side in sides],
-                *bases,
-                *bases,
-            ],
-            out_specs=[pl.BlockSpec(shape(what), lambda i, p: (0, 0, 0, 0)) for _, what in pieces],
+            in_specs=[whole] * 6,
+            out_specs=[whole] * len(pieces),
         ),
         out_shape=[
-            jax.ShapeDtypeStruct(shape(what), BF16 if what in (SEND_Y, SEND_Z) else F32)
-            for _, what in pieces
+            jax.ShapeDtypeStruct(shape(*piece), BF16 if piece[1] in (SEND_Y, SEND_Z) else F32)
+            for piece in pieces
         ],
         cost_estimate=cost(4 * lanes * rows * planes * width, 10 * lanes * planes * width),
-        compiler_params=params(),
+        compiler_params=params(10),
         name="add_extra",
     )(
         place,
         low,
         slots,
-        *hbm(*([mine] * (planes * len(sides))), *([other] * len(sides))),
-        *hbm(*([keep] * count), *([recv] * count)),
+        *[pltpu.with_memory_space_constraint(x, pltpu.VMEM) for x in (mine, other, keep, recv)],
     )
 
 
@@ -348,7 +302,8 @@
         blocks = [hidden] + [along(hidden_z, o) for o in range(1, planes)]
         near = middle = blocks[1]
     for_far = pack_factors(place, order, after(first, for_near), units, 3)
-    for_core = pack_core(place, order, after(first, for_far), second, width)
+    for_self = pack_factors(place, order, after(first, for_far), units, 0)
+    for_core = pack_core(place, order, after(first, for_self), second, width)
     send, keep = base_blocks(place, after(hidden, for_core), down_matrix, planes, width)
     near, middle, send, near_y = lax.optimization_barrier((near, middle, send, near_y))
     from_core = in_plane(after(for_core, near), 1)
@@ -359,18 +314,19 @@
     slots = jnp.tile(slot_row[None, :], (1, steps))
 
     def low_at(chunk, owners, tables, sources, first_plane):
+        share = 1 if chunk[0] == 0 else 1000
         lanes = slots[:, chunk[0] * requests : chunk[1] * requests]
         return low_part(
-            place, order, lanes, owners, tables, sources, first_plane, chunk, per_shard, rank
+            place, lanes, owners, tables, sources, first_plane, chunk, per_shard, rank, share
         )
 
     def early_of(*ready):
-        near_by = (first, after(from_core, *ready), near_y)
+        near_by = (for_self, after(from_core, *ready), near_y)
         part = low_at((0, steps), (0, 1, 2), near_by, at_hand, 0)
         return part, low_at((0, steps), (3,), (after(far_y, part),), at_hand, 0)
 
     def late_of(chunk, plane, source, *ready):
-        tables = (first, after(from_core, *ready), near_y, far_y)
+        tables = (for_self, after(from_core, *ready), near_y, far_y)
         return low_at(chunk, range(PLANE), tables, [source], plane)
 
     if planes == 4:
@@ -381,11 +337,12 @@
         outer_two = hop(after(middle_two, outer_one), outward)
         early, early_far = early_of(outer_one, middle_two)
         part = late_of((a, b), 2, [middle, outer_one], early_far)
-        late = [[part, [middle_two, outer_two]]]
+        middle_two_first = middle_two
         middle_two = hop(after(near[c:d], middle_two), across)
         outer_one = hop(after(middle[c:d], outer_one), outward)
-        outer_two = hop(after(middle_two, outer_two, part), outward)
-        late.append([[middle, outer_one], [middle_two, outer_two]])
+        last = late_of((a, b), 3, [middle_two_first, outer_two], part)
+        outer_two = hop(after(middle_two, last), outward)
+        late = [[part, last], [[middle, outer_one], [middle_two, outer_two]]]
         second_wave = [outer_one]
     else:
         early, early_far = early_of()
@@ -406,8 +363,8 @@
 
     along_z = [1 << bit for bit in range(planes.bit_length() - 1)]
     y_first, z_first = ["y", *along_z], [*along_z[:1], "y", *along_z[1:]]
-    plans = [list(plan) for plan in (y_first, z_first, y_first, z_first)]
-    state = [None] * steps
+    plans = [list(plan) for plan in (y_first, z_first, y_first, z_first, y_first)]
+    state = [None] * len(plans)
 
     def send(value, stage):
         return in_plane(value, 2) if stage == "y" else along(value, stage)
@@ -438,10 +395,10 @@
         ready = part
     low = core_sum(LOW_CHUNKS[0], parts)
     low = low + in_plane(low, 2)
-    (goes,) = with_extra(low[:, :requests], 0, [(0, SEND_Y)])
+    (goes,) = with_extra(low[:, :requests], 0, [(0, SEND_Y, 0, 1)])
     low = after(low, goes, *second_wave)
     moved = send(goes[0], "y")
-    stays, goes, next_stays = with_extra(low, 0, [(0, KEEP_Y), (1, SEND_Z), (1, KEEP_Z)])
+    stays, goes, next_stays = with_extra(low, 0, [(0, KEEP_Y, 0, 1), (1, SEND_Z, 0, 1), (1, KEEP_Z, 0, 1)])
     state[0] = (stays[0], moved)
     parts, ready = [], (stays, goes, next_stays)
     for i, source in enumerate(late[1]):
@@ -454,20 +411,27 @@
     across_y = in_plane(low, 2)
     done = add(0, low)
     low = low + after(across_y, done)
-    moved, stays, goes, next_stays = with_extra(
-        low, 2, [(2, SEND_Y), (2, KEEP_Y), (3, SEND_Z), (3, KEEP_Z)]
+    (moved,) = with_extra(low[:, :requests], 2, [(2, SEND_Y, 0, 1)])
+    done = add(1, moved)
+    low = after(low, done)
+    sent_y = send(moved[0], "y")
+    stays, goes, next_stays, last_goes, last_stays = with_extra(
+        low,
+        2,
+        [(2, KEEP_Y, 0, 1), (3, SEND_Z, 0, 2), (3, KEEP_Z, 0, 2), (3, SEND_Y, 1, 2), (3, KEEP_Y, 1, 2)],
     )
-    begin(2, stays, moved)
+    state[2] = (stays[0], sent_y)
     begin(3, next_stays, goes)
+    begin(4, last_stays, last_goes)
     done = next_stays
-    for c in (1, 0, 2, 1, 3, 0, 2, 3, 1, 2, 3):
+    for c in (0, 2, 3, 1, 4, 0, 2, 3, 4, 1, 2, 3, 4):
         if plans[c]:
             done = add(c, done)
-    for c in range(steps):
+    for c in range(len(plans)):
         while plans[c]:
             done = add(c, done)
-    outputs = [value.astype(BF16) for value, _ in state]
-    return jnp.concatenate(outputs, axis=0)
+    outputs = [value[0].astype(BF16) for value, _ in state]
+    return jnp.concatenate(outputs, axis=0).reshape(steps, requests, width)
 
 
 def solution(mesh):

time: 146 us -> 139 us (0.952)
  Pallas kernels: 52.4 us -> 34.9 us
  waiting for transfers between devices: 54.4 us -> 68.1 us
  starting transfers between devices: 34.4 us -> 32.1 us
    pallas_call x6, Pallas kernels: 17.7 us -> 7.33 us  [low_part(): pl.pallas_call(body, grid_spec=pltpu.PrefetchScalarGridSpec(num_scalar_pr...]
    ppermute x7, waiting for transfers between devices: 19.1 us -> 29.3 us  [hop(): return lax.ppermute(value, 'tensor', pairs)]
    pallas_call x3 -> x4, Pallas kernels: 12.8 us -> 5.18 us  [add_extra(): pl.pallas_call(body, grid_spec=pltpu.PrefetchScalarGridSpec(num_scalar_pr...]
    ppermute x9 -> x11, waiting for transfers between devices: 14.8 us -> 21.2 us  [along(): lax.ppermute(value, 'tensor', [(t, t ^ other * PLANE) for t in range(devi...]
    ppermute x9 -> x11, starting transfers between devices: 17.3 us -> 11.1 us  [along(): lax.ppermute(value, 'tensor', [(t, t ^ other * PLANE) for t in range(devi...]
    ppermute x12 -> x13, starting transfers between devices: 9.92 us -> 13.8 us  [in_plane(): lax.ppermute(value, 'tensor', [(t, t ^ other) for t in range(devices)])]
    ppermute x12 -> x13, waiting for transfers between devices: 20.6 us -> 17.6 us  [in_plane(): lax.ppermute(value, 'tensor', [(t, t ^ other) for t in range(devices)])]
    pallas_call x2 -> x3, Pallas kernels: 3.61 us -> 5.42 us  [pack_factors(): pl.pallas_call(body, grid_spec=pltpu.PrefetchScalarGridSpec(num_scalar_pr...]
  transfers between devices with their start and end apart: 28 -> 31, of which waited for: 17 -> 20; matrix products, arithmetic and copies ran while one was open for 1% -> 1% of each run, Pallas kernels for 35% -> 24%
where the time goes in v4:
time: 139 us; the launch traced here: 138 us
  waiting for transfers between devices  68.1 us (49%)
  Pallas kernels  34.9 us (25%)
  starting transfers between devices  32.1 us (23%)
  other arithmetic  1.43 us (1%)
    ppermute x7, waiting for transfers between devices, hop(): return lax.ppermute(value, 'tensor', pairs)  29.3 us
    ppermute x11, waiting for transfers between devices, along(): lax.ppermute(value, 'tensor', [(t, t ^ other * PLANE) for t in range(devi...  21.2 us
    ppermute x13, waiting for transfers between devices, in_plane(): lax.ppermute(value, 'tensor', [(t, t ^ other) for t in range(devices)])  17.6 us
    pallas_call x1, Pallas kernels, base_blocks(): pl.pallas_call(body, grid_spec=pltpu.PrefetchScalarGridSpec(num_scalar_pr...  13.9 us
    ppermute x13, starting transfers between devices, in_plane(): lax.ppermute(value, 'tensor', [(t, t ^ other) for t in range(devices)])  13.8 us
    ppermute x11, starting transfers between devices, along(): lax.ppermute(value, 'tensor', [(t, t ^ other * PLANE) for t in range(devi...  11.1 us
    pallas_call x6, Pallas kernels, low_part(): pl.pallas_call(body, grid_spec=pltpu.PrefetchScalarGridSpec(num_scalar_pr...  7.33 us
    ppermute x7, starting transfers between devices, hop(): return lax.ppermute(value, 'tensor', pairs)  7.26 us
  transfers between devices with their start and end apart: 31, of which 20 were waited for; matrix products, arithmetic and copies ran while one was open for 1% of the time, Pallas kernels for 24%

profile of v4, /device:TPU:0, one launch (start us, length us, event | category | flops | bytes accessed | tf_op | source)
XLA Modules:
  0.0 138.3 jit_solution(10792041174047084086)
XLA Ops:
  0.2 1.8 %pack_factors.3 = bf16[4,128,1024]{2,1,0:T(8,128)(2,1)S(1)} custom-call(s32[3]{0:T(128)S(1)} %pad_add_fusion.place_ref, s32[4]{0:T(128)S(1)} %pad_add_fusion.1.order_ref, bf16[128,16384]{1,0:T(8,128)(2,1)} %bitcast.56, bf16[128,16384]{1,0:T(8,128)(2,1)} %bitcast.57, bf16[128,16384]{1,0:T(8,128)(2,1)} %bitcast.58, bf16[128,16384]{1,0:T(8,128)(2,1)} %bitcast.59), custom_call_target="tpu_custom_call" | custom-call | bytes 2097 | tf_op jit(solution)/shard_map/pack_factors/pallas_call | solution.py:52
  2.0 3.0 %collective-permute-start.2 = (bf16[4,128,1024]{2,1,0:T(8,128)(2,1)S(1)}, bf16[4,128,1024]{2,1,0:T(8,128)(2,1)S(1)}, u32[]{:S(2)}, u32[]{:S(2)}) collective-permute-start(bf16[4,128,1024]{2,1,0:T(8,128)(2,1)S(1)} %pack_factors.3), channel_id=1, source_target_pairs={{0,2},{1,3},{2,0},{3,1},{4,6},{5,7},{6,4},{7,5},{8,10},{9,11},{10,... | collective-permute-start | bytes 3145736 | tf_op jit(solution)/shard_map/ppermute | solution.py:272
  5.7 4.4 %collective-permute-start = (bf16[4,128,1024]{2,1,0:T(8,128)(2,1)S(1)}, bf16[4,128,1024]{2,1,0:T(8,128)(2,1)S(1)}, u32[]{:S(2)}, u32[]{:S(2)}) collective-permute-start(bf16[4,128,1024]{2,1,0:T(8,128)(2,1)S(1)} %copy-done.1), channel_id=1, source_target_pairs={{0,4},{1,5},{2,6},{3,7},{4,0},{5,1},{6,2},{7,3},{8,12},{9,13},{10,... | collective-permute-start | bytes 3145736 | tf_op jit(solution)/shard_map/ppermute | solution.py:275
  10.1 1.8 %pack_factors.4 = bf16[4,128,1024]{2,1,0:T(8,128)(2,1)S(1)} custom-call(s32[3]{0:T(128)S(1)} %pad_add_fusion.place_ref, s32[4]{0:T(128)S(1)} %pad_add_fusion.1.order_ref, bf16[128,16384]{1,0:T(8,128)(2,1)} %bitcast.60, bf16[128,16384]{1,0:T(8,128)(2,1)} %bitcast.61, bf16[128,16384]{1,0:T(8,128)(2,1)} %bitcast.62, bf16[128,16384]{1,0:T(8,128)(2,1)} %bitcast.63), custom_call_target="tpu_custom_call" | custom-call | bytes 2097 | tf_op jit(solution)/shard_map/pack_factors/pallas_call | solution.py:52
  11.9 1.8 %pack_factors.5.refs_0_ = bf16[4,128,1024]{2,1,0:T(8,128)(2,1)S(1)} custom-call(s32[3]{0:T(128)S(1)} %pad_add_fusion.place_ref, s32[4]{0:T(128)S(1)} %pad_add_fusion.1.order_ref, bf16[128,16384]{1,0:T(8,128)(2,1)} %bitcast.64, bf16[128,16384]{1,0:T(8,128)(2,1)} %bitcast.65, bf16[128,16384]{1,0:T(8,128)(2,1)} %bitcast.66, bf16[128,16384]{1,0:T(8,128)(2,1)} %bitcast.67), custom_call_target="tpu_custom_call" | custom-call | bytes 2097 | tf_op jit(solution)/shard_map/pack_factors/pallas_call | solution.py:52
  13.7 3.1 %pack_core.1 = bf16[2,4,128,1024]{3,2,1,0:T(8,128)(2,1)S(1)} custom-call(s32[3]{0:T(128)S(1)} %pad_add_fusion.place_ref, s32[4]{0:T(128)S(1)} %pad_add_fusion.1.order_ref, bf16[128,16384]{1,0:T(8,128)(2,1)} %bitcast.68, bf16[128,8192]{1,0:T(8,128)(2,1)} %bitcast.43, bf16[128,8192]{1,0:T(8,128)(2,1)} %bitcast.44), custom_call_target="tpu_custom_call" | custom-call | bytes 4194 | tf_op jit(solution)/shard_map/pack_core/pallas_call | solution.py:82
  16.9 13.9 %base_blocks.1 = (bf16[2,4,4,128,512]{4,3,2,1,0:T(8,128)(2,1)S(1)}, f32[2,4,4,128,512]{4,3,2,1,0:T(8,128)S(1)}) custom-call(s32[3]{0:T(128)S(1)} %pad_add_fusion.place_ref, bf16[4,128,1024]{2,1,0:T(8,128)(2,1)} %refs_1_.1, bf16[1024,8192]{1,0:T(8,128)(2,1)} %d3.1, bf16[1024,8192]{1,0:T(8,128)(2,1)} %d3.1, bf16[1024,8192]{1,0:T(8,128)(2,1)} %d3.1, ...), custom_call_target="tpu_custom_call" | custom-call | flops 8589934 | bytes 29360 | tf_op jit(solution)/shard_map/base_blocks/pallas_call | solution.py:114
  30.8 1.9 %collective-permute-done.refs_4_.refs_2_ = bf16[4,128,1024]{2,1,0:T(8,128)(2,1)S(1)} collective-permute-done((bf16[4,128,1024]{2,1,0:T(8,128)(2,1)S(1)}, bf16[4,128,1024]{2,1,0:T(8,128)(2,1)S(1)}, u32[]{:S(2)}, u32[]{:S(2)}) %collective-permute-start) | collective-permute-done | bytes 1048608 | tf_op jit(solution)/shard_map/ppermute | solution.py:275
  33.5 1.3 collective-permute-start.4
  35.5 14.2 %collective-permute-done.4.refs_5_ = bf16[2,128,1024]{2,1,0:T(8,128)(2,1)S(1)} collective-permute-done((bf16[2,128,1024]{2,1,0:T(8,128)(2,1)S(1)}, bf16[2,128,1024]{2,1,0:T(8,128)(2,1)S(1)}, u32[]{:S(2)}, u32[]{:S(2)}) %collective-permute-start.4) | collective-permute-done | bytes 524320 | tf_op jit(solution)/shard_map/ppermute | solution.py:279
  49.8 1.3 collective-permute-start.7
  52.0 1.3 collective-permute-start.11
  53.3 1.5 %low_part.6 = f32[16,512]{1,0:T(8,128)S(1)} custom-call(s32[3]{0:T(128)S(1)} %pad_add_fusion.place_ref, s32[1,512]{1,0:T(1,128)S(1)} %bitcast.52, bf16[4,128,1024]{2,1,0:T(8,128)(2,1)S(1)} %pack_factors.5.refs_0_, bf16[2,4,128,1024]{3,2,1,0:T(8,128)(2,1)S(1)} %collective-permute-done.3.refs_1_.t_ref, ...), custom_call_target="tpu_custom_call" | custom-call | flops 805306368 | bytes 3670016 | tf_op jit(solution)/shard_map/low_part/pallas_call | solution.py:175
  54.8 3.7 %collective-permute-done.6.refs_0_.refs_3_ = bf16[4,128,1024]{2,1,0:T(8,128)(2,1)S(1)} collective-permute-done((bf16[4,128,1024]{2,1,0:T(8,128)(2,1)S(1)}, bf16[4,128,1024]{2,1,0:T(8,128)(2,1)S(1)}, u32[]{:S(2)}, u32[]{:S(2)}) %collective-permute-start.6) | collective-permute-done | bytes 1048608 | tf_op jit(solution)/shard_map/ppermute | solution.py:272
  58.5 1.4 low_part.7
  59.9 1.1 low_part.8
  61.0 6.5 %collective-permute-done.7.refs_5_ = bf16[2,128,1024]{2,1,0:T(8,128)(2,1)S(1)} collective-permute-done((bf16[2,128,1024]{2,1,0:T(8,128)(2,1)S(1)}, bf16[2,128,1024]{2,1,0:T(8,128)(2,1)S(1)}, u32[]{:S(2)}, u32[]{:S(2)}) %collective-permute-start.7) | collective-permute-done | bytes 524320 | tf_op jit(solution)/shard_map/ppermute | solution.py:279
  67.5 1.1 low_part.9
  68.6 1.3 collective-permute-start.14
  70.0 1.2 collective-permute-done.8
  71.2 1.5 %collective-permute-start.9 = (f32[16,256]{1,0:T(8,128)S(1)}, f32[16,256]{1,0:T(8,128)S(1)}, u32[]{:S(2)}, u32[]{:S(2)}) collective-permute-start(f32[16,256]{1,0:T(8,128)S(1)} %add.82), channel_id=1, source_target_pairs={{0,2},{1,3},{2,0},{3,1},{4,6},{5,7},{6,4},{7,5},{8,10},{9,11},{10,... | collective-permute-start | bytes 49160 | tf_op jit(solution)/shard_map/ppermute | solution.py:272
  72.7 2.2 %collective-permute-done.9 = f32[16,256]{1,0:T(8,128)S(1)} collective-permute-done((f32[16,256]{1,0:T(8,128)S(1)}, f32[16,256]{1,0:T(8,128)S(1)}, u32[]{:S(2)}, u32[]{:S(2)}) %collective-permute-start.9) | collective-permute-done | bytes 16416 | tf_op jit(solution)/shard_map/ppermute | solution.py:272
  74.9 1.0 add_extra.4
  75.9 1.6 %collective-permute-start.12 = (bf16[4,128,512]{2,1,0:T(8,128)(2,1)S(1)}, bf16[4,128,512]{2,1,0:T(8,128)(2,1)S(1)}, u32[]{:S(2)}, u32[]{:S(2)}) collective-permute-start(bf16[4,128,512]{2,1,0:T(8,128)(2,1)S(1)} %bitcast.49), channel_id=1, source_target_pairs={{0,2},{1,3},{2,0},{3,1},{4,6},{5,7},{6,4},{7,5},{8,10},{9,11},{10,... | collective-permute-start | bytes 1572872 | tf_op jit(solution)/shard_map/ppermute | solution.py:272
  77.5 1.2 collective-permute-done.11.refs_5_
  78.8 1.6 %add_extra.5 = (f32[1,4,128,512]{3,2,1,0:T(8,128)S(1)}, bf16[2,2,128,512]{3,2,1,0:T(8,128)(2,1)S(1)}, f32[2,2,128,512]{3,2,1,0:T(8,128)S(1)}) custom-call(s32[3]{0:T(128)S(1)} %pad_add_fusion.place_ref, f32[16,256]{1,0:T(8,128)S(1)} %add.83.low_ref, s32[1,256]{1,0:T(1,128)S(1)} %get-tuple-element.124.slots_ref, bf16[128,8192]{1,0:T(8,128)(2,1)S(1)} %bitcast.46, ...), custom_call_target="tpu_custom_call" | custom-call | flops 268435 | bytes 5242 | tf_op jit(solution)/shard_map/add_extra/pallas_call | solution.py:236
  80.3 1.1 low_part.10
  81.4 7.3 %collective-permute-done.14.refs_5_ = bf16[2,128,1024]{2,1,0:T(8,128)(2,1)S(1)} collective-permute-done((bf16[2,128,1024]{2,1,0:T(8,128)(2,1)S(1)}, bf16[2,128,1024]{2,1,0:T(8,128)(2,1)S(1)}, u32[]{:S(2)}, u32[]{:S(2)}) %collective-permute-start.14) | collective-permute-done | bytes 524320 | tf_op jit(solution)/shard_map/ppermute | solution.py:279
  88.7 1.2 low_part.11
  90.0 1.2 collective-permute-done.15
  91.2 1.5 %collective-permute-start.17 = (f32[16,256]{1,0:T(8,128)S(1)}, f32[16,256]{1,0:T(8,128)S(1)}, u32[]{:S(2)}, u32[]{:S(2)}) collective-permute-start(f32[16,256]{1,0:T(8,128)S(1)} %add.86), channel_id=1, source_target_pairs={{0,2},{1,3},{2,0},{3,1},{4,6},{5,7},{6,4},{7,5},{8,10},{9,11},{10,... | collective-permute-start | bytes 49160 | tf_op jit(solution)/shard_map/ppermute | solution.py:272
  92.9 2.0 %collective-permute-done.17 = f32[16,256]{1,0:T(8,128)S(1)} collective-permute-done((f32[16,256]{1,0:T(8,128)S(1)}, f32[16,256]{1,0:T(8,128)S(1)}, u32[]{:S(2)}, u32[]{:S(2)}) %collective-permute-start.17) | collective-permute-done | bytes 16416 | tf_op jit(solution)/shard_map/ppermute | solution.py:272
  94.9 2.0 %collective-permute-start.16 = (bf16[2,128,512]{2,1,0:T(8,128)(2,1)S(1)}, bf16[2,128,512]{2,1,0:T(8,128)(2,1)S(1)}, u32[]{:S(2)}, u32[]{:S(2)}) collective-permute-start(bf16[2,128,512]{2,1,0:T(8,128)(2,1)S(1)} %slice.207), channel_id=1, source_target_pairs={{0,4},{1,5},{2,6},{3,7},{4,0},{5,1},{6,2},{7,3},{8,12},{9,13},{10,... | collective-permute-start | bytes 786440 | tf_op jit(solution)/shard_map/ppermute | solution.py:275
  97.0 1.0 add_extra.6
  98.0 1.6 %collective-permute-start.23 = (bf16[4,128,512]{2,1,0:T(8,128)(2,1)S(1)}, bf16[4,128,512]{2,1,0:T(8,128)(2,1)S(1)}, u32[]{:S(2)}, u32[]{:S(2)}) collective-permute-start(bf16[4,128,512]{2,1,0:T(8,128)(2,1)S(1)} %bitcast.50), channel_id=1, source_target_pairs={{0,2},{1,3},{2,0},{3,1},{4,6},{5,7},{6,4},{7,5},{8,10},{9,11},{10,... | collective-permute-start | bytes 1572872 | tf_op jit(solution)/shard_map/ppermute | solution.py:272
  99.6 4.0 %collective-permute-done.18 = bf16[2,2,128,512]{3,2,1,0:T(8,128)(2,1)S(1)} collective-permute-done((bf16[2,2,128,512]{3,2,1,0:T(8,128)(2,1)S(1)}, bf16[2,2,128,512]{3,2,1,0:T(8,128)(2,1)S(1)}, u32[]{:S(2)}, u32[]{:S(2)}) %collective-permute-start.18) | collective-permute-done | bytes 524320 | tf_op jit(solution)/shard_map/ppermute | solution.py:275
  103.8 1.6 %collective-permute-start.21 = (bf16[2,128,512]{2,1,0:T(8,128)(2,1)S(1)}, bf16[2,128,512]{2,1,0:T(8,128)(2,1)S(1)}, u32[]{:S(2)}, u32[]{:S(2)}) collective-permute-start(bf16[2,128,512]{2,1,0:T(8,128)(2,1)S(1)} %fusion.1), channel_id=1, source_target_pairs={{0,2},{1,3},{2,0},{3,1},{4,6},{5,7},{6,4},{7,5},{8,10},{9,11},{10,... | collective-permute-start | bytes 786440 | tf_op jit(solution)/shard_map/ppermute | solution.py:272
  105.3 1.6 %add_extra.7 = (f32[1,4,128,512]{3,2,1,0:T(8,128)S(1)}, bf16[2,2,64,512]{3,2,1,0:T(8,128)(2,1)S(1)}, f32[2,2,64,512]{3,2,1,0:T(8,128)S(1)}, bf16[1,4,64,512]{3,2,1,0:T(8,128)(2,1)S(1)}, f32[1,4,64,512]{3,2,1,0:T(8,128)S(1)}) custom-call(s32[3]{0:T(128)S(1)} %pad_add_fusion.place_ref, f32[16,256]{1,0:T(8,128)S(1)} %add.88.low_ref, ...), custom_call_target="tpu_custom_call" | custom-call | flops 268435 | bytes 5242 | tf_op jit(solution)/shard_map/add_extra/pallas_call | solution.py:236
  107.5 1.1 collective-permute-done.16
  109.6 3.3 %collective-permute-done.23 = bf16[4,128,512]{2,1,0:T(8,128)(2,1)S(1)} collective-permute-done((bf16[4,128,512]{2,1,0:T(8,128)(2,1)S(1)}, bf16[4,128,512]{2,1,0:T(8,128)(2,1)S(1)}, u32[]{:S(2)}, u32[]{:S(2)}) %collective-permute-start.23) | collective-permute-done | bytes 524320 | tf_op jit(solution)/shard_map/ppermute | solution.py:272
  113.2 4.4 %collective-permute-done.22 = bf16[2,2,64,512]{3,2,1,0:T(8,128)(2,1)S(1)} collective-permute-done((bf16[2,2,64,512]{3,2,1,0:T(8,128)(2,1)S(1)}, bf16[2,2,64,512]{3,2,1,0:T(8,128)(2,1)S(1)}, u32[]{:S(2)}, u32[]{:S(2)}) %collective-permute-start.22) | collective-permute-done | bytes 262176 | tf_op jit(solution)/shard_map/ppermute | solution.py:275
  117.7 1.6 %collective-permute-start.26 = (bf16[2,64,512]{2,1,0:T(8,128)(2,1)S(1)}, bf16[2,64,512]{2,1,0:T(8,128)(2,1)S(1)}, u32[]{:S(2)}, u32[]{:S(2)}) collective-permute-start(bf16[2,64,512]{2,1,0:T(8,128)(2,1)S(1)} %fusion.3), channel_id=1, source_target_pairs={{0,2},{1,3},{2,0},{3,1},{4,6},{5,7},{6,4},{7,5},{8,10},{9,11},{10,... | collective-permute-start | bytes 393224 | tf_op jit(solution)/shard_map/ppermute | solution.py:272
  119.5 4.1 %collective-permute-done.20 = bf16[4,64,512]{2,1,0:T(8,128)(2,1)S(1)} collective-permute-done((bf16[4,64,512]{2,1,0:T(8,128)(2,1)S(1)}, bf16[4,64,512]{2,1,0:T(8,128)(2,1)S(1)}, u32[]{:S(2)}, u32[]{:S(2)}) %collective-permute-start.20) | collective-permute-done | bytes 262176 | tf_op jit(solution)/shard_map/ppermute | solution.py:272
  124.2 1.7 %collective-permute-start.28 = (bf16[1,128,512]{2,1,0:T(8,128)(2,1)S(1)}, bf16[1,128,512]{2,1,0:T(8,128)(2,1)S(1)}, u32[]{:S(2)}, u32[]{:S(2)}) collective-permute-start(bf16[1,128,512]{2,1,0:T(8,128)(2,1)S(1)} %slice.208), channel_id=1, source_target_pairs={{0,8},{1,9},{2,10},{3,11},{4,12},{5,13},{6,14},{7,15},{8,0},{9,1},... | collective-permute-start | bytes 393224 | tf_op jit(solution)/shard_map/ppermute | solution.py:275
  125.9 1.4 collective-permute-start.29
  127.3 2.6 %collective-permute-done.25 = bf16[2,64,512]{2,1,0:T(8,128)(2,1)S(1)} collective-permute-done((bf16[2,64,512]{2,1,0:T(8,128)(2,1)S(1)}, bf16[2,64,512]{2,1,0:T(8,128)(2,1)S(1)}, u32[]{:S(2)}, u32[]{:S(2)}) %collective-permute-start.25) | collective-permute-done | bytes 131104 | tf_op jit(solution)/shard_map/ppermute | solution.py:275
  130.2 2.1 %collective-permute-done.24 = bf16[1,128,512]{2,1,0:T(8,128)(2,1)S(1)} collective-permute-done((bf16[1,128,512]{2,1,0:T(8,128)(2,1)S(1)}, bf16[1,128,512]{2,1,0:T(8,128)(2,1)S(1)}, u32[]{:S(2)}, u32[]{:S(2)}) %collective-permute-start.24) | collective-permute-done | bytes 131104 | tf_op jit(solution)/shard_map/ppermute | solution.py:275
  132.3 3.5 %collective-permute-done.28 = bf16[1,128,512]{2,1,0:T(8,128)(2,1)S(1)} collective-permute-done((bf16[1,128,512]{2,1,0:T(8,128)(2,1)S(1)}, bf16[1,128,512]{2,1,0:T(8,128)(2,1)S(1)}, u32[]{:S(2)}, u32[]{:S(2)}) %collective-permute-start.28) | collective-permute-done | bytes 131104 | tf_op jit(solution)/shard_map/ppermute | solution.py:275
  (83 shorter events, 9.3 us)
Async XLA Ops:
  0.2 4.8 %copy-start.1 = (bf16[4,128,1024]{2,1,0:T(8,128)(2,1)S(1)}, bf16[4,128,1024]{2,1,0:T(8,128)(2,1)}, u32[]{:S(2)}) copy-start(bf16[4,128,1024]{2,1,0:T(8,128)(2,1)} %refs_1_.1) | copy-start | bytes 3145732
  2.0 28.8 %collective-permute-start.2 = (bf16[4,128,1024]{2,1,0:T(8,128)(2,1)S(1)}, bf16[4,128,1024]{2,1,0:T(8,128)(2,1)S(1)}, u32[]{:S(2)}, u32[]{:S(2)}) collective-permute-start(bf16[4,128,1024]{2,1,0:T(8,128)(2,1)S(1)} %pack_factors.3), channel_id=1, source_target_pairs={{0,2},{1,3},{2,0},{3,1},{4,6},{5,7},{6,4},{7,5},{8,10},{9,11},{10,... | collective-permute-start | bytes 3145736 | tf_op jit(solution)/shard_map/ppermute | solution.py:272
  5.0 25.8 %collective-permute-start.1 = (bf16[4,128,1024]{2,1,0:T(8,128)(2,1)S(1)}, bf16[4,128,1024]{2,1,0:T(8,128)(2,1)S(1)}, u32[]{:S(2)}, u32[]{:S(2)}) collective-permute-start(bf16[4,128,1024]{2,1,0:T(8,128)(2,1)S(1)} %copy-done.1), channel_id=1, source_target_pairs={{4,8},{5,9},{6,10},{7,11},{8,4},{9,5},{10,6},{11,7},{20,24},{21,25... | collective-permute-start | bytes 3145736 | tf_op jit(solution)/shard_map/ppermute | solution.py:279
  5.7 27.0 %collective-permute-start = (bf16[4,128,1024]{2,1,0:T(8,128)(2,1)S(1)}, bf16[4,128,1024]{2,1,0:T(8,128)(2,1)S(1)}, u32[]{:S(2)}, u32[]{:S(2)}) collective-permute-start(bf16[4,128,1024]{2,1,0:T(8,128)(2,1)S(1)} %copy-done.1), channel_id=1, source_target_pairs={{0,4},{1,5},{2,6},{3,7},{4,0},{5,1},{6,2},{7,3},{8,12},{9,13},{10,... | collective-permute-start | bytes 3145736 | tf_op jit(solution)/shard_map/ppermute | solution.py:275
  30.8 21.0 %copy-start.4 = (s32[128]{0:T(128)S(1)}, s32[128]{0:T(128)}, u32[]{:S(2)}) copy-start(s32[128]{0:T(128)} %param.10) | copy-start | bytes 1540
  30.8 21.0 %copy-start.5 = (s32[128]{0:T(128)S(1)}, s32[128]{0:T(128)}, u32[]{:S(2)}) copy-start(s32[128]{0:T(128)} %param.11) | copy-start | bytes 1540
  30.8 22.5 %copy-start.2 = (bf16[4,128,1024]{2,1,0:T(8,128)(2,1)S(1)}, bf16[4,128,1024]{2,1,0:T(8,128)(2,1)}, u32[]{:S(2)}) copy-start(bf16[4,128,1024]{2,1,0:T(8,128)(2,1)} %refs_1_.1) | copy-start | bytes 3145732
  32.7 42.2 %collective-permute-start.10 = (bf16[2,4,4,128,512]{4,3,2,1,0:T(8,128)(2,1)S(1)}, bf16[2,4,4,128,512]{4,3,2,1,0:T(8,128)(2,1)S(1)}, u32[]{:S(2)}, u32[]{:S(2)}) collective-permute-start(bf16[2,4,4,128,512]{4,3,2,1,0:T(8,128)(2,1)S(1)} %get-tuple-element.74), channel_id=1, source_target_pairs={{0,1},{1,0},{2,3},{3,2},{4,5},{5,4},{6,7},{7,6},{8,9},{9,8},{10,11... | collective-permute-start | bytes 12582920 | tf_op jit(solution)/shard_map/ppermute | solution.py:272
  32.7 19.2 %collective-permute-start.3 = (bf16[2,4,128,1024]{3,2,1,0:T(8,128)(2,1)S(1)}, bf16[2,4,128,1024]{3,2,1,0:T(8,128)(2,1)S(1)}, u32[]{:S(2)}, u32[]{:S(2)}) collective-permute-start(bf16[2,4,128,1024]{3,2,1,0:T(8,128)(2,1)S(1)} %pack_core.1), channel_id=1, source_target_pairs={{0,1},{1,0},{2,3},{3,2},{4,5},{5,4},{6,7},{7,6},{8,9},{9,8},{10,11... | collective-permute-start | bytes 6291464 | tf_op jit(solution)/shard_map/ppermute | solution.py:272
  33.2 25.3 %collective-permute-start.6 = (bf16[4,128,1024]{2,1,0:T(8,128)(2,1)S(1)}, bf16[4,128,1024]{2,1,0:T(8,128)(2,1)S(1)}, u32[]{:S(2)}, u32[]{:S(2)}) collective-permute-start(bf16[4,128,1024]{2,1,0:T(8,128)(2,1)S(1)} %pack_factors.4), channel_id=1, source_target_pairs={{0,3},{1,2},{2,1},{3,0},{4,7},{5,6},{6,5},{7,4},{8,11},{9,10},{10,... | collective-permute-start | bytes 3145736 | tf_op jit(solution)/shard_map/ppermute | solution.py:272
  33.5 16.2 %collective-permute-start.4 = (bf16[2,128,1024]{2,1,0:T(8,128)(2,1)S(1)}, bf16[2,128,1024]{2,1,0:T(8,128)(2,1)S(1)}, u32[]{:S(2)}, u32[]{:S(2)}) collective-permute-start(bf16[2,128,1024]{2,1,0:T(8,128)(2,1)S(1)} %get-tuple-element.122), channel_id=1, source_target_pairs={{4,0},{5,1},{6,2},{7,3},{8,12},{9,13},{10,14},{11,15},{20,16},{21,... | collective-permute-start | bytes 1572872 | tf_op jit(solution)/shard_map/ppermute | solution.py:279
  34.8 14.9 %collective-permute-start.5 = (bf16[2,128,1024]{2,1,0:T(8,128)(2,1)S(1)}, bf16[2,128,1024]{2,1,0:T(8,128)(2,1)S(1)}, u32[]{:S(2)}, u32[]{:S(2)}) collective-permute-start(bf16[2,128,1024]{2,1,0:T(8,128)(2,1)S(1)} %get-tuple-element.120), channel_id=1, source_target_pairs={{4,8},{5,9},{6,10},{7,11},{8,4},{9,5},{10,6},{11,7},{20,24},{21,25... | collective-permute-start | bytes 1572872 | tf_op jit(solution)/shard_map/ppermute | solution.py:279
  49.8 17.8 %collective-permute-start.7 = (bf16[2,128,1024]{2,1,0:T(8,128)(2,1)S(1)}, bf16[2,128,1024]{2,1,0:T(8,128)(2,1)S(1)}, u32[]{:S(2)}, u32[]{:S(2)}) collective-permute-start(bf16[2,128,1024]{2,1,0:T(8,128)(2,1)S(1)} %collective-permute-done.5.refs_4_), channel_id=1, source_target_pairs={{4,0},{5,1},{6,2},{7,3},{8,12},{9,13},{10,14},{11,15},{20,16},{21,... | collective-permute-start | bytes 1572872 | tf_op jit(solution)/shard_map/ppermute | solution.py:279
  51.0 17.5 %collective-permute-start.13 = (bf16[2,128,1024]{2,1,0:T(8,128)(2,1)S(1)}, bf16[2,128,1024]{2,1,0:T(8,128)(2,1)S(1)}, u32[]{:S(2)}, u32[]{:S(2)}) collective-permute-start(bf16[2,128,1024]{2,1,0:T(8,128)(2,1)S(1)} %get-tuple-element.84), channel_id=1, source_target_pairs={{4,8},{5,9},{6,10},{7,11},{8,4},{9,5},{10,6},{11,7},{20,24},{21,25... | collective-permute-start | bytes 1572872 | tf_op jit(solution)/shard_map/ppermute | solution.py:279
  52.0 26.8 %collective-permute-start.11 = (bf16[2,128,1024]{2,1,0:T(8,128)(2,1)S(1)}, bf16[2,128,1024]{2,1,0:T(8,128)(2,1)S(1)}, u32[]{:S(2)}, u32[]{:S(2)}) collective-permute-start(bf16[2,128,1024]{2,1,0:T(8,128)(2,1)S(1)} %get-tuple-element.75), channel_id=1, source_target_pairs={{4,0},{5,1},{6,2},{7,3},{8,12},{9,13},{10,14},{11,15},{20,16},{21,... | collective-permute-start | bytes 1572872 | tf_op jit(solution)/shard_map/ppermute | solution.py:279
  61.0 13.9 %copy-start = (bf16[8,16,8192]{2,1,0:T(8,128)(2,1)S(1)}, bf16[8,16,8192]{2,1,0:T(8,128)(2,1)}, u32[]{:S(2)}) copy-start(bf16[8,16,8192]{2,1,0:T(8,128)(2,1)} %param.9) | copy-start | bytes 6291460
  68.6 20.1 %collective-permute-start.14 = (bf16[2,128,1024]{2,1,0:T(8,128)(2,1)S(1)}, bf16[2,128,1024]{2,1,0:T(8,128)(2,1)S(1)}, u32[]{:S(2)}, u32[]{:S(2)}) collective-permute-start(bf16[2,128,1024]{2,1,0:T(8,128)(2,1)S(1)} %collective-permute-done.13.refs_4_), channel_id=1, source_target_pairs={{4,0},{5,1},{6,2},{7,3},{8,12},{9,13},{10,14},{11,15},{20,16},{21,... | collective-permute-start | bytes 1572872 | tf_op jit(solution)/shard_map/ppermute | solution.py:279
  69.9 1.2 collective-permute-start.8
  71.2 3.7 %collective-permute-start.9 = (f32[16,256]{1,0:T(8,128)S(1)}, f32[16,256]{1,0:T(8,128)S(1)}, u32[]{:S(2)}, u32[]{:S(2)}) collective-permute-start(f32[16,256]{1,0:T(8,128)S(1)} %add.82), channel_id=1, source_target_pairs={{0,2},{1,3},{2,0},{3,1},{4,6},{5,7},{6,4},{7,5},{8,10},{9,11},{10,... | collective-permute-start | bytes 49160 | tf_op jit(solution)/shard_map/ppermute | solution.py:272
  75.9 16.8 %collective-permute-start.12 = (bf16[4,128,512]{2,1,0:T(8,128)(2,1)S(1)}, bf16[4,128,512]{2,1,0:T(8,128)(2,1)S(1)}, u32[]{:S(2)}, u32[]{:S(2)}) collective-permute-start(bf16[4,128,512]{2,1,0:T(8,128)(2,1)S(1)} %bitcast.49), channel_id=1, source_target_pairs={{0,2},{1,3},{2,0},{3,1},{4,6},{5,7},{6,4},{7,5},{8,10},{9,11},{10,... | collective-permute-start | bytes 1572872 | tf_op jit(solution)/shard_map/ppermute | solution.py:272
  88.7 14.9 %collective-permute-start.18 = (bf16[2,2,128,512]{3,2,1,0:T(8,128)(2,1)S(1)}, bf16[2,2,128,512]{3,2,1,0:T(8,128)(2,1)S(1)}, u32[]{:S(2)}, u32[]{:S(2)}) collective-permute-start(bf16[2,2,128,512]{3,2,1,0:T(8,128)(2,1)S(1)} %get-tuple-element.90), channel_id=1, source_target_pairs={{0,4},{1,5},{2,6},{3,7},{4,0},{5,1},{6,2},{7,3},{8,12},{9,13},{10,... | collective-permute-start | bytes 1572872 | tf_op jit(solution)/shard_map/ppermute | solution.py:275
  89.9 1.2 collective-permute-start.15
  91.2 3.7 %collective-permute-start.17 = (f32[16,256]{1,0:T(8,128)S(1)}, f32[16,256]{1,0:T(8,128)S(1)}, u32[]{:S(2)}, u32[]{:S(2)}) collective-permute-start(f32[16,256]{1,0:T(8,128)S(1)} %add.86), channel_id=1, source_target_pairs={{0,2},{1,3},{2,0},{3,1},{4,6},{5,7},{6,4},{7,5},{8,10},{9,11},{10,... | collective-permute-start | bytes 49160 | tf_op jit(solution)/shard_map/ppermute | solution.py:272
  94.9 13.6 %collective-permute-start.16 = (bf16[2,128,512]{2,1,0:T(8,128)(2,1)S(1)}, bf16[2,128,512]{2,1,0:T(8,128)(2,1)S(1)}, u32[]{:S(2)}, u32[]{:S(2)}) collective-permute-start(bf16[2,128,512]{2,1,0:T(8,128)(2,1)S(1)} %slice.207), channel_id=1, source_target_pairs={{0,4},{1,5},{2,6},{3,7},{4,0},{5,1},{6,2},{7,3},{8,12},{9,13},{10,... | collective-permute-start | bytes 786440 | tf_op jit(solution)/shard_map/ppermute | solution.py:275
  98.0 14.9 %collective-permute-start.23 = (bf16[4,128,512]{2,1,0:T(8,128)(2,1)S(1)}, bf16[4,128,512]{2,1,0:T(8,128)(2,1)S(1)}, u32[]{:S(2)}, u32[]{:S(2)}) collective-permute-start(bf16[4,128,512]{2,1,0:T(8,128)(2,1)S(1)} %bitcast.50), channel_id=1, source_target_pairs={{0,2},{1,3},{2,0},{3,1},{4,6},{5,7},{6,4},{7,5},{8,10},{9,11},{10,... | collective-permute-start | bytes 1572872 | tf_op jit(solution)/shard_map/ppermute | solution.py:272
  103.8 15.6 %collective-permute-start.21 = (bf16[2,128,512]{2,1,0:T(8,128)(2,1)S(1)}, bf16[2,128,512]{2,1,0:T(8,128)(2,1)S(1)}, u32[]{:S(2)}, u32[]{:S(2)}) collective-permute-start(bf16[2,128,512]{2,1,0:T(8,128)(2,1)S(1)} %fusion.1), channel_id=1, source_target_pairs={{0,2},{1,3},{2,0},{3,1},{4,6},{5,7},{6,4},{7,5},{8,10},{9,11},{10,... | collective-permute-start | bytes 786440 | tf_op jit(solution)/shard_map/ppermute | solution.py:272
  106.9 16.6 %collective-permute-start.20 = (bf16[4,64,512]{2,1,0:T(8,128)(2,1)S(1)}, bf16[4,64,512]{2,1,0:T(8,128)(2,1)S(1)}, u32[]{:S(2)}, u32[]{:S(2)}) collective-permute-start(bf16[4,64,512]{2,1,0:T(8,128)(2,1)S(1)} %bitcast.55), channel_id=1, source_target_pairs={{0,2},{1,3},{2,0},{3,1},{4,6},{5,7},{6,4},{7,5},{8,10},{9,11},{10,... | collective-permute-start | bytes 786440 | tf_op jit(solution)/shard_map/ppermute | solution.py:272
  107.5 10.1 %collective-permute-start.22 = (bf16[2,2,64,512]{3,2,1,0:T(8,128)(2,1)S(1)}, bf16[2,2,64,512]{3,2,1,0:T(8,128)(2,1)S(1)}, u32[]{:S(2)}, u32[]{:S(2)}) collective-permute-start(bf16[2,2,64,512]{3,2,1,0:T(8,128)(2,1)S(1)} %get-tuple-element.97), channel_id=1, source_target_pairs={{0,4},{1,5},{2,6},{3,7},{4,0},{5,1},{6,2},{7,3},{8,12},{9,13},{10,... | collective-permute-start | bytes 786440 | tf_op jit(solution)/shard_map/ppermute | solution.py:275
  108.7 15.4 %collective-permute-start.19 = (bf16[1,128,512]{2,1,0:T(8,128)(2,1)S(1)}, bf16[1,128,512]{2,1,0:T(8,128)(2,1)S(1)}, u32[]{:S(2)}, u32[]{:S(2)}) collective-permute-start(bf16[1,128,512]{2,1,0:T(8,128)(2,1)S(1)} %slice.211), channel_id=1, source_target_pairs={{0,8},{1,9},{2,10},{3,11},{4,12},{5,13},{6,14},{7,15},{8,0},{9,1},... | collective-permute-start | bytes 393224 | tf_op jit(solution)/shard_map/ppermute | solution.py:275
  113.1 11.0 %collective-permute-start.27 = (bf16[2,128,512]{2,1,0:T(8,128)(2,1)S(1)}, bf16[2,128,512]{2,1,0:T(8,128)(2,1)S(1)}, u32[]{:S(2)}, u32[]{:S(2)}) collective-permute-start(bf16[2,128,512]{2,1,0:T(8,128)(2,1)S(1)} %slice.206), channel_id=1, source_target_pairs={{0,4},{1,5},{2,6},{3,7},{4,0},{5,1},{6,2},{7,3},{8,12},{9,13},{10,... | collective-permute-start | bytes 786440 | tf_op jit(solution)/shard_map/ppermute | solution.py:275
  117.7 8.2 %collective-permute-start.26 = (bf16[2,64,512]{2,1,0:T(8,128)(2,1)S(1)}, bf16[2,64,512]{2,1,0:T(8,128)(2,1)S(1)}, u32[]{:S(2)}, u32[]{:S(2)}) collective-permute-start(bf16[2,64,512]{2,1,0:T(8,128)(2,1)S(1)} %fusion.3), channel_id=1, source_target_pairs={{0,2},{1,3},{2,0},{3,1},{4,6},{5,7},{6,4},{7,5},{8,10},{9,11},{10,... | collective-permute-start | bytes 393224 | tf_op jit(solution)/shard_map/ppermute | solution.py:272
  119.4 12.9 %collective-permute-start.24 = (bf16[1,128,512]{2,1,0:T(8,128)(2,1)S(1)}, bf16[1,128,512]{2,1,0:T(8,128)(2,1)S(1)}, u32[]{:S(2)}, u32[]{:S(2)}) collective-permute-start(bf16[1,128,512]{2,1,0:T(8,128)(2,1)S(1)} %slice.210), channel_id=1, source_target_pairs={{0,8},{1,9},{2,10},{3,11},{4,12},{5,13},{6,14},{7,15},{8,0},{9,1},... | collective-permute-start | bytes 393224 | tf_op jit(solution)/shard_map/ppermute | solution.py:275
  123.7 6.3 %collective-permute-start.25 = (bf16[2,64,512]{2,1,0:T(8,128)(2,1)S(1)}, bf16[2,64,512]{2,1,0:T(8,128)(2,1)S(1)}, u32[]{:S(2)}, u32[]{:S(2)}) collective-permute-start(bf16[2,64,512]{2,1,0:T(8,128)(2,1)S(1)} %slice.209), channel_id=1, source_target_pairs={{0,4},{1,5},{2,6},{3,7},{4,0},{5,1},{6,2},{7,3},{8,12},{9,13},{10,... | collective-permute-start | bytes 393224 | tf_op jit(solution)/shard_map/ppermute | solution.py:275
  124.2 11.6 %collective-permute-start.28 = (bf16[1,128,512]{2,1,0:T(8,128)(2,1)S(1)}, bf16[1,128,512]{2,1,0:T(8,128)(2,1)S(1)}, u32[]{:S(2)}, u32[]{:S(2)}) collective-permute-start(bf16[1,128,512]{2,1,0:T(8,128)(2,1)S(1)} %slice.208), channel_id=1, source_target_pairs={{0,8},{1,9},{2,10},{3,11},{4,12},{5,13},{6,14},{7,15},{8,0},{9,1},... | collective-permute-start | bytes 393224 | tf_op jit(solution)/shard_map/ppermute | solution.py:275
  125.9 10.8 %collective-permute-start.29 = (bf16[1,64,512]{2,1,0:T(8,128)(2,1)S(1)}, bf16[1,64,512]{2,1,0:T(8,128)(2,1)S(1)}, u32[]{:S(2)}, u32[]{:S(2)}) collective-permute-start(bf16[1,64,512]{2,1,0:T(8,128)(2,1)S(1)} %slice.213), channel_id=1, source_target_pairs={{0,8},{1,9},{2,10},{3,11},{4,12},{5,13},{6,14},{7,15},{8,0},{9,1},... | collective-permute-start | bytes 196616 | tf_op jit(solution)/shard_map/ppermute | solution.py:275
  130.0 7.5 %collective-permute-start.30 = (bf16[1,64,512]{2,1,0:T(8,128)(2,1)S(1)}, bf16[1,64,512]{2,1,0:T(8,128)(2,1)S(1)}, u32[]{:S(2)}, u32[]{:S(2)}) collective-permute-start(bf16[1,64,512]{2,1,0:T(8,128)(2,1)S(1)} %slice.212), channel_id=1, source_target_pairs={{0,8},{1,9},{2,10},{3,11},{4,12},{5,13},{6,14},{7,15},{8,0},{9,1},... | collective-permute-start | bytes 196616 | tf_op jit(solution)/shard_map/ppermute | solution.py:275
  137.5 0.8 copy-start.3

commit v5 on v4

--- a/solution.py
+++ b/solution.py
@@ -195,8 +195,8 @@
     )(place, slots, *held_in)
 
 
-def add_extra(place, low, slots, mine, other, keep, recv, first_step, pieces, per_shard, rank):
-    _, planes, _, requests, width = keep.shape
+def add_extra(place, low, slots, mine, other, keep, recv, first_row, pieces, per_shard, rank):
+    _, planes, _, width = keep.shape
     rows, lanes = mine.shape[0], low.shape[1]
     half = planes // 2
     parts = {
@@ -214,11 +214,10 @@
             first = (place_ref[0] * PLANE + (place_ref[1] ^ i)) * per_shard
             masked = [jnp.where(wanted == first + a, rounded, 0.0) for a in range(per_shard)]
             spread.append(jnp.concatenate(masked, axis=0).T.astype(BF16))
-        for (step, what, part, share), out_ref in zip(pieces, out_refs):
-            size = requests // share
-            start = (step - first_step) * requests + part * size
+        for (what, row, size), out_ref in zip(pieces, out_refs):
+            start = row - first_row
             here = [value[start : start + size] for value in spread]
-            rows_at = slice(part * size, (part + 1) * size)
+            rows_at = slice(row, row + size)
             for side_at, side in enumerate(parts[what][0]):
                 for block_at, i in enumerate(parts[what][1]):
                     block = (place_ref[0] ^ halving(i, planes)) * PLANE + (place_ref[1] ^ (2 * side))
@@ -226,11 +225,11 @@
                     own, other_own = m_ref[:, columns], t_ref[1, i, :, side * width : (side + 1) * width]
                     extra = jnp.dot(here[0], own, preferred_element_type=F32)
                     extra += jnp.dot(here[1], other_own, preferred_element_type=F32)
-                    base = k_ref[side, i, step, rows_at] + r_ref[side, i, step, rows_at].astype(F32)
+                    base = k_ref[side, i, rows_at] + r_ref[side, i, rows_at].astype(F32)
                     out_ref[side_at, block_at] = (base + extra).astype(out_ref.dtype)
 
-    def shape(step, what, part, share):
-        return (len(parts[what][0]), len(parts[what][1]), requests // share, width)
+    def shape(what, row, size):
+        return (len(parts[what][0]), len(parts[what][1]), size, width)
 
     whole = pl.BlockSpec(memory_space=pltpu.VMEM)
     return pl.pallas_call(
@@ -242,7 +241,7 @@
             out_specs=[whole] * len(pieces),
         ),
         out_shape=[
-            jax.ShapeDtypeStruct(shape(*piece), BF16 if piece[1] in (SEND_Y, SEND_Z) else F32)
+            jax.ShapeDtypeStruct(shape(*piece), BF16 if piece[0] in (SEND_Y, SEND_Z) else F32)
             for piece in pieces
         ],
         cost_estimate=cost(4 * lanes * rows * planes * width, 10 * lanes * planes * width),
@@ -355,10 +354,13 @@
             low = low + part
         return low + in_plane(low, 1)
 
-    def with_extra(low, first_step, pieces):
+    flat = (2, planes, steps * requests, width)
+    keep, recv = keep.reshape(flat), recv.reshape(flat)
+
+    def with_extra(low, first_row, pieces):
         lanes = slots[:, : low.shape[1]]
         return add_extra(
-            place, low, lanes, second, from_core, keep, recv, first_step, pieces, per_shard, rank
+            place, low, lanes, second, from_core, keep, recv, first_row, pieces, per_shard, rank
         )
 
     along_z = [1 << bit for bit in range(planes.bit_length() - 1)]
@@ -395,10 +397,15 @@
         ready = part
     low = core_sum(LOW_CHUNKS[0], parts)
     low = low + in_plane(low, 2)
-    (goes,) = with_extra(low[:, :requests], 0, [(0, SEND_Y, 0, 1)])
+    half = requests // 2
+    rows = [0, requests + half // 2, 2 * requests, 3 * requests, 3 * requests + half, steps * requests]
+    spans = [(a, b - a) for a, b in zip(rows, rows[1:])]
+    (goes,) = with_extra(low, 0, [(SEND_Y, *spans[0])])
     low = after(low, goes, *second_wave)
     moved = send(goes[0], "y")
-    stays, goes, next_stays = with_extra(low, 0, [(0, KEEP_Y, 0, 1), (1, SEND_Z, 0, 1), (1, KEEP_Z, 0, 1)])
+    stays, goes, next_stays = with_extra(
+        low, 0, [(KEEP_Y, *spans[0]), (SEND_Z, *spans[1]), (KEEP_Z, *spans[1])]
+    )
     state[0] = (stays[0], moved)
     parts, ready = [], (stays, goes, next_stays)
     for i, source in enumerate(late[1]):
@@ -411,20 +418,26 @@
     across_y = in_plane(low, 2)
     done = add(0, low)
     low = low + after(across_y, done)
-    (moved,) = with_extra(low[:, :requests], 2, [(2, SEND_Y, 0, 1)])
+    (moved,) = with_extra(low, spans[2][0], [(SEND_Y, *spans[2])])
     done = add(1, moved)
     low = after(low, done)
     sent_y = send(moved[0], "y")
     stays, goes, next_stays, last_goes, last_stays = with_extra(
         low,
-        2,
-        [(2, KEEP_Y, 0, 1), (3, SEND_Z, 0, 2), (3, KEEP_Z, 0, 2), (3, SEND_Y, 1, 2), (3, KEEP_Y, 1, 2)],
+        spans[2][0],
+        [
+            (KEEP_Y, *spans[2]),
+            (SEND_Z, *spans[3]),
+            (KEEP_Z, *spans[3]),
+            (SEND_Y, *spans[4]),
+            (KEEP_Y, *spans[4]),
+        ],
     )
     state[2] = (stays[0], sent_y)
     begin(3, next_stays, goes)
     begin(4, last_stays, last_goes)
     done = next_stays
-    for c in (0, 2, 3, 1, 4, 0, 2, 3, 4, 1, 2, 3, 4):
+    for c in (0, 2, 1, 3, 4, 2, 3, 4, 0, 1, 2, 3, 4):
         if plans[c]:
             done = add(c, done)
     for c in range(len(plans)):

time: 139 us -> 137 us (0.986)
  waiting for transfers between devices: 68.1 us -> 65.4 us
    ppermute x11, waiting for transfers between devices: 21.2 us -> 13.4 us  [along(): lax.ppermute(value, 'tensor', [(t, t ^ other * PLANE) for t in range(devi...]
    ppermute x13, waiting for transfers between devices: 17.6 us -> 22.9 us  [in_plane(): lax.ppermute(value, 'tensor', [(t, t ^ other) for t in range(devices)])]
  transfers between devices with their start and end apart: 31 -> 31, of which waited for: 20 -> 19; matrix products, arithmetic and copies ran while one was open for 1% -> 1% of each run, Pallas kernels for 24% -> 24%
where the time goes in v5:
time: 137 us; the launch traced here: 136 us
  waiting for transfers between devices  65.4 us (48%)
  Pallas kernels  35 us (26%)
  starting transfers between devices  32.8 us (24%)
  other arithmetic  1.4 us (1%)
    ppermute x7, waiting for transfers between devices, hop(): return lax.ppermute(value, 'tensor', pairs)  29.1 us
    ppermute x13, waiting for transfers between devices, in_plane(): lax.ppermute(value, 'tensor', [(t, t ^ other) for t in range(devices)])  22.9 us
    pallas_call x1, Pallas kernels, base_blocks(): pl.pallas_call(body, grid_spec=pltpu.PrefetchScalarGridSpec(num_scalar_pr...  13.9 us
    ppermute x13, starting transfers between devices, in_plane(): lax.ppermute(value, 'tensor', [(t, t ^ other) for t in range(devices)])  13.8 us
    ppermute x11, waiting for transfers between devices, along(): lax.ppermute(value, 'tensor', [(t, t ^ other * PLANE) for t in range(devi...  13.4 us
    ppermute x11, starting transfers between devices, along(): lax.ppermute(value, 'tensor', [(t, t ^ other * PLANE) for t in range(devi...  11.8 us
    pallas_call x6, Pallas kernels, low_part(): pl.pallas_call(body, grid_spec=pltpu.PrefetchScalarGridSpec(num_scalar_pr...  7.34 us
    ppermute x7, starting transfers between devices, hop(): return lax.ppermute(value, 'tensor', pairs)  7.26 us
  transfers between devices with their start and end apart: 31, of which 19 were waited for; matrix products, arithmetic and copies ran while one was open for 1% of the time, Pallas kernels for 24%

profile of v5, /device:TPU:0, one launch (start us, length us, event | category | flops | bytes accessed | tf_op | source)
XLA Modules:
  0.0 136.4 jit_solution(2901717523847783931)
XLA Ops:
  0.2 1.8 %pack_factors.3 = bf16[4,128,1024]{2,1,0:T(8,128)(2,1)S(1)} custom-call(s32[3]{0:T(128)S(1)} %pad_add_fusion.place_ref, s32[4]{0:T(128)S(1)} %pad_add_fusion.1.order_ref, bf16[128,16384]{1,0:T(8,128)(2,1)} %bitcast.65, bf16[128,16384]{1,0:T(8,128)(2,1)} %bitcast.66, bf16[128,16384]{1,0:T(8,128)(2,1)} %bitcast.67, bf16[128,16384]{1,0:T(8,128)(2,1)} %bitcast.68), custom_call_target="tpu_custom_call" | custom-call | bytes 2097 | tf_op jit(solution)/shard_map/pack_factors/pallas_call | solution.py:52
  2.0 3.0 %collective-permute-start.2 = (bf16[4,128,1024]{2,1,0:T(8,128)(2,1)S(1)}, bf16[4,128,1024]{2,1,0:T(8,128)(2,1)S(1)}, u32[]{:S(2)}, u32[]{:S(2)}) collective-permute-start(bf16[4,128,1024]{2,1,0:T(8,128)(2,1)S(1)} %pack_factors.3), channel_id=1, source_target_pairs={{0,2},{1,3},{2,0},{3,1},{4,6},{5,7},{6,4},{7,5},{8,10},{9,11},{10,... | collective-permute-start | bytes 3145736 | tf_op jit(solution)/shard_map/ppermute | solution.py:271
  5.7 4.4 %collective-permute-start = (bf16[4,128,1024]{2,1,0:T(8,128)(2,1)S(1)}, bf16[4,128,1024]{2,1,0:T(8,128)(2,1)S(1)}, u32[]{:S(2)}, u32[]{:S(2)}) collective-permute-start(bf16[4,128,1024]{2,1,0:T(8,128)(2,1)S(1)} %copy-done.1), channel_id=1, source_target_pairs={{0,4},{1,5},{2,6},{3,7},{4,0},{5,1},{6,2},{7,3},{8,12},{9,13},{10,... | collective-permute-start | bytes 3145736 | tf_op jit(solution)/shard_map/ppermute | solution.py:274
  10.1 1.8 %pack_factors.4 = bf16[4,128,1024]{2,1,0:T(8,128)(2,1)S(1)} custom-call(s32[3]{0:T(128)S(1)} %pad_add_fusion.place_ref, s32[4]{0:T(128)S(1)} %pad_add_fusion.1.order_ref, bf16[128,16384]{1,0:T(8,128)(2,1)} %bitcast.69, bf16[128,16384]{1,0:T(8,128)(2,1)} %bitcast.70, bf16[128,16384]{1,0:T(8,128)(2,1)} %bitcast.71, bf16[128,16384]{1,0:T(8,128)(2,1)} %bitcast.72), custom_call_target="tpu_custom_call" | custom-call | bytes 2097 | tf_op jit(solution)/shard_map/pack_factors/pallas_call | solution.py:52
  11.9 1.8 %pack_factors.5.refs_0_ = bf16[4,128,1024]{2,1,0:T(8,128)(2,1)S(1)} custom-call(s32[3]{0:T(128)S(1)} %pad_add_fusion.place_ref, s32[4]{0:T(128)S(1)} %pad_add_fusion.1.order_ref, bf16[128,16384]{1,0:T(8,128)(2,1)} %bitcast.73, bf16[128,16384]{1,0:T(8,128)(2,1)} %bitcast.74, bf16[128,16384]{1,0:T(8,128)(2,1)} %bitcast.75, bf16[128,16384]{1,0:T(8,128)(2,1)} %bitcast.76), custom_call_target="tpu_custom_call" | custom-call | bytes 2097 | tf_op jit(solution)/shard_map/pack_factors/pallas_call | solution.py:52
  13.7 3.1 %pack_core.1 = bf16[2,4,128,1024]{3,2,1,0:T(8,128)(2,1)S(1)} custom-call(s32[3]{0:T(128)S(1)} %pad_add_fusion.place_ref, s32[4]{0:T(128)S(1)} %pad_add_fusion.1.order_ref, bf16[128,16384]{1,0:T(8,128)(2,1)} %bitcast.77, bf16[128,8192]{1,0:T(8,128)(2,1)} %bitcast.49, bf16[128,8192]{1,0:T(8,128)(2,1)} %bitcast.50), custom_call_target="tpu_custom_call" | custom-call | bytes 4194 | tf_op jit(solution)/shard_map/pack_core/pallas_call | solution.py:82
  16.9 13.9 %base_blocks.1 = (bf16[2,4,4,128,512]{4,3,2,1,0:T(8,128)(2,1)S(1)}, f32[2,4,4,128,512]{4,3,2,1,0:T(8,128)S(1)}) custom-call(s32[3]{0:T(128)S(1)} %pad_add_fusion.place_ref, bf16[4,128,1024]{2,1,0:T(8,128)(2,1)} %refs_1_.1, bf16[1024,8192]{1,0:T(8,128)(2,1)} %d3.1, bf16[1024,8192]{1,0:T(8,128)(2,1)} %d3.1, bf16[1024,8192]{1,0:T(8,128)(2,1)} %d3.1, ...), custom_call_target="tpu_custom_call" | custom-call | flops 8589934 | bytes 29360 | tf_op jit(solution)/shard_map/base_blocks/pallas_call | solution.py:114
  30.8 1.9 %collective-permute-done.refs_4_.refs_2_ = bf16[4,128,1024]{2,1,0:T(8,128)(2,1)S(1)} collective-permute-done((bf16[4,128,1024]{2,1,0:T(8,128)(2,1)S(1)}, bf16[4,128,1024]{2,1,0:T(8,128)(2,1)S(1)}, u32[]{:S(2)}, u32[]{:S(2)}) %collective-permute-start) | collective-permute-done | bytes 1048608 | tf_op jit(solution)/shard_map/ppermute | solution.py:274
  33.6 1.3 collective-permute-start.4
  35.6 14.2 %collective-permute-done.4.refs_5_ = bf16[2,128,1024]{2,1,0:T(8,128)(2,1)S(1)} collective-permute-done((bf16[2,128,1024]{2,1,0:T(8,128)(2,1)S(1)}, bf16[2,128,1024]{2,1,0:T(8,128)(2,1)S(1)}, u32[]{:S(2)}, u32[]{:S(2)}) %collective-permute-start.4) | collective-permute-done | bytes 524320 | tf_op jit(solution)/shard_map/ppermute | solution.py:278
  49.7 1.3 collective-permute-start.7
  52.0 1.3 collective-permute-start.11
  53.3 1.5 %low_part.6 = f32[16,512]{1,0:T(8,128)S(1)} custom-call(s32[3]{0:T(128)S(1)} %pad_add_fusion.place_ref, s32[1,512]{1,0:T(1,128)S(1)} %bitcast.62, bf16[4,128,1024]{2,1,0:T(8,128)(2,1)S(1)} %pack_factors.5.refs_0_, bf16[2,4,128,1024]{3,2,1,0:T(8,128)(2,1)S(1)} %collective-permute-done.3.refs_1_.t_ref, ...), custom_call_target="tpu_custom_call" | custom-call | flops 805306368 | bytes 3670016 | tf_op jit(solution)/shard_map/low_part/pallas_call | solution.py:175
  54.8 3.6 %collective-permute-done.6.refs_0_.refs_3_ = bf16[4,128,1024]{2,1,0:T(8,128)(2,1)S(1)} collective-permute-done((bf16[4,128,1024]{2,1,0:T(8,128)(2,1)S(1)}, bf16[4,128,1024]{2,1,0:T(8,128)(2,1)S(1)}, u32[]{:S(2)}, u32[]{:S(2)}) %collective-permute-start.6) | collective-permute-done | bytes 1048608 | tf_op jit(solution)/shard_map/ppermute | solution.py:271
  58.4 1.4 %low_part.7 = f32[16,512]{1,0:T(8,128)S(1)} custom-call(s32[3]{0:T(128)S(1)} %pad_add_fusion.place_ref, s32[1,512]{1,0:T(1,128)S(1)} %bitcast.63, bf16[4,128,1024]{2,1,0:T(8,128)(2,1)S(1)} %collective-permute-done.6.refs_0_.refs_3_, bf16[4,128,1024]{2,1,0:T(8,128)(2,1)S(1)} %copy-done.2, bf16[4,128,1024]{2,1,0:T(8,128)(2,1)S(1)} %collective-permute-done.refs_4_.refs_2_), custom_call_target="tpu_custom_call" | custom-call | flops 268435456 | bytes 2621440 | tf_op jit(solution)/shard_map/low_part/pallas_call | solution.py:175
  59.8 1.1 low_part.8
  60.9 6.6 %collective-permute-done.7.refs_5_ = bf16[2,128,1024]{2,1,0:T(8,128)(2,1)S(1)} collective-permute-done((bf16[2,128,1024]{2,1,0:T(8,128)(2,1)S(1)}, bf16[2,128,1024]{2,1,0:T(8,128)(2,1)S(1)}, u32[]{:S(2)}, u32[]{:S(2)}) %collective-permute-start.7) | collective-permute-done | bytes 524320 | tf_op jit(solution)/shard_map/ppermute | solution.py:278
  67.5 1.1 low_part.9
  68.6 1.3 collective-permute-start.14
  70.0 1.2 collective-permute-done.8
  71.2 1.5 %collective-permute-start.9 = (f32[16,256]{1,0:T(8,128)S(1)}, f32[16,256]{1,0:T(8,128)S(1)}, u32[]{:S(2)}, u32[]{:S(2)}) collective-permute-start(f32[16,256]{1,0:T(8,128)S(1)} %add.82), channel_id=1, source_target_pairs={{0,2},{1,3},{2,0},{3,1},{4,6},{5,7},{6,4},{7,5},{8,10},{9,11},{10,... | collective-permute-start | bytes 49160 | tf_op jit(solution)/shard_map/ppermute | solution.py:271
  72.7 2.2 %collective-permute-done.9 = f32[16,256]{1,0:T(8,128)S(1)} collective-permute-done((f32[16,256]{1,0:T(8,128)S(1)}, f32[16,256]{1,0:T(8,128)S(1)}, u32[]{:S(2)}, u32[]{:S(2)}) %collective-permute-start.9) | collective-permute-done | bytes 16416 | tf_op jit(solution)/shard_map/ppermute | solution.py:271
  74.9 1.1 add_extra.4
  76.0 1.6 %collective-permute-start.12 = (bf16[4,160,512]{2,1,0:T(8,128)(2,1)S(1)}, bf16[4,160,512]{2,1,0:T(8,128)(2,1)S(1)}, u32[]{:S(2)}, u32[]{:S(2)}) collective-permute-start(bf16[4,160,512]{2,1,0:T(8,128)(2,1)S(1)} %bitcast.59), channel_id=1, source_target_pairs={{0,2},{1,3},{2,0},{3,1},{4,6},{5,7},{6,4},{7,5},{8,10},{9,11},{10,... | collective-permute-start | bytes 1966088 | tf_op jit(solution)/shard_map/ppermute | solution.py:271
  77.6 1.1 collective-permute-done.11.refs_5_
  78.7 1.5 %add_extra.5 = (f32[1,4,160,512]{3,2,1,0:T(8,128)S(1)}, bf16[2,2,96,512]{3,2,1,0:T(8,128)(2,1)S(1)}, f32[2,2,96,512]{3,2,1,0:T(8,128)S(1)}) custom-call(s32[3]{0:T(128)S(1)} %pad_add_fusion.place_ref, f32[16,256]{1,0:T(8,128)S(1)} %add.83.low_ref, s32[1,256]{1,0:T(1,128)S(1)} %get-tuple-element.124.slots_ref, bf16[128,8192]{1,0:T(8,128)(2,1)S(1)} %bitcast.52, ...), custom_call_target="tpu_custom_call" | custom-call | flops 268435 | bytes 5242 | tf_op jit(solution)/shard_map/add_extra/pallas_call | solution.py:235
  80.3 1.1 low_part.10
  81.4 7.2 %collective-permute-done.14.refs_5_ = bf16[2,128,1024]{2,1,0:T(8,128)(2,1)S(1)} collective-permute-done((bf16[2,128,1024]{2,1,0:T(8,128)(2,1)S(1)}, bf16[2,128,1024]{2,1,0:T(8,128)(2,1)S(1)}, u32[]{:S(2)}, u32[]{:S(2)}) %collective-permute-start.14) | collective-permute-done | bytes 524320 | tf_op jit(solution)/shard_map/ppermute | solution.py:278
  88.6 1.2 low_part.11
  89.9 1.2 collective-permute-done.15
  91.1 1.5 %collective-permute-start.17 = (f32[16,256]{1,0:T(8,128)S(1)}, f32[16,256]{1,0:T(8,128)S(1)}, u32[]{:S(2)}, u32[]{:S(2)}) collective-permute-start(f32[16,256]{1,0:T(8,128)S(1)} %add.86), channel_id=1, source_target_pairs={{0,2},{1,3},{2,0},{3,1},{4,6},{5,7},{6,4},{7,5},{8,10},{9,11},{10,... | collective-permute-start | bytes 49160 | tf_op jit(solution)/shard_map/ppermute | solution.py:271
  92.9 1.9 %collective-permute-done.17 = f32[16,256]{1,0:T(8,128)S(1)} collective-permute-done((f32[16,256]{1,0:T(8,128)S(1)}, f32[16,256]{1,0:T(8,128)S(1)}, u32[]{:S(2)}, u32[]{:S(2)}) %collective-permute-start.17) | collective-permute-done | bytes 16416 | tf_op jit(solution)/shard_map/ppermute | solution.py:271
  94.8 2.0 %collective-permute-start.16 = (bf16[2,160,512]{2,1,0:T(8,128)(2,1)S(1)}, bf16[2,160,512]{2,1,0:T(8,128)(2,1)S(1)}, u32[]{:S(2)}, u32[]{:S(2)}) collective-permute-start(bf16[2,160,512]{2,1,0:T(8,128)(2,1)S(1)} %slice.192), channel_id=1, source_target_pairs={{0,4},{1,5},{2,6},{3,7},{4,0},{5,1},{6,2},{7,3},{8,12},{9,13},{10,... | collective-permute-start | bytes 983048 | tf_op jit(solution)/shard_map/ppermute | solution.py:274
  96.9 1.0 add_extra.6
  97.9 1.6 %collective-permute-done.18 = bf16[2,2,96,512]{3,2,1,0:T(8,128)(2,1)S(1)} collective-permute-done((bf16[2,2,96,512]{3,2,1,0:T(8,128)(2,1)S(1)}, bf16[2,2,96,512]{3,2,1,0:T(8,128)(2,1)S(1)}, u32[]{:S(2)}, u32[]{:S(2)}) %collective-permute-start.18) | collective-permute-done | bytes 393248 | tf_op jit(solution)/shard_map/ppermute | solution.py:274
  99.5 1.5 %collective-permute-start.23 = (bf16[4,128,512]{2,1,0:T(8,128)(2,1)S(1)}, bf16[4,128,512]{2,1,0:T(8,128)(2,1)S(1)}, u32[]{:S(2)}, u32[]{:S(2)}) collective-permute-start(bf16[4,128,512]{2,1,0:T(8,128)(2,1)S(1)} %bitcast.60), channel_id=1, source_target_pairs={{0,2},{1,3},{2,0},{3,1},{4,6},{5,7},{6,4},{7,5},{8,10},{9,11},{10,... | collective-permute-start | bytes 1572872 | tf_op jit(solution)/shard_map/ppermute | solution.py:271
  101.7 1.6 %add_extra.7 = (f32[1,4,128,512]{3,2,1,0:T(8,128)S(1)}, bf16[2,2,64,512]{3,2,1,0:T(8,128)(2,1)S(1)}, f32[2,2,64,512]{3,2,1,0:T(8,128)S(1)}, bf16[1,4,64,512]{3,2,1,0:T(8,128)(2,1)S(1)}, f32[1,4,64,512]{3,2,1,0:T(8,128)S(1)}) custom-call(s32[3]{0:T(128)S(1)} %pad_add_fusion.place_ref, f32[16,256]{1,0:T(8,128)S(1)} %add.88.low_ref, ...), custom_call_target="tpu_custom_call" | custom-call | flops 268435 | bytes 5242 | tf_op jit(solution)/shard_map/add_extra/pallas_call | solution.py:235
  103.4 1.6 %collective-permute-start.20 = (bf16[4,64,512]{2,1,0:T(8,128)(2,1)S(1)}, bf16[4,64,512]{2,1,0:T(8,128)(2,1)S(1)}, u32[]{:S(2)}, u32[]{:S(2)}) collective-permute-start(bf16[4,64,512]{2,1,0:T(8,128)(2,1)S(1)} %bitcast.64), channel_id=1, source_target_pairs={{0,2},{1,3},{2,0},{3,1},{4,6},{5,7},{6,4},{7,5},{8,10},{9,11},{10,... | collective-permute-start | bytes 786440 | tf_op jit(solution)/shard_map/ppermute | solution.py:271
  105.0 1.4 %collective-permute-done.16 = bf16[2,160,512]{2,1,0:T(8,128)(2,1)S(1)} collective-permute-done((bf16[2,160,512]{2,1,0:T(8,128)(2,1)S(1)}, bf16[2,160,512]{2,1,0:T(8,128)(2,1)S(1)}, u32[]{:S(2)}, u32[]{:S(2)}) %collective-permute-start.16) | collective-permute-done | bytes 327712 | tf_op jit(solution)/shard_map/ppermute | solution.py:274
  107.1 7.3 %collective-permute-done.23 = bf16[4,128,512]{2,1,0:T(8,128)(2,1)S(1)} collective-permute-done((bf16[4,128,512]{2,1,0:T(8,128)(2,1)S(1)}, bf16[4,128,512]{2,1,0:T(8,128)(2,1)S(1)}, u32[]{:S(2)}, u32[]{:S(2)}) %collective-permute-start.23) | collective-permute-done | bytes 524320 | tf_op jit(solution)/shard_map/ppermute | solution.py:271
  114.6 3.9 %collective-permute-done.22 = bf16[2,96,512]{2,1,0:T(8,128)(2,1)S(1)} collective-permute-done((bf16[2,96,512]{2,1,0:T(8,128)(2,1)S(1)}, bf16[2,96,512]{2,1,0:T(8,128)(2,1)S(1)}, u32[]{:S(2)}, u32[]{:S(2)}) %collective-permute-start.22) | collective-permute-done | bytes 196640 | tf_op jit(solution)/shard_map/ppermute | solution.py:271
  118.9 1.6 %collective-permute-start.25 = (bf16[2,64,512]{2,1,0:T(8,128)(2,1)S(1)}, bf16[2,64,512]{2,1,0:T(8,128)(2,1)S(1)}, u32[]{:S(2)}, u32[]{:S(2)}) collective-permute-start(bf16[2,64,512]{2,1,0:T(8,128)(2,1)S(1)} %fusion.3), channel_id=1, source_target_pairs={{0,2},{1,3},{2,0},{3,1},{4,6},{5,7},{6,4},{7,5},{8,10},{9,11},{10,... | collective-permute-start | bytes 393224 | tf_op jit(solution)/shard_map/ppermute | solution.py:271
  120.5 1.6 %collective-permute-done.20 = bf16[4,64,512]{2,1,0:T(8,128)(2,1)S(1)} collective-permute-done((bf16[4,64,512]{2,1,0:T(8,128)(2,1)S(1)}, bf16[4,64,512]{2,1,0:T(8,128)(2,1)S(1)}, u32[]{:S(2)}, u32[]{:S(2)}) %collective-permute-start.20) | collective-permute-done | bytes 262176 | tf_op jit(solution)/shard_map/ppermute | solution.py:271
  122.6 1.7 %collective-permute-start.28 = (bf16[1,128,512]{2,1,0:T(8,128)(2,1)S(1)}, bf16[1,128,512]{2,1,0:T(8,128)(2,1)S(1)}, u32[]{:S(2)}, u32[]{:S(2)}) collective-permute-start(bf16[1,128,512]{2,1,0:T(8,128)(2,1)S(1)} %slice.195), channel_id=1, source_target_pairs={{0,8},{1,9},{2,10},{3,11},{4,12},{5,13},{6,14},{7,15},{8,0},{9,1},... | collective-permute-start | bytes 393224 | tf_op jit(solution)/shard_map/ppermute | solution.py:274
  124.4 2.5 %collective-permute-start.29 = (bf16[1,64,512]{2,1,0:T(8,128)(2,1)S(1)}, bf16[1,64,512]{2,1,0:T(8,128)(2,1)S(1)}, u32[]{:S(2)}, u32[]{:S(2)}) collective-permute-start(bf16[1,64,512]{2,1,0:T(8,128)(2,1)S(1)} %slice.199), channel_id=1, source_target_pairs={{0,8},{1,9},{2,10},{3,11},{4,12},{5,13},{6,14},{7,15},{8,0},{9,1},... | collective-permute-start | bytes 196616 | tf_op jit(solution)/shard_map/ppermute | solution.py:274
  126.9 2.5 %collective-permute-done.24 = bf16[2,64,512]{2,1,0:T(8,128)(2,1)S(1)} collective-permute-done((bf16[2,64,512]{2,1,0:T(8,128)(2,1)S(1)}, bf16[2,64,512]{2,1,0:T(8,128)(2,1)S(1)}, u32[]{:S(2)}, u32[]{:S(2)}) %collective-permute-start.24) | collective-permute-done | bytes 131104 | tf_op jit(solution)/shard_map/ppermute | solution.py:274
  129.7 4.3 %collective-permute-done.28 = bf16[1,128,512]{2,1,0:T(8,128)(2,1)S(1)} collective-permute-done((bf16[1,128,512]{2,1,0:T(8,128)(2,1)S(1)}, bf16[1,128,512]{2,1,0:T(8,128)(2,1)S(1)}, u32[]{:S(2)}, u32[]{:S(2)}) %collective-permute-start.28) | collective-permute-done | bytes 131104 | tf_op jit(solution)/shard_map/ppermute | solution.py:274
  134.0 0.9 collective-permute-done.29
  (80 shorter events, 8.0 us)
Async XLA Ops:
  0.2 4.8 %copy-start.1 = (bf16[4,128,1024]{2,1,0:T(8,128)(2,1)S(1)}, bf16[4,128,1024]{2,1,0:T(8,128)(2,1)}, u32[]{:S(2)}) copy-start(bf16[4,128,1024]{2,1,0:T(8,128)(2,1)} %refs_1_.1) | copy-start | bytes 3145732
  2.0 28.8 %collective-permute-start.2 = (bf16[4,128,1024]{2,1,0:T(8,128)(2,1)S(1)}, bf16[4,128,1024]{2,1,0:T(8,128)(2,1)S(1)}, u32[]{:S(2)}, u32[]{:S(2)}) collective-permute-start(bf16[4,128,1024]{2,1,0:T(8,128)(2,1)S(1)} %pack_factors.3), channel_id=1, source_target_pairs={{0,2},{1,3},{2,0},{3,1},{4,6},{5,7},{6,4},{7,5},{8,10},{9,11},{10,... | collective-permute-start | bytes 3145736 | tf_op jit(solution)/shard_map/ppermute | solution.py:271
  5.0 25.8 %collective-permute-start.1 = (bf16[4,128,1024]{2,1,0:T(8,128)(2,1)S(1)}, bf16[4,128,1024]{2,1,0:T(8,128)(2,1)S(1)}, u32[]{:S(2)}, u32[]{:S(2)}) collective-permute-start(bf16[4,128,1024]{2,1,0:T(8,128)(2,1)S(1)} %copy-done.1), channel_id=1, source_target_pairs={{4,8},{5,9},{6,10},{7,11},{8,4},{9,5},{10,6},{11,7},{20,24},{21,25... | collective-permute-start | bytes 3145736 | tf_op jit(solution)/shard_map/ppermute | solution.py:278
  5.7 27.0 %collective-permute-start = (bf16[4,128,1024]{2,1,0:T(8,128)(2,1)S(1)}, bf16[4,128,1024]{2,1,0:T(8,128)(2,1)S(1)}, u32[]{:S(2)}, u32[]{:S(2)}) collective-permute-start(bf16[4,128,1024]{2,1,0:T(8,128)(2,1)S(1)} %copy-done.1), channel_id=1, source_target_pairs={{0,4},{1,5},{2,6},{3,7},{4,0},{5,1},{6,2},{7,3},{8,12},{9,13},{10,... | collective-permute-start | bytes 3145736 | tf_op jit(solution)/shard_map/ppermute | solution.py:274
  32.7 19.0 %copy-start.4 = (s32[128]{0:T(128)S(1)}, s32[128]{0:T(128)}, u32[]{:S(2)}) copy-start(s32[128]{0:T(128)} %param.10) | copy-start | bytes 1540
  32.7 19.0 %copy-start.5 = (s32[128]{0:T(128)S(1)}, s32[128]{0:T(128)}, u32[]{:S(2)}) copy-start(s32[128]{0:T(128)} %param.11) | copy-start | bytes 1540
  32.7 20.5 %copy-start.2 = (bf16[4,128,1024]{2,1,0:T(8,128)(2,1)S(1)}, bf16[4,128,1024]{2,1,0:T(8,128)(2,1)}, u32[]{:S(2)}) copy-start(bf16[4,128,1024]{2,1,0:T(8,128)(2,1)} %refs_1_.1) | copy-start | bytes 3145732
  32.7 42.2 %collective-permute-start.10 = (bf16[2,4,4,128,512]{4,3,2,1,0:T(8,128)(2,1)S(1)}, bf16[2,4,4,128,512]{4,3,2,1,0:T(8,128)(2,1)S(1)}, u32[]{:S(2)}, u32[]{:S(2)}) collective-permute-start(bf16[2,4,4,128,512]{4,3,2,1,0:T(8,128)(2,1)S(1)} %get-tuple-element.74), channel_id=1, source_target_pairs={{0,1},{1,0},{2,3},{3,2},{4,5},{5,4},{6,7},{7,6},{8,9},{9,8},{10,11... | collective-permute-start | bytes 12582920 | tf_op jit(solution)/shard_map/ppermute | solution.py:271
  32.7 19.2 %collective-permute-start.3 = (bf16[2,4,128,1024]{3,2,1,0:T(8,128)(2,1)S(1)}, bf16[2,4,128,1024]{3,2,1,0:T(8,128)(2,1)S(1)}, u32[]{:S(2)}, u32[]{:S(2)}) collective-permute-start(bf16[2,4,128,1024]{3,2,1,0:T(8,128)(2,1)S(1)} %pack_core.1), channel_id=1, source_target_pairs={{0,1},{1,0},{2,3},{3,2},{4,5},{5,4},{6,7},{7,6},{8,9},{9,8},{10,11... | collective-permute-start | bytes 6291464 | tf_op jit(solution)/shard_map/ppermute | solution.py:271
  33.2 25.2 %collective-permute-start.6 = (bf16[4,128,1024]{2,1,0:T(8,128)(2,1)S(1)}, bf16[4,128,1024]{2,1,0:T(8,128)(2,1)S(1)}, u32[]{:S(2)}, u32[]{:S(2)}) collective-permute-start(bf16[4,128,1024]{2,1,0:T(8,128)(2,1)S(1)} %pack_factors.4), channel_id=1, source_target_pairs={{0,3},{1,2},{2,1},{3,0},{4,7},{5,6},{6,5},{7,4},{8,11},{9,10},{10,... | collective-permute-start | bytes 3145736 | tf_op jit(solution)/shard_map/ppermute | solution.py:271
  33.6 16.2 %collective-permute-start.4 = (bf16[2,128,1024]{2,1,0:T(8,128)(2,1)S(1)}, bf16[2,128,1024]{2,1,0:T(8,128)(2,1)S(1)}, u32[]{:S(2)}, u32[]{:S(2)}) collective-permute-start(bf16[2,128,1024]{2,1,0:T(8,128)(2,1)S(1)} %get-tuple-element.122), channel_id=1, source_target_pairs={{4,0},{5,1},{6,2},{7,3},{8,12},{9,13},{10,14},{11,15},{20,16},{21,... | collective-permute-start | bytes 1572872 | tf_op jit(solution)/shard_map/ppermute | solution.py:278
  34.9 14.9 %collective-permute-start.5 = (bf16[2,128,1024]{2,1,0:T(8,128)(2,1)S(1)}, bf16[2,128,1024]{2,1,0:T(8,128)(2,1)S(1)}, u32[]{:S(2)}, u32[]{:S(2)}) collective-permute-start(bf16[2,128,1024]{2,1,0:T(8,128)(2,1)S(1)} %get-tuple-element.120), channel_id=1, source_target_pairs={{4,8},{5,9},{6,10},{7,11},{8,4},{9,5},{10,6},{11,7},{20,24},{21,25... | collective-permute-start | bytes 1572872 | tf_op jit(solution)/shard_map/ppermute | solution.py:278
  49.7 17.8 %collective-permute-start.7 = (bf16[2,128,1024]{2,1,0:T(8,128)(2,1)S(1)}, bf16[2,128,1024]{2,1,0:T(8,128)(2,1)S(1)}, u32[]{:S(2)}, u32[]{:S(2)}) collective-permute-start(bf16[2,128,1024]{2,1,0:T(8,128)(2,1)S(1)} %collective-permute-done.5.refs_4_), channel_id=1, source_target_pairs={{4,0},{5,1},{6,2},{7,3},{8,12},{9,13},{10,14},{11,15},{20,16},{21,... | collective-permute-start | bytes 1572872 | tf_op jit(solution)/shard_map/ppermute | solution.py:278
  51.0 17.5 %collective-permute-start.13 = (bf16[2,128,1024]{2,1,0:T(8,128)(2,1)S(1)}, bf16[2,128,1024]{2,1,0:T(8,128)(2,1)S(1)}, u32[]{:S(2)}, u32[]{:S(2)}) collective-permute-start(bf16[2,128,1024]{2,1,0:T(8,128)(2,1)S(1)} %get-tuple-element.84), channel_id=1, source_target_pairs={{4,8},{5,9},{6,10},{7,11},{8,4},{9,5},{10,6},{11,7},{20,24},{21,25... | collective-permute-start | bytes 1572872 | tf_op jit(solution)/shard_map/ppermute | solution.py:278
  52.0 26.8 %collective-permute-start.11 = (bf16[2,128,1024]{2,1,0:T(8,128)(2,1)S(1)}, bf16[2,128,1024]{2,1,0:T(8,128)(2,1)S(1)}, u32[]{:S(2)}, u32[]{:S(2)}) collective-permute-start(bf16[2,128,1024]{2,1,0:T(8,128)(2,1)S(1)} %get-tuple-element.75), channel_id=1, source_target_pairs={{4,0},{5,1},{6,2},{7,3},{8,12},{9,13},{10,14},{11,15},{20,16},{21,... | collective-permute-start | bytes 1572872 | tf_op jit(solution)/shard_map/ppermute | solution.py:278
  60.9 14.0 %copy-start = (bf16[8,16,8192]{2,1,0:T(8,128)(2,1)S(1)}, bf16[8,16,8192]{2,1,0:T(8,128)(2,1)}, u32[]{:S(2)}) copy-start(bf16[8,16,8192]{2,1,0:T(8,128)(2,1)} %param.9) | copy-start | bytes 6291460
  68.6 20.0 %collective-permute-start.14 = (bf16[2,128,1024]{2,1,0:T(8,128)(2,1)S(1)}, bf16[2,128,1024]{2,1,0:T(8,128)(2,1)S(1)}, u32[]{:S(2)}, u32[]{:S(2)}) collective-permute-start(bf16[2,128,1024]{2,1,0:T(8,128)(2,1)S(1)} %collective-permute-done.13.refs_4_), channel_id=1, source_target_pairs={{4,0},{5,1},{6,2},{7,3},{8,12},{9,13},{10,14},{11,15},{20,16},{21,... | collective-permute-start | bytes 1572872 | tf_op jit(solution)/shard_map/ppermute | solution.py:278
  69.9 1.2 collective-permute-start.8
  71.2 3.7 %collective-permute-start.9 = (f32[16,256]{1,0:T(8,128)S(1)}, f32[16,256]{1,0:T(8,128)S(1)}, u32[]{:S(2)}, u32[]{:S(2)}) collective-permute-start(f32[16,256]{1,0:T(8,128)S(1)} %add.82), channel_id=1, source_target_pairs={{0,2},{1,3},{2,0},{3,1},{4,6},{5,7},{6,4},{7,5},{8,10},{9,11},{10,... | collective-permute-start | bytes 49160 | tf_op jit(solution)/shard_map/ppermute | solution.py:271
  76.0 16.6 %collective-permute-start.12 = (bf16[4,160,512]{2,1,0:T(8,128)(2,1)S(1)}, bf16[4,160,512]{2,1,0:T(8,128)(2,1)S(1)}, u32[]{:S(2)}, u32[]{:S(2)}) collective-permute-start(bf16[4,160,512]{2,1,0:T(8,128)(2,1)S(1)} %bitcast.59), channel_id=1, source_target_pairs={{0,2},{1,3},{2,0},{3,1},{4,6},{5,7},{6,4},{7,5},{8,10},{9,11},{10,... | collective-permute-start | bytes 1966088 | tf_op jit(solution)/shard_map/ppermute | solution.py:271
  88.6 10.9 %collective-permute-start.18 = (bf16[2,2,96,512]{3,2,1,0:T(8,128)(2,1)S(1)}, bf16[2,2,96,512]{3,2,1,0:T(8,128)(2,1)S(1)}, u32[]{:S(2)}, u32[]{:S(2)}) collective-permute-start(bf16[2,2,96,512]{3,2,1,0:T(8,128)(2,1)S(1)} %get-tuple-element.90), channel_id=1, source_target_pairs={{0,4},{1,5},{2,6},{3,7},{4,0},{5,1},{6,2},{7,3},{8,12},{9,13},{10,... | collective-permute-start | bytes 1179656 | tf_op jit(solution)/shard_map/ppermute | solution.py:274
  89.8 1.2 collective-permute-start.15
  91.1 3.7 %collective-permute-start.17 = (f32[16,256]{1,0:T(8,128)S(1)}, f32[16,256]{1,0:T(8,128)S(1)}, u32[]{:S(2)}, u32[]{:S(2)}) collective-permute-start(f32[16,256]{1,0:T(8,128)S(1)} %add.86), channel_id=1, source_target_pairs={{0,2},{1,3},{2,0},{3,1},{4,6},{5,7},{6,4},{7,5},{8,10},{9,11},{10,... | collective-permute-start | bytes 49160 | tf_op jit(solution)/shard_map/ppermute | solution.py:271
  94.8 11.5 %collective-permute-start.16 = (bf16[2,160,512]{2,1,0:T(8,128)(2,1)S(1)}, bf16[2,160,512]{2,1,0:T(8,128)(2,1)S(1)}, u32[]{:S(2)}, u32[]{:S(2)}) collective-permute-start(bf16[2,160,512]{2,1,0:T(8,128)(2,1)S(1)} %slice.192), channel_id=1, source_target_pairs={{0,4},{1,5},{2,6},{3,7},{4,0},{5,1},{6,2},{7,3},{8,12},{9,13},{10,... | collective-permute-start | bytes 983048 | tf_op jit(solution)/shard_map/ppermute | solution.py:274
  99.5 14.9 %collective-permute-start.23 = (bf16[4,128,512]{2,1,0:T(8,128)(2,1)S(1)}, bf16[4,128,512]{2,1,0:T(8,128)(2,1)S(1)}, u32[]{:S(2)}, u32[]{:S(2)}) collective-permute-start(bf16[4,128,512]{2,1,0:T(8,128)(2,1)S(1)} %bitcast.60), channel_id=1, source_target_pairs={{0,2},{1,3},{2,0},{3,1},{4,6},{5,7},{6,4},{7,5},{8,10},{9,11},{10,... | collective-permute-start | bytes 1572872 | tf_op jit(solution)/shard_map/ppermute | solution.py:271
  101.2 17.4 %collective-permute-start.22 = (bf16[2,96,512]{2,1,0:T(8,128)(2,1)S(1)}, bf16[2,96,512]{2,1,0:T(8,128)(2,1)S(1)}, u32[]{:S(2)}, u32[]{:S(2)}) collective-permute-start(bf16[2,96,512]{2,1,0:T(8,128)(2,1)S(1)} %fusion.2), channel_id=1, source_target_pairs={{0,2},{1,3},{2,0},{3,1},{4,6},{5,7},{6,4},{7,5},{8,10},{9,11},{10,... | collective-permute-start | bytes 589832 | tf_op jit(solution)/shard_map/ppermute | solution.py:271
  103.4 18.7 %collective-permute-start.20 = (bf16[4,64,512]{2,1,0:T(8,128)(2,1)S(1)}, bf16[4,64,512]{2,1,0:T(8,128)(2,1)S(1)}, u32[]{:S(2)}, u32[]{:S(2)}) collective-permute-start(bf16[4,64,512]{2,1,0:T(8,128)(2,1)S(1)} %bitcast.64), channel_id=1, source_target_pairs={{0,2},{1,3},{2,0},{3,1},{4,6},{5,7},{6,4},{7,5},{8,10},{9,11},{10,... | collective-permute-start | bytes 786440 | tf_op jit(solution)/shard_map/ppermute | solution.py:271
  105.0 13.8 %collective-permute-start.21 = (bf16[2,2,64,512]{3,2,1,0:T(8,128)(2,1)S(1)}, bf16[2,2,64,512]{3,2,1,0:T(8,128)(2,1)S(1)}, u32[]{:S(2)}, u32[]{:S(2)}) collective-permute-start(bf16[2,2,64,512]{3,2,1,0:T(8,128)(2,1)S(1)} %get-tuple-element.97), channel_id=1, source_target_pairs={{0,4},{1,5},{2,6},{3,7},{4,0},{5,1},{6,2},{7,3},{8,12},{9,13},{10,... | collective-permute-start | bytes 786440 | tf_op jit(solution)/shard_map/ppermute | solution.py:274
  106.5 23.1 %collective-permute-start.19 = (bf16[1,160,512]{2,1,0:T(8,128)(2,1)S(1)}, bf16[1,160,512]{2,1,0:T(8,128)(2,1)S(1)}, u32[]{:S(2)}, u32[]{:S(2)}) collective-permute-start(bf16[1,160,512]{2,1,0:T(8,128)(2,1)S(1)} %slice.194), channel_id=1, source_target_pairs={{0,8},{1,9},{2,10},{3,11},{4,12},{5,13},{6,14},{7,15},{8,0},{9,1},... | collective-permute-start | bytes 491528 | tf_op jit(solution)/shard_map/ppermute | solution.py:274
  114.6 8.0 %collective-permute-start.26 = (bf16[2,128,512]{2,1,0:T(8,128)(2,1)S(1)}, bf16[2,128,512]{2,1,0:T(8,128)(2,1)S(1)}, u32[]{:S(2)}, u32[]{:S(2)}) collective-permute-start(bf16[2,128,512]{2,1,0:T(8,128)(2,1)S(1)} %slice.193), channel_id=1, source_target_pairs={{0,4},{1,5},{2,6},{3,7},{4,0},{5,1},{6,2},{7,3},{8,12},{9,13},{10,... | collective-permute-start | bytes 786440 | tf_op jit(solution)/shard_map/ppermute | solution.py:274
  118.7 11.0 %collective-permute-start.27 = (bf16[1,96,512]{2,1,0:T(8,128)(2,1)S(1)}, bf16[1,96,512]{2,1,0:T(8,128)(2,1)S(1)}, u32[]{:S(2)}, u32[]{:S(2)}) collective-permute-start(bf16[1,96,512]{2,1,0:T(8,128)(2,1)S(1)} %slice.197), channel_id=1, source_target_pairs={{0,8},{1,9},{2,10},{3,11},{4,12},{5,13},{6,14},{7,15},{8,0},{9,1},... | collective-permute-start | bytes 294920 | tf_op jit(solution)/shard_map/ppermute | solution.py:274
  118.9 5.5 %collective-permute-start.25 = (bf16[2,64,512]{2,1,0:T(8,128)(2,1)S(1)}, bf16[2,64,512]{2,1,0:T(8,128)(2,1)S(1)}, u32[]{:S(2)}, u32[]{:S(2)}) collective-permute-start(bf16[2,64,512]{2,1,0:T(8,128)(2,1)S(1)} %fusion.3), channel_id=1, source_target_pairs={{0,2},{1,3},{2,0},{3,1},{4,6},{5,7},{6,4},{7,5},{8,10},{9,11},{10,... | collective-permute-start | bytes 393224 | tf_op jit(solution)/shard_map/ppermute | solution.py:271
  122.2 7.3 %collective-permute-start.24 = (bf16[2,64,512]{2,1,0:T(8,128)(2,1)S(1)}, bf16[2,64,512]{2,1,0:T(8,128)(2,1)S(1)}, u32[]{:S(2)}, u32[]{:S(2)}) collective-permute-start(bf16[2,64,512]{2,1,0:T(8,128)(2,1)S(1)} %slice.196), channel_id=1, source_target_pairs={{0,4},{1,5},{2,6},{3,7},{4,0},{5,1},{6,2},{7,3},{8,12},{9,13},{10,... | collective-permute-start | bytes 393224 | tf_op jit(solution)/shard_map/ppermute | solution.py:274
  122.6 11.3 %collective-permute-start.28 = (bf16[1,128,512]{2,1,0:T(8,128)(2,1)S(1)}, bf16[1,128,512]{2,1,0:T(8,128)(2,1)S(1)}, u32[]{:S(2)}, u32[]{:S(2)}) collective-permute-start(bf16[1,128,512]{2,1,0:T(8,128)(2,1)S(1)} %slice.195), channel_id=1, source_target_pairs={{0,8},{1,9},{2,10},{3,11},{4,12},{5,13},{6,14},{7,15},{8,0},{9,1},... | collective-permute-start | bytes 393224 | tf_op jit(solution)/shard_map/ppermute | solution.py:274
  124.4 10.5 %collective-permute-start.29 = (bf16[1,64,512]{2,1,0:T(8,128)(2,1)S(1)}, bf16[1,64,512]{2,1,0:T(8,128)(2,1)S(1)}, u32[]{:S(2)}, u32[]{:S(2)}) collective-permute-start(bf16[1,64,512]{2,1,0:T(8,128)(2,1)S(1)} %slice.199), channel_id=1, source_target_pairs={{0,8},{1,9},{2,10},{3,11},{4,12},{5,13},{6,14},{7,15},{8,0},{9,1},... | collective-permute-start | bytes 196616 | tf_op jit(solution)/shard_map/ppermute | solution.py:274
  129.5 6.1 %collective-permute-start.30 = (bf16[1,64,512]{2,1,0:T(8,128)(2,1)S(1)}, bf16[1,64,512]{2,1,0:T(8,128)(2,1)S(1)}, u32[]{:S(2)}, u32[]{:S(2)}) collective-permute-start(bf16[1,64,512]{2,1,0:T(8,128)(2,1)S(1)} %slice.198), channel_id=1, source_target_pairs={{0,8},{1,9},{2,10},{3,11},{4,12},{5,13},{6,14},{7,15},{8,0},{9,1},... | collective-permute-start | bytes 196616 | tf_op jit(solution)/shard_map/ppermute | solution.py:274
  135.6 0.8 copy-start.3

commit v6 on v5

--- a/solution.py
+++ b/solution.py
@@ -244,7 +244,7 @@
             jax.ShapeDtypeStruct(shape(*piece), BF16 if piece[0] in (SEND_Y, SEND_Z) else F32)
             for piece in pieces
         ],
-        cost_estimate=cost(4 * lanes * rows * planes * width, 10 * lanes * planes * width),
+        cost_estimate=cost(4 * lanes * rows * planes * width, 10 * lanes * planes * width, 1),
         compiler_params=params(10),
         name="add_extra",
     )(

time: 137 us -> 136 us (level)
  waiting for transfers between devices: 65.4 us -> 62.9 us
  starting transfers between devices: 32.8 us -> 34.9 us
    ppermute x13, waiting for transfers between devices: 22.9 us -> 17.9 us  [in_plane(): lax.ppermute(value, 'tensor', [(t, t ^ other) for t in range(devices)])]
    ppermute x11, waiting for transfers between devices: 13.4 us -> 15.8 us  [along(): lax.ppermute(value, 'tensor', [(t, t ^ other * PLANE) for t in range(devi...]
    ppermute x11, starting transfers between devices: 11.8 us -> 13.6 us  [along(): lax.ppermute(value, 'tensor', [(t, t ^ other * PLANE) for t in range(devi...]
  transfers between devices with their start and end apart: 31 -> 31, of which waited for: 19 -> 17; matrix products, arithmetic and copies ran while one was open for 1% -> 1% of each run, Pallas kernels for 24% -> 24%
where the time goes in v6:
time: 136 us
  waiting for transfers between devices  62.9 us (46%)
  Pallas kernels  35.1 us (26%)
  starting transfers between devices  34.9 us (26%)
  other arithmetic  1.4 us (1%)
    ppermute x7, waiting for transfers between devices, hop(): return lax.ppermute(value, 'tensor', pairs)  29.1 us
    ppermute x13, waiting for transfers between devices, in_plane(): lax.ppermute(value, 'tensor', [(t, t ^ other) for t in range(devices)])  17.9 us
    ppermute x11, waiting for transfers between devices, along(): lax.ppermute(value, 'tensor', [(t, t ^ other * PLANE) for t in range(devi...  15.8 us
    ppermute x13, starting transfers between devices, in_plane(): lax.ppermute(value, 'tensor', [(t, t ^ other) for t in range(devices)])  14.1 us
    pallas_call x1, Pallas kernels, base_blocks(): pl.pallas_call(body, grid_spec=pltpu.PrefetchScalarGridSpec(num_scalar_pr...  13.9 us
    ppermute x11, starting transfers between devices, along(): lax.ppermute(value, 'tensor', [(t, t ^ other * PLANE) for t in range(devi...  13.6 us
    pallas_call x6, Pallas kernels, low_part(): pl.pallas_call(body, grid_spec=pltpu.PrefetchScalarGridSpec(num_scalar_pr...  7.34 us
    ppermute x7, starting transfers between devices, hop(): return lax.ppermute(value, 'tensor', pairs)  7.26 us
  transfers between devices with their start and end apart: 31, of which 17 were waited for; matrix products, arithmetic and copies ran while one was open for 1% of the time, Pallas kernels for 24%

profile of v6, /device:TPU:0, one launch (start us, length us, event | category | flops | bytes accessed | tf_op | source)
XLA Modules:
  0.0 135.9 jit_solution(1029135183288112234)
XLA Ops:
  0.2 1.8 %pack_factors.3 = bf16[4,128,1024]{2,1,0:T(8,128)(2,1)S(1)} custom-call(s32[3]{0:T(128)S(1)} %pad_add_fusion.place_ref, s32[4]{0:T(128)S(1)} %pad_add_fusion.1.order_ref, bf16[128,16384]{1,0:T(8,128)(2,1)} %bitcast.65, bf16[128,16384]{1,0:T(8,128)(2,1)} %bitcast.66, bf16[128,16384]{1,0:T(8,128)(2,1)} %bitcast.67, bf16[128,16384]{1,0:T(8,128)(2,1)} %bitcast.68), custom_call_target="tpu_custom_call" | custom-call | bytes 2097 | tf_op jit(solution)/shard_map/pack_factors/pallas_call | solution.py:52
  2.0 3.0 %collective-permute-start.2 = (bf16[4,128,1024]{2,1,0:T(8,128)(2,1)S(1)}, bf16[4,128,1024]{2,1,0:T(8,128)(2,1)S(1)}, u32[]{:S(2)}, u32[]{:S(2)}) collective-permute-start(bf16[4,128,1024]{2,1,0:T(8,128)(2,1)S(1)} %pack_factors.3), channel_id=1, source_target_pairs={{0,2},{1,3},{2,0},{3,1},{4,6},{5,7},{6,4},{7,5},{8,10},{9,11},{10,... | collective-permute-start | bytes 3145736 | tf_op jit(solution)/shard_map/ppermute | solution.py:271
  5.7 4.4 %collective-permute-start = (bf16[4,128,1024]{2,1,0:T(8,128)(2,1)S(1)}, bf16[4,128,1024]{2,1,0:T(8,128)(2,1)S(1)}, u32[]{:S(2)}, u32[]{:S(2)}) collective-permute-start(bf16[4,128,1024]{2,1,0:T(8,128)(2,1)S(1)} %copy-done.1), channel_id=1, source_target_pairs={{0,4},{1,5},{2,6},{3,7},{4,0},{5,1},{6,2},{7,3},{8,12},{9,13},{10,... | collective-permute-start | bytes 3145736 | tf_op jit(solution)/shard_map/ppermute | solution.py:274
  10.1 1.8 %pack_factors.4 = bf16[4,128,1024]{2,1,0:T(8,128)(2,1)S(1)} custom-call(s32[3]{0:T(128)S(1)} %pad_add_fusion.place_ref, s32[4]{0:T(128)S(1)} %pad_add_fusion.1.order_ref, bf16[128,16384]{1,0:T(8,128)(2,1)} %bitcast.69, bf16[128,16384]{1,0:T(8,128)(2,1)} %bitcast.70, bf16[128,16384]{1,0:T(8,128)(2,1)} %bitcast.71, bf16[128,16384]{1,0:T(8,128)(2,1)} %bitcast.72), custom_call_target="tpu_custom_call" | custom-call | bytes 2097 | tf_op jit(solution)/shard_map/pack_factors/pallas_call | solution.py:52
  11.9 1.8 %pack_factors.5.refs_0_ = bf16[4,128,1024]{2,1,0:T(8,128)(2,1)S(1)} custom-call(s32[3]{0:T(128)S(1)} %pad_add_fusion.place_ref, s32[4]{0:T(128)S(1)} %pad_add_fusion.1.order_ref, bf16[128,16384]{1,0:T(8,128)(2,1)} %bitcast.73, bf16[128,16384]{1,0:T(8,128)(2,1)} %bitcast.74, bf16[128,16384]{1,0:T(8,128)(2,1)} %bitcast.75, bf16[128,16384]{1,0:T(8,128)(2,1)} %bitcast.76), custom_call_target="tpu_custom_call" | custom-call | bytes 2097 | tf_op jit(solution)/shard_map/pack_factors/pallas_call | solution.py:52
  13.7 3.1 %pack_core.1 = bf16[2,4,128,1024]{3,2,1,0:T(8,128)(2,1)S(1)} custom-call(s32[3]{0:T(128)S(1)} %pad_add_fusion.place_ref, s32[4]{0:T(128)S(1)} %pad_add_fusion.1.order_ref, bf16[128,16384]{1,0:T(8,128)(2,1)} %bitcast.77, bf16[128,8192]{1,0:T(8,128)(2,1)} %bitcast.49, bf16[128,8192]{1,0:T(8,128)(2,1)} %bitcast.50), custom_call_target="tpu_custom_call" | custom-call | bytes 4194 | tf_op jit(solution)/shard_map/pack_core/pallas_call | solution.py:82
  16.9 13.9 %base_blocks.1 = (bf16[2,4,4,128,512]{4,3,2,1,0:T(8,128)(2,1)S(1)}, f32[2,4,4,128,512]{4,3,2,1,0:T(8,128)S(1)}) custom-call(s32[3]{0:T(128)S(1)} %pad_add_fusion.place_ref, bf16[4,128,1024]{2,1,0:T(8,128)(2,1)} %refs_1_.1, bf16[1024,8192]{1,0:T(8,128)(2,1)} %d3.1, bf16[1024,8192]{1,0:T(8,128)(2,1)} %d3.1, bf16[1024,8192]{1,0:T(8,128)(2,1)} %d3.1, ...), custom_call_target="tpu_custom_call" | custom-call | flops 8589934 | bytes 29360 | tf_op jit(solution)/shard_map/base_blocks/pallas_call | solution.py:114
  30.8 1.9 %collective-permute-done.refs_4_.refs_2_ = bf16[4,128,1024]{2,1,0:T(8,128)(2,1)S(1)} collective-permute-done((bf16[4,128,1024]{2,1,0:T(8,128)(2,1)S(1)}, bf16[4,128,1024]{2,1,0:T(8,128)(2,1)S(1)}, u32[]{:S(2)}, u32[]{:S(2)}) %collective-permute-start) | collective-permute-done | bytes 1048608 | tf_op jit(solution)/shard_map/ppermute | solution.py:274
  33.6 1.3 collective-permute-start.4
  35.6 14.2 %collective-permute-done.4.refs_5_ = bf16[2,128,1024]{2,1,0:T(8,128)(2,1)S(1)} collective-permute-done((bf16[2,128,1024]{2,1,0:T(8,128)(2,1)S(1)}, bf16[2,128,1024]{2,1,0:T(8,128)(2,1)S(1)}, u32[]{:S(2)}, u32[]{:S(2)}) %collective-permute-start.4) | collective-permute-done | bytes 524320 | tf_op jit(solution)/shard_map/ppermute | solution.py:278
  49.7 1.3 collective-permute-start.7
  52.0 1.3 collective-permute-start.11
  53.3 1.5 %low_part.6 = f32[16,512]{1,0:T(8,128)S(1)} custom-call(s32[3]{0:T(128)S(1)} %pad_add_fusion.place_ref, s32[1,512]{1,0:T(1,128)S(1)} %bitcast.62, bf16[4,128,1024]{2,1,0:T(8,128)(2,1)S(1)} %pack_factors.5.refs_0_, bf16[2,4,128,1024]{3,2,1,0:T(8,128)(2,1)S(1)} %collective-permute-done.3.refs_1_.t_ref, ...), custom_call_target="tpu_custom_call" | custom-call | flops 805306368 | bytes 3670016 | tf_op jit(solution)/shard_map/low_part/pallas_call | solution.py:175
  54.8 3.6 %collective-permute-done.6.refs_0_.refs_3_ = bf16[4,128,1024]{2,1,0:T(8,128)(2,1)S(1)} collective-permute-done((bf16[4,128,1024]{2,1,0:T(8,128)(2,1)S(1)}, bf16[4,128,1024]{2,1,0:T(8,128)(2,1)S(1)}, u32[]{:S(2)}, u32[]{:S(2)}) %collective-permute-start.6) | collective-permute-done | bytes 1048608 | tf_op jit(solution)/shard_map/ppermute | solution.py:271
  58.4 1.4 %low_part.7 = f32[16,512]{1,0:T(8,128)S(1)} custom-call(s32[3]{0:T(128)S(1)} %pad_add_fusion.place_ref, s32[1,512]{1,0:T(1,128)S(1)} %bitcast.63, bf16[4,128,1024]{2,1,0:T(8,128)(2,1)S(1)} %collective-permute-done.6.refs_0_.refs_3_, bf16[4,128,1024]{2,1,0:T(8,128)(2,1)S(1)} %copy-done.2, bf16[4,128,1024]{2,1,0:T(8,128)(2,1)S(1)} %collective-permute-done.refs_4_.refs_2_), custom_call_target="tpu_custom_call" | custom-call | flops 268435456 | bytes 2621440 | tf_op jit(solution)/shard_map/low_part/pallas_call | solution.py:175
  59.8 1.1 low_part.8
  60.9 6.6 %collective-permute-done.7.refs_5_ = bf16[2,128,1024]{2,1,0:T(8,128)(2,1)S(1)} collective-permute-done((bf16[2,128,1024]{2,1,0:T(8,128)(2,1)S(1)}, bf16[2,128,1024]{2,1,0:T(8,128)(2,1)S(1)}, u32[]{:S(2)}, u32[]{:S(2)}) %collective-permute-start.7) | collective-permute-done | bytes 524320 | tf_op jit(solution)/shard_map/ppermute | solution.py:278
  67.5 1.1 low_part.9
  68.6 1.3 collective-permute-start.14
  70.0 1.2 collective-permute-done.8
  71.2 1.5 %collective-permute-start.9 = (f32[16,256]{1,0:T(8,128)S(1)}, f32[16,256]{1,0:T(8,128)S(1)}, u32[]{:S(2)}, u32[]{:S(2)}) collective-permute-start(f32[16,256]{1,0:T(8,128)S(1)} %add.82), channel_id=1, source_target_pairs={{0,2},{1,3},{2,0},{3,1},{4,6},{5,7},{6,4},{7,5},{8,10},{9,11},{10,... | collective-permute-start | bytes 49160 | tf_op jit(solution)/shard_map/ppermute | solution.py:271
  72.7 2.2 %collective-permute-done.9 = f32[16,256]{1,0:T(8,128)S(1)} collective-permute-done((f32[16,256]{1,0:T(8,128)S(1)}, f32[16,256]{1,0:T(8,128)S(1)}, u32[]{:S(2)}, u32[]{:S(2)}) %collective-permute-start.9) | collective-permute-done | bytes 16416 | tf_op jit(solution)/shard_map/ppermute | solution.py:271
  74.9 1.1 add_extra.4
  76.0 1.6 %collective-permute-start.12 = (bf16[4,160,512]{2,1,0:T(8,128)(2,1)S(1)}, bf16[4,160,512]{2,1,0:T(8,128)(2,1)S(1)}, u32[]{:S(2)}, u32[]{:S(2)}) collective-permute-start(bf16[4,160,512]{2,1,0:T(8,128)(2,1)S(1)} %bitcast.59), channel_id=1, source_target_pairs={{0,2},{1,3},{2,0},{3,1},{4,6},{5,7},{6,4},{7,5},{8,10},{9,11},{10,... | collective-permute-start | bytes 1966088 | tf_op jit(solution)/shard_map/ppermute | solution.py:271
  77.6 1.1 collective-permute-done.11.refs_5_
  78.7 1.5 %add_extra.5 = (f32[1,4,160,512]{3,2,1,0:T(8,128)S(1)}, bf16[2,2,96,512]{3,2,1,0:T(8,128)(2,1)S(1)}, f32[2,2,96,512]{3,2,1,0:T(8,128)S(1)}) custom-call(s32[3]{0:T(128)S(1)} %pad_add_fusion.place_ref, f32[16,256]{1,0:T(8,128)S(1)} %add.83.low_ref, s32[1,256]{1,0:T(1,128)S(1)} %get-tuple-element.124.slots_ref, bf16[128,8192]{1,0:T(8,128)(2,1)S(1)} %bitcast.52, ...), custom_call_target="tpu_custom_call" | custom-call | flops 268435456 | bytes 5242880 | tf_op jit(solution)/shard_map/add_extra/pallas_call | solution.py:235
  80.3 1.1 low_part.10
  81.4 7.2 %collective-permute-done.14.refs_5_ = bf16[2,128,1024]{2,1,0:T(8,128)(2,1)S(1)} collective-permute-done((bf16[2,128,1024]{2,1,0:T(8,128)(2,1)S(1)}, bf16[2,128,1024]{2,1,0:T(8,128)(2,1)S(1)}, u32[]{:S(2)}, u32[]{:S(2)}) %collective-permute-start.14) | collective-permute-done | bytes 524320 | tf_op jit(solution)/shard_map/ppermute | solution.py:278
  88.6 1.2 low_part.11
  89.9 1.2 collective-permute-done.15
  91.1 1.5 %collective-permute-start.17 = (f32[16,256]{1,0:T(8,128)S(1)}, f32[16,256]{1,0:T(8,128)S(1)}, u32[]{:S(2)}, u32[]{:S(2)}) collective-permute-start(f32[16,256]{1,0:T(8,128)S(1)} %add.86), channel_id=1, source_target_pairs={{0,2},{1,3},{2,0},{3,1},{4,6},{5,7},{6,4},{7,5},{8,10},{9,11},{10,... | collective-permute-start | bytes 49160 | tf_op jit(solution)/shard_map/ppermute | solution.py:271
  92.9 2.1 %collective-permute-start.16 = (bf16[2,160,512]{2,1,0:T(8,128)(2,1)S(1)}, bf16[2,160,512]{2,1,0:T(8,128)(2,1)S(1)}, u32[]{:S(2)}, u32[]{:S(2)}) collective-permute-start(bf16[2,160,512]{2,1,0:T(8,128)(2,1)S(1)} %slice.192), channel_id=1, source_target_pairs={{0,4},{1,5},{2,6},{3,7},{4,0},{5,1},{6,2},{7,3},{8,12},{9,13},{10,... | collective-permute-start | bytes 983048 | tf_op jit(solution)/shard_map/ppermute | solution.py:274
  95.0 1.0 add_extra.6
  96.0 4.6 %collective-permute-done.18 = bf16[2,2,96,512]{3,2,1,0:T(8,128)(2,1)S(1)} collective-permute-done((bf16[2,2,96,512]{3,2,1,0:T(8,128)(2,1)S(1)}, bf16[2,2,96,512]{3,2,1,0:T(8,128)(2,1)S(1)}, u32[]{:S(2)}, u32[]{:S(2)}) %collective-permute-start.18) | collective-permute-done | bytes 393248 | tf_op jit(solution)/shard_map/ppermute | solution.py:274
  100.7 1.6 %collective-permute-start.23 = (bf16[4,128,512]{2,1,0:T(8,128)(2,1)S(1)}, bf16[4,128,512]{2,1,0:T(8,128)(2,1)S(1)}, u32[]{:S(2)}, u32[]{:S(2)}) collective-permute-start(bf16[4,128,512]{2,1,0:T(8,128)(2,1)S(1)} %bitcast.60), channel_id=1, source_target_pairs={{0,2},{1,3},{2,0},{3,1},{4,6},{5,7},{6,4},{7,5},{8,10},{9,11},{10,... | collective-permute-start | bytes 1572872 | tf_op jit(solution)/shard_map/ppermute | solution.py:271
  102.9 1.6 %add_extra.7 = (f32[1,4,128,512]{3,2,1,0:T(8,128)S(1)}, bf16[2,2,64,512]{3,2,1,0:T(8,128)(2,1)S(1)}, f32[2,2,64,512]{3,2,1,0:T(8,128)S(1)}, bf16[1,4,64,512]{3,2,1,0:T(8,128)(2,1)S(1)}, f32[1,4,64,512]{3,2,1,0:T(8,128)S(1)}) custom-call(s32[3]{0:T(128)S(1)} %pad_add_fusion.place_ref, f32[16,256]{1,0:T(8,128)S(1)} %add.88.low_ref, ...), custom_call_target="tpu_custom_call" | custom-call | flops 268435456 | bytes 5242880 | tf_op jit(solution)/shard_map/add_extra/pallas_call | solution.py:235
  104.6 1.6 %collective-permute-start.20 = (bf16[4,64,512]{2,1,0:T(8,128)(2,1)S(1)}, bf16[4,64,512]{2,1,0:T(8,128)(2,1)S(1)}, u32[]{:S(2)}, u32[]{:S(2)}) collective-permute-start(bf16[4,64,512]{2,1,0:T(8,128)(2,1)S(1)} %bitcast.64), channel_id=1, source_target_pairs={{0,2},{1,3},{2,0},{3,1},{4,6},{5,7},{6,4},{7,5},{8,10},{9,11},{10,... | collective-permute-start | bytes 786440 | tf_op jit(solution)/shard_map/ppermute | solution.py:271
  106.2 2.1 %collective-permute-done.16 = bf16[2,160,512]{2,1,0:T(8,128)(2,1)S(1)} collective-permute-done((bf16[2,160,512]{2,1,0:T(8,128)(2,1)S(1)}, bf16[2,160,512]{2,1,0:T(8,128)(2,1)S(1)}, u32[]{:S(2)}, u32[]{:S(2)}) %collective-permute-start.16) | collective-permute-done | bytes 327712 | tf_op jit(solution)/shard_map/ppermute | solution.py:274
  108.5 7.2 %collective-permute-done.23 = bf16[4,128,512]{2,1,0:T(8,128)(2,1)S(1)} collective-permute-done((bf16[4,128,512]{2,1,0:T(8,128)(2,1)S(1)}, bf16[4,128,512]{2,1,0:T(8,128)(2,1)S(1)}, u32[]{:S(2)}, u32[]{:S(2)}) %collective-permute-start.23) | collective-permute-done | bytes 524320 | tf_op jit(solution)/shard_map/ppermute | solution.py:271
  116.0 2.6 %collective-permute-done.22 = bf16[2,96,512]{2,1,0:T(8,128)(2,1)S(1)} collective-permute-done((bf16[2,96,512]{2,1,0:T(8,128)(2,1)S(1)}, bf16[2,96,512]{2,1,0:T(8,128)(2,1)S(1)}, u32[]{:S(2)}, u32[]{:S(2)}) %collective-permute-start.22) | collective-permute-done | bytes 196640 | tf_op jit(solution)/shard_map/ppermute | solution.py:271
  118.6 0.9 collective-permute-start.27
  119.6 1.8 %collective-permute-start.25 = (bf16[2,64,512]{2,1,0:T(8,128)(2,1)S(1)}, bf16[2,64,512]{2,1,0:T(8,128)(2,1)S(1)}, u32[]{:S(2)}, u32[]{:S(2)}) collective-permute-start(bf16[2,64,512]{2,1,0:T(8,128)(2,1)S(1)} %fusion.3), channel_id=1, source_target_pairs={{0,2},{1,3},{2,0},{3,1},{4,6},{5,7},{6,4},{7,5},{8,10},{9,11},{10,... | collective-permute-start | bytes 393224 | tf_op jit(solution)/shard_map/ppermute | solution.py:271
  121.5 1.1 collective-permute-start.24
  123.6 1.2 collective-permute-start.28
  124.9 2.0 %collective-permute-start.29 = (bf16[1,64,512]{2,1,0:T(8,128)(2,1)S(1)}, bf16[1,64,512]{2,1,0:T(8,128)(2,1)S(1)}, u32[]{:S(2)}, u32[]{:S(2)}) collective-permute-start(bf16[1,64,512]{2,1,0:T(8,128)(2,1)S(1)} %slice.199), channel_id=1, source_target_pairs={{0,8},{1,9},{2,10},{3,11},{4,12},{5,13},{6,14},{7,15},{8,0},{9,1},... | collective-permute-start | bytes 196616 | tf_op jit(solution)/shard_map/ppermute | solution.py:274
  126.9 1.7 %collective-permute-start.30 = (bf16[1,64,512]{2,1,0:T(8,128)(2,1)S(1)}, bf16[1,64,512]{2,1,0:T(8,128)(2,1)S(1)}, u32[]{:S(2)}, u32[]{:S(2)}) collective-permute-start(bf16[1,64,512]{2,1,0:T(8,128)(2,1)S(1)} %slice.198), channel_id=1, source_target_pairs={{0,8},{1,9},{2,10},{3,11},{4,12},{5,13},{6,14},{7,15},{8,0},{9,1},... | collective-permute-start | bytes 196616 | tf_op jit(solution)/shard_map/ppermute | solution.py:274
  128.7 4.3 %collective-permute-done.28 = bf16[1,128,512]{2,1,0:T(8,128)(2,1)S(1)} collective-permute-done((bf16[1,128,512]{2,1,0:T(8,128)(2,1)S(1)}, bf16[1,128,512]{2,1,0:T(8,128)(2,1)S(1)}, u32[]{:S(2)}, u32[]{:S(2)}) %collective-permute-start.28) | collective-permute-done | bytes 131104 | tf_op jit(solution)/shard_map/ppermute | solution.py:274
  133.0 1.4 %collective-permute-done.29 = bf16[1,64,512]{2,1,0:T(8,128)(2,1)S(1)} collective-permute-done((bf16[1,64,512]{2,1,0:T(8,128)(2,1)S(1)}, bf16[1,64,512]{2,1,0:T(8,128)(2,1)S(1)}, u32[]{:S(2)}, u32[]{:S(2)}) %collective-permute-start.29) | collective-permute-done | bytes 65568 | tf_op jit(solution)/shard_map/ppermute | solution.py:274
  (80 shorter events, 7.8 us)
Async XLA Ops:
  0.2 4.8 %copy-start.1 = (bf16[4,128,1024]{2,1,0:T(8,128)(2,1)S(1)}, bf16[4,128,1024]{2,1,0:T(8,128)(2,1)}, u32[]{:S(2)}) copy-start(bf16[4,128,1024]{2,1,0:T(8,128)(2,1)} %refs_1_.1) | copy-start | bytes 3145732
  2.0 28.8 %collective-permute-start.2 = (bf16[4,128,1024]{2,1,0:T(8,128)(2,1)S(1)}, bf16[4,128,1024]{2,1,0:T(8,128)(2,1)S(1)}, u32[]{:S(2)}, u32[]{:S(2)}) collective-permute-start(bf16[4,128,1024]{2,1,0:T(8,128)(2,1)S(1)} %pack_factors.3), channel_id=1, source_target_pairs={{0,2},{1,3},{2,0},{3,1},{4,6},{5,7},{6,4},{7,5},{8,10},{9,11},{10,... | collective-permute-start | bytes 3145736 | tf_op jit(solution)/shard_map/ppermute | solution.py:271
  5.0 25.8 %collective-permute-start.1 = (bf16[4,128,1024]{2,1,0:T(8,128)(2,1)S(1)}, bf16[4,128,1024]{2,1,0:T(8,128)(2,1)S(1)}, u32[]{:S(2)}, u32[]{:S(2)}) collective-permute-start(bf16[4,128,1024]{2,1,0:T(8,128)(2,1)S(1)} %copy-done.1), channel_id=1, source_target_pairs={{4,8},{5,9},{6,10},{7,11},{8,4},{9,5},{10,6},{11,7},{20,24},{21,25... | collective-permute-start | bytes 3145736 | tf_op jit(solution)/shard_map/ppermute | solution.py:278
  5.7 27.0 %collective-permute-start = (bf16[4,128,1024]{2,1,0:T(8,128)(2,1)S(1)}, bf16[4,128,1024]{2,1,0:T(8,128)(2,1)S(1)}, u32[]{:S(2)}, u32[]{:S(2)}) collective-permute-start(bf16[4,128,1024]{2,1,0:T(8,128)(2,1)S(1)} %copy-done.1), channel_id=1, source_target_pairs={{0,4},{1,5},{2,6},{3,7},{4,0},{5,1},{6,2},{7,3},{8,12},{9,13},{10,... | collective-permute-start | bytes 3145736 | tf_op jit(solution)/shard_map/ppermute | solution.py:274
  32.7 19.0 %copy-start.4 = (s32[128]{0:T(128)S(1)}, s32[128]{0:T(128)}, u32[]{:S(2)}) copy-start(s32[128]{0:T(128)} %param.10) | copy-start | bytes 1540
  32.7 19.0 %copy-start.5 = (s32[128]{0:T(128)S(1)}, s32[128]{0:T(128)}, u32[]{:S(2)}) copy-start(s32[128]{0:T(128)} %param.11) | copy-start | bytes 1540
  32.7 20.5 %copy-start.2 = (bf16[4,128,1024]{2,1,0:T(8,128)(2,1)S(1)}, bf16[4,128,1024]{2,1,0:T(8,128)(2,1)}, u32[]{:S(2)}) copy-start(bf16[4,128,1024]{2,1,0:T(8,128)(2,1)} %refs_1_.1) | copy-start | bytes 3145732
  32.7 42.2 %collective-permute-start.10 = (bf16[2,4,4,128,512]{4,3,2,1,0:T(8,128)(2,1)S(1)}, bf16[2,4,4,128,512]{4,3,2,1,0:T(8,128)(2,1)S(1)}, u32[]{:S(2)}, u32[]{:S(2)}) collective-permute-start(bf16[2,4,4,128,512]{4,3,2,1,0:T(8,128)(2,1)S(1)} %get-tuple-element.74), channel_id=1, source_target_pairs={{0,1},{1,0},{2,3},{3,2},{4,5},{5,4},{6,7},{7,6},{8,9},{9,8},{10,11... | collective-permute-start | bytes 12582920 | tf_op jit(solution)/shard_map/ppermute | solution.py:271
  32.7 19.2 %collective-permute-start.3 = (bf16[2,4,128,1024]{3,2,1,0:T(8,128)(2,1)S(1)}, bf16[2,4,128,1024]{3,2,1,0:T(8,128)(2,1)S(1)}, u32[]{:S(2)}, u32[]{:S(2)}) collective-permute-start(bf16[2,4,128,1024]{3,2,1,0:T(8,128)(2,1)S(1)} %pack_core.1), channel_id=1, source_target_pairs={{0,1},{1,0},{2,3},{3,2},{4,5},{5,4},{6,7},{7,6},{8,9},{9,8},{10,11... | collective-permute-start | bytes 6291464 | tf_op jit(solution)/shard_map/ppermute | solution.py:271
  33.2 25.2 %collective-permute-start.6 = (bf16[4,128,1024]{2,1,0:T(8,128)(2,1)S(1)}, bf16[4,128,1024]{2,1,0:T(8,128)(2,1)S(1)}, u32[]{:S(2)}, u32[]{:S(2)}) collective-permute-start(bf16[4,128,1024]{2,1,0:T(8,128)(2,1)S(1)} %pack_factors.4), channel_id=1, source_target_pairs={{0,3},{1,2},{2,1},{3,0},{4,7},{5,6},{6,5},{7,4},{8,11},{9,10},{10,... | collective-permute-start | bytes 3145736 | tf_op jit(solution)/shard_map/ppermute | solution.py:271
  33.6 16.2 %collective-permute-start.4 = (bf16[2,128,1024]{2,1,0:T(8,128)(2,1)S(1)}, bf16[2,128,1024]{2,1,0:T(8,128)(2,1)S(1)}, u32[]{:S(2)}, u32[]{:S(2)}) collective-permute-start(bf16[2,128,1024]{2,1,0:T(8,128)(2,1)S(1)} %get-tuple-element.122), channel_id=1, source_target_pairs={{4,0},{5,1},{6,2},{7,3},{8,12},{9,13},{10,14},{11,15},{20,16},{21,... | collective-permute-start | bytes 1572872 | tf_op jit(solution)/shard_map/ppermute | solution.py:278
  34.9 14.9 %collective-permute-start.5 = (bf16[2,128,1024]{2,1,0:T(8,128)(2,1)S(1)}, bf16[2,128,1024]{2,1,0:T(8,128)(2,1)S(1)}, u32[]{:S(2)}, u32[]{:S(2)}) collective-permute-start(bf16[2,128,1024]{2,1,0:T(8,128)(2,1)S(1)} %get-tuple-element.120), channel_id=1, source_target_pairs={{4,8},{5,9},{6,10},{7,11},{8,4},{9,5},{10,6},{11,7},{20,24},{21,25... | collective-permute-start | bytes 1572872 | tf_op jit(solution)/shard_map/ppermute | solution.py:278
  49.7 17.8 %collective-permute-start.7 = (bf16[2,128,1024]{2,1,0:T(8,128)(2,1)S(1)}, bf16[2,128,1024]{2,1,0:T(8,128)(2,1)S(1)}, u32[]{:S(2)}, u32[]{:S(2)}) collective-permute-start(bf16[2,128,1024]{2,1,0:T(8,128)(2,1)S(1)} %collective-permute-done.5.refs_4_), channel_id=1, source_target_pairs={{4,0},{5,1},{6,2},{7,3},{8,12},{9,13},{10,14},{11,15},{20,16},{21,... | collective-permute-start | bytes 1572872 | tf_op jit(solution)/shard_map/ppermute | solution.py:278
  51.0 17.5 %collective-permute-start.13 = (bf16[2,128,1024]{2,1,0:T(8,128)(2,1)S(1)}, bf16[2,128,1024]{2,1,0:T(8,128)(2,1)S(1)}, u32[]{:S(2)}, u32[]{:S(2)}) collective-permute-start(bf16[2,128,1024]{2,1,0:T(8,128)(2,1)S(1)} %get-tuple-element.84), channel_id=1, source_target_pairs={{4,8},{5,9},{6,10},{7,11},{8,4},{9,5},{10,6},{11,7},{20,24},{21,25... | collective-permute-start | bytes 1572872 | tf_op jit(solution)/shard_map/ppermute | solution.py:278
  52.0 26.8 %collective-permute-start.11 = (bf16[2,128,1024]{2,1,0:T(8,128)(2,1)S(1)}, bf16[2,128,1024]{2,1,0:T(8,128)(2,1)S(1)}, u32[]{:S(2)}, u32[]{:S(2)}) collective-permute-start(bf16[2,128,1024]{2,1,0:T(8,128)(2,1)S(1)} %get-tuple-element.75), channel_id=1, source_target_pairs={{4,0},{5,1},{6,2},{7,3},{8,12},{9,13},{10,14},{11,15},{20,16},{21,... | collective-permute-start | bytes 1572872 | tf_op jit(solution)/shard_map/ppermute | solution.py:278
  60.9 14.0 %copy-start = (bf16[8,16,8192]{2,1,0:T(8,128)(2,1)S(1)}, bf16[8,16,8192]{2,1,0:T(8,128)(2,1)}, u32[]{:S(2)}) copy-start(bf16[8,16,8192]{2,1,0:T(8,128)(2,1)} %param.9) | copy-start | bytes 6291460
  68.6 20.0 %collective-permute-start.14 = (bf16[2,128,1024]{2,1,0:T(8,128)(2,1)S(1)}, bf16[2,128,1024]{2,1,0:T(8,128)(2,1)S(1)}, u32[]{:S(2)}, u32[]{:S(2)}) collective-permute-start(bf16[2,128,1024]{2,1,0:T(8,128)(2,1)S(1)} %collective-permute-done.13.refs_4_), channel_id=1, source_target_pairs={{4,0},{5,1},{6,2},{7,3},{8,12},{9,13},{10,14},{11,15},{20,16},{21,... | collective-permute-start | bytes 1572872 | tf_op jit(solution)/shard_map/ppermute | solution.py:278
  69.9 1.2 collective-permute-start.8
  71.2 3.7 %collective-permute-start.9 = (f32[16,256]{1,0:T(8,128)S(1)}, f32[16,256]{1,0:T(8,128)S(1)}, u32[]{:S(2)}, u32[]{:S(2)}) collective-permute-start(f32[16,256]{1,0:T(8,128)S(1)} %add.82), channel_id=1, source_target_pairs={{0,2},{1,3},{2,0},{3,1},{4,6},{5,7},{6,4},{7,5},{8,10},{9,11},{10,... | collective-permute-start | bytes 49160 | tf_op jit(solution)/shard_map/ppermute | solution.py:271
  76.0 16.6 %collective-permute-start.12 = (bf16[4,160,512]{2,1,0:T(8,128)(2,1)S(1)}, bf16[4,160,512]{2,1,0:T(8,128)(2,1)S(1)}, u32[]{:S(2)}, u32[]{:S(2)}) collective-permute-start(bf16[4,160,512]{2,1,0:T(8,128)(2,1)S(1)} %bitcast.59), channel_id=1, source_target_pairs={{0,2},{1,3},{2,0},{3,1},{4,6},{5,7},{6,4},{7,5},{8,10},{9,11},{10,... | collective-permute-start | bytes 1966088 | tf_op jit(solution)/shard_map/ppermute | solution.py:271
  88.6 12.1 %collective-permute-start.18 = (bf16[2,2,96,512]{3,2,1,0:T(8,128)(2,1)S(1)}, bf16[2,2,96,512]{3,2,1,0:T(8,128)(2,1)S(1)}, u32[]{:S(2)}, u32[]{:S(2)}) collective-permute-start(bf16[2,2,96,512]{3,2,1,0:T(8,128)(2,1)S(1)} %get-tuple-element.90), channel_id=1, source_target_pairs={{0,4},{1,5},{2,6},{3,7},{4,0},{5,1},{6,2},{7,3},{8,12},{9,13},{10,... | collective-permute-start | bytes 1179656 | tf_op jit(solution)/shard_map/ppermute | solution.py:274
  89.8 1.2 collective-permute-start.15
  91.1 3.9 %collective-permute-start.17 = (f32[16,256]{1,0:T(8,128)S(1)}, f32[16,256]{1,0:T(8,128)S(1)}, u32[]{:S(2)}, u32[]{:S(2)}) collective-permute-start(f32[16,256]{1,0:T(8,128)S(1)} %add.86), channel_id=1, source_target_pairs={{0,2},{1,3},{2,0},{3,1},{4,6},{5,7},{6,4},{7,5},{8,10},{9,11},{10,... | collective-permute-start | bytes 49160 | tf_op jit(solution)/shard_map/ppermute | solution.py:271
  92.9 15.4 %collective-permute-start.16 = (bf16[2,160,512]{2,1,0:T(8,128)(2,1)S(1)}, bf16[2,160,512]{2,1,0:T(8,128)(2,1)S(1)}, u32[]{:S(2)}, u32[]{:S(2)}) collective-permute-start(bf16[2,160,512]{2,1,0:T(8,128)(2,1)S(1)} %slice.192), channel_id=1, source_target_pairs={{0,4},{1,5},{2,6},{3,7},{4,0},{5,1},{6,2},{7,3},{8,12},{9,13},{10,... | collective-permute-start | bytes 983048 | tf_op jit(solution)/shard_map/ppermute | solution.py:274
  100.7 14.9 %collective-permute-start.23 = (bf16[4,128,512]{2,1,0:T(8,128)(2,1)S(1)}, bf16[4,128,512]{2,1,0:T(8,128)(2,1)S(1)}, u32[]{:S(2)}, u32[]{:S(2)}) collective-permute-start(bf16[4,128,512]{2,1,0:T(8,128)(2,1)S(1)} %bitcast.60), channel_id=1, source_target_pairs={{0,2},{1,3},{2,0},{3,1},{4,6},{5,7},{6,4},{7,5},{8,10},{9,11},{10,... | collective-permute-start | bytes 1572872 | tf_op jit(solution)/shard_map/ppermute | solution.py:271
  102.4 16.2 %collective-permute-start.22 = (bf16[2,96,512]{2,1,0:T(8,128)(2,1)S(1)}, bf16[2,96,512]{2,1,0:T(8,128)(2,1)S(1)}, u32[]{:S(2)}, u32[]{:S(2)}) collective-permute-start(bf16[2,96,512]{2,1,0:T(8,128)(2,1)S(1)} %fusion.2), channel_id=1, source_target_pairs={{0,2},{1,3},{2,0},{3,1},{4,6},{5,7},{6,4},{7,5},{8,10},{9,11},{10,... | collective-permute-start | bytes 589832 | tf_op jit(solution)/shard_map/ppermute | solution.py:271
  104.6 16.8 %collective-permute-start.20 = (bf16[4,64,512]{2,1,0:T(8,128)(2,1)S(1)}, bf16[4,64,512]{2,1,0:T(8,128)(2,1)S(1)}, u32[]{:S(2)}, u32[]{:S(2)}) collective-permute-start(bf16[4,64,512]{2,1,0:T(8,128)(2,1)S(1)} %bitcast.64), channel_id=1, source_target_pairs={{0,2},{1,3},{2,0},{3,1},{4,6},{5,7},{6,4},{7,5},{8,10},{9,11},{10,... | collective-permute-start | bytes 786440 | tf_op jit(solution)/shard_map/ppermute | solution.py:271
  106.1 13.3 %collective-permute-start.21 = (bf16[2,2,64,512]{3,2,1,0:T(8,128)(2,1)S(1)}, bf16[2,2,64,512]{3,2,1,0:T(8,128)(2,1)S(1)}, u32[]{:S(2)}, u32[]{:S(2)}) collective-permute-start(bf16[2,2,64,512]{3,2,1,0:T(8,128)(2,1)S(1)} %get-tuple-element.97), channel_id=1, source_target_pairs={{0,4},{1,5},{2,6},{3,7},{4,0},{5,1},{6,2},{7,3},{8,12},{9,13},{10,... | collective-permute-start | bytes 786440 | tf_op jit(solution)/shard_map/ppermute | solution.py:274
  108.4 20.2 %collective-permute-start.19 = (bf16[1,160,512]{2,1,0:T(8,128)(2,1)S(1)}, bf16[1,160,512]{2,1,0:T(8,128)(2,1)S(1)}, u32[]{:S(2)}, u32[]{:S(2)}) collective-permute-start(bf16[1,160,512]{2,1,0:T(8,128)(2,1)S(1)} %slice.194), channel_id=1, source_target_pairs={{0,8},{1,9},{2,10},{3,11},{4,12},{5,13},{6,14},{7,15},{8,0},{9,1},... | collective-permute-start | bytes 491528 | tf_op jit(solution)/shard_map/ppermute | solution.py:274
  115.9 7.6 %collective-permute-start.26 = (bf16[2,128,512]{2,1,0:T(8,128)(2,1)S(1)}, bf16[2,128,512]{2,1,0:T(8,128)(2,1)S(1)}, u32[]{:S(2)}, u32[]{:S(2)}) collective-permute-start(bf16[2,128,512]{2,1,0:T(8,128)(2,1)S(1)} %slice.193), channel_id=1, source_target_pairs={{0,4},{1,5},{2,6},{3,7},{4,0},{5,1},{6,2},{7,3},{8,12},{9,13},{10,... | collective-permute-start | bytes 786440 | tf_op jit(solution)/shard_map/ppermute | solution.py:274
  118.6 10.1 %collective-permute-start.27 = (bf16[1,96,512]{2,1,0:T(8,128)(2,1)S(1)}, bf16[1,96,512]{2,1,0:T(8,128)(2,1)S(1)}, u32[]{:S(2)}, u32[]{:S(2)}) collective-permute-start(bf16[1,96,512]{2,1,0:T(8,128)(2,1)S(1)} %slice.197), channel_id=1, source_target_pairs={{0,8},{1,9},{2,10},{3,11},{4,12},{5,13},{6,14},{7,15},{8,0},{9,1},... | collective-permute-start | bytes 294920 | tf_op jit(solution)/shard_map/ppermute | solution.py:274
  119.6 5.2 %collective-permute-start.25 = (bf16[2,64,512]{2,1,0:T(8,128)(2,1)S(1)}, bf16[2,64,512]{2,1,0:T(8,128)(2,1)S(1)}, u32[]{:S(2)}, u32[]{:S(2)}) collective-permute-start(bf16[2,64,512]{2,1,0:T(8,128)(2,1)S(1)} %fusion.3), channel_id=1, source_target_pairs={{0,2},{1,3},{2,0},{3,1},{4,6},{5,7},{6,4},{7,5},{8,10},{9,11},{10,... | collective-permute-start | bytes 393224 | tf_op jit(solution)/shard_map/ppermute | solution.py:271
  121.5 5.4 %collective-permute-start.24 = (bf16[2,64,512]{2,1,0:T(8,128)(2,1)S(1)}, bf16[2,64,512]{2,1,0:T(8,128)(2,1)S(1)}, u32[]{:S(2)}, u32[]{:S(2)}) collective-permute-start(bf16[2,64,512]{2,1,0:T(8,128)(2,1)S(1)} %slice.196), channel_id=1, source_target_pairs={{0,4},{1,5},{2,6},{3,7},{4,0},{5,1},{6,2},{7,3},{8,12},{9,13},{10,... | collective-permute-start | bytes 393224 | tf_op jit(solution)/shard_map/ppermute | solution.py:274
  123.6 9.4 %collective-permute-start.28 = (bf16[1,128,512]{2,1,0:T(8,128)(2,1)S(1)}, bf16[1,128,512]{2,1,0:T(8,128)(2,1)S(1)}, u32[]{:S(2)}, u32[]{:S(2)}) collective-permute-start(bf16[1,128,512]{2,1,0:T(8,128)(2,1)S(1)} %slice.195), channel_id=1, source_target_pairs={{0,8},{1,9},{2,10},{3,11},{4,12},{5,13},{6,14},{7,15},{8,0},{9,1},... | collective-permute-start | bytes 393224 | tf_op jit(solution)/shard_map/ppermute | solution.py:274
  124.9 9.5 %collective-permute-start.29 = (bf16[1,64,512]{2,1,0:T(8,128)(2,1)S(1)}, bf16[1,64,512]{2,1,0:T(8,128)(2,1)S(1)}, u32[]{:S(2)}, u32[]{:S(2)}) collective-permute-start(bf16[1,64,512]{2,1,0:T(8,128)(2,1)S(1)} %slice.199), channel_id=1, source_target_pairs={{0,8},{1,9},{2,10},{3,11},{4,12},{5,13},{6,14},{7,15},{8,0},{9,1},... | collective-permute-start | bytes 196616 | tf_op jit(solution)/shard_map/ppermute | solution.py:274
  126.9 8.2 %collective-permute-start.30 = (bf16[1,64,512]{2,1,0:T(8,128)(2,1)S(1)}, bf16[1,64,512]{2,1,0:T(8,128)(2,1)S(1)}, u32[]{:S(2)}, u32[]{:S(2)}) collective-permute-start(bf16[1,64,512]{2,1,0:T(8,128)(2,1)S(1)} %slice.198), channel_id=1, source_target_pairs={{0,8},{1,9},{2,10},{3,11},{4,12},{5,13},{6,14},{7,15},{8,0},{9,1},... | collective-permute-start | bytes 196616 | tf_op jit(solution)/shard_map/ppermute | solution.py:274
  135.1 0.8 copy-start.3

commit v7 on v5

--- a/solution.py
+++ b/solution.py
@@ -437,7 +437,7 @@
     begin(3, next_stays, goes)
     begin(4, last_stays, last_goes)
     done = next_stays
-    for c in (0, 2, 1, 3, 4, 2, 3, 4, 0, 1, 2, 3, 4):
+    for c in (0, 2, 1, 3, 4, 2, 4, 3, 0, 1, 2, 4, 3):
         if plans[c]:
             done = add(c, done)
     for c in range(len(plans)):

time: 137 us -> 137 us (level)
  transfers between devices with their start and end apart: 31 -> 31, of which waited for: 19 -> 18; matrix products, arithmetic and copies ran while one was open for 1% -> 1% of each run, Pallas kernels for 24% -> 24%
where the time goes in v7:
time: 137 us
  waiting for transfers between devices  65.1 us (48%)
  Pallas kernels  35 us (26%)
  starting transfers between devices  33.7 us (25%)
  other arithmetic  1.41 us (1%)
    ppermute x7, waiting for transfers between devices, hop(): return lax.ppermute(value, 'tensor', pairs)  29.1 us
    ppermute x13, waiting for transfers between devices, in_plane(): lax.ppermute(value, 'tensor', [(t, t ^ other) for t in range(devices)])  22.4 us
    pallas_call x1, Pallas kernels, base_blocks(): pl.pallas_call(body, grid_spec=pltpu.PrefetchScalarGridSpec(num_scalar_pr...  13.9 us
    ppermute x13, starting transfers between devices, in_plane(): lax.ppermute(value, 'tensor', [(t, t ^ other) for t in range(devices)])  13.8 us
    ppermute x11, waiting for transfers between devices, along(): lax.ppermute(value, 'tensor', [(t, t ^ other * PLANE) for t in range(devi...  13.5 us
    ppermute x11, starting transfers between devices, along(): lax.ppermute(value, 'tensor', [(t, t ^ other * PLANE) for t in range(devi...  12.7 us
    pallas_call x6, Pallas kernels, low_part(): pl.pallas_call(body, grid_spec=pltpu.PrefetchScalarGridSpec(num_scalar_pr...  7.34 us
    ppermute x7, starting transfers between devices, hop(): return lax.ppermute(value, 'tensor', pairs)  7.26 us
  transfers between devices with their start and end apart: 31, of which 18 were waited for; matrix products, arithmetic and copies ran while one was open for 1% of the time, Pallas kernels for 24%

profile of v7, /device:TPU:0, one launch (start us, length us, event | category | flops | bytes accessed | tf_op | source)
XLA Modules:
  0.0 137.0 jit_solution(10581281434505969763)
XLA Ops:
  0.2 1.8 %pack_factors.3 = bf16[4,128,1024]{2,1,0:T(8,128)(2,1)S(1)} custom-call(s32[3]{0:T(128)S(1)} %pad_add_fusion.place_ref, s32[4]{0:T(128)S(1)} %pad_add_fusion.1.order_ref, bf16[128,16384]{1,0:T(8,128)(2,1)} %bitcast.65, bf16[128,16384]{1,0:T(8,128)(2,1)} %bitcast.66, bf16[128,16384]{1,0:T(8,128)(2,1)} %bitcast.67, bf16[128,16384]{1,0:T(8,128)(2,1)} %bitcast.68), custom_call_target="tpu_custom_call" | custom-call | bytes 2097 | tf_op jit(solution)/shard_map/pack_factors/pallas_call | solution.py:52
  2.0 3.0 %collective-permute-start.2 = (bf16[4,128,1024]{2,1,0:T(8,128)(2,1)S(1)}, bf16[4,128,1024]{2,1,0:T(8,128)(2,1)S(1)}, u32[]{:S(2)}, u32[]{:S(2)}) collective-permute-start(bf16[4,128,1024]{2,1,0:T(8,128)(2,1)S(1)} %pack_factors.3), channel_id=1, source_target_pairs={{0,2},{1,3},{2,0},{3,1},{4,6},{5,7},{6,4},{7,5},{8,10},{9,11},{10,... | collective-permute-start | bytes 3145736 | tf_op jit(solution)/shard_map/ppermute | solution.py:271
  5.7 4.4 %collective-permute-start = (bf16[4,128,1024]{2,1,0:T(8,128)(2,1)S(1)}, bf16[4,128,1024]{2,1,0:T(8,128)(2,1)S(1)}, u32[]{:S(2)}, u32[]{:S(2)}) collective-permute-start(bf16[4,128,1024]{2,1,0:T(8,128)(2,1)S(1)} %copy-done.1), channel_id=1, source_target_pairs={{0,4},{1,5},{2,6},{3,7},{4,0},{5,1},{6,2},{7,3},{8,12},{9,13},{10,... | collective-permute-start | bytes 3145736 | tf_op jit(solution)/shard_map/ppermute | solution.py:274
  10.1 1.8 %pack_factors.4 = bf16[4,128,1024]{2,1,0:T(8,128)(2,1)S(1)} custom-call(s32[3]{0:T(128)S(1)} %pad_add_fusion.place_ref, s32[4]{0:T(128)S(1)} %pad_add_fusion.1.order_ref, bf16[128,16384]{1,0:T(8,128)(2,1)} %bitcast.69, bf16[128,16384]{1,0:T(8,128)(2,1)} %bitcast.70, bf16[128,16384]{1,0:T(8,128)(2,1)} %bitcast.71, bf16[128,16384]{1,0:T(8,128)(2,1)} %bitcast.72), custom_call_target="tpu_custom_call" | custom-call | bytes 2097 | tf_op jit(solution)/shard_map/pack_factors/pallas_call | solution.py:52
  11.9 1.8 %pack_factors.5.refs_0_ = bf16[4,128,1024]{2,1,0:T(8,128)(2,1)S(1)} custom-call(s32[3]{0:T(128)S(1)} %pad_add_fusion.place_ref, s32[4]{0:T(128)S(1)} %pad_add_fusion.1.order_ref, bf16[128,16384]{1,0:T(8,128)(2,1)} %bitcast.73, bf16[128,16384]{1,0:T(8,128)(2,1)} %bitcast.74, bf16[128,16384]{1,0:T(8,128)(2,1)} %bitcast.75, bf16[128,16384]{1,0:T(8,128)(2,1)} %bitcast.76), custom_call_target="tpu_custom_call" | custom-call | bytes 2097 | tf_op jit(solution)/shard_map/pack_factors/pallas_call | solution.py:52
  13.7 3.1 %pack_core.1 = bf16[2,4,128,1024]{3,2,1,0:T(8,128)(2,1)S(1)} custom-call(s32[3]{0:T(128)S(1)} %pad_add_fusion.place_ref, s32[4]{0:T(128)S(1)} %pad_add_fusion.1.order_ref, bf16[128,16384]{1,0:T(8,128)(2,1)} %bitcast.77, bf16[128,8192]{1,0:T(8,128)(2,1)} %bitcast.49, bf16[128,8192]{1,0:T(8,128)(2,1)} %bitcast.50), custom_call_target="tpu_custom_call" | custom-call | bytes 4194 | tf_op jit(solution)/shard_map/pack_core/pallas_call | solution.py:82
  16.9 13.9 %base_blocks.1 = (bf16[2,4,4,128,512]{4,3,2,1,0:T(8,128)(2,1)S(1)}, f32[2,4,4,128,512]{4,3,2,1,0:T(8,128)S(1)}) custom-call(s32[3]{0:T(128)S(1)} %pad_add_fusion.place_ref, bf16[4,128,1024]{2,1,0:T(8,128)(2,1)} %refs_1_.1, bf16[1024,8192]{1,0:T(8,128)(2,1)} %d3.1, bf16[1024,8192]{1,0:T(8,128)(2,1)} %d3.1, bf16[1024,8192]{1,0:T(8,128)(2,1)} %d3.1, ...), custom_call_target="tpu_custom_call" | custom-call | flops 8589934 | bytes 29360 | tf_op jit(solution)/shard_map/base_blocks/pallas_call | solution.py:114
  30.8 1.9 %collective-permute-done.refs_4_.refs_2_ = bf16[4,128,1024]{2,1,0:T(8,128)(2,1)S(1)} collective-permute-done((bf16[4,128,1024]{2,1,0:T(8,128)(2,1)S(1)}, bf16[4,128,1024]{2,1,0:T(8,128)(2,1)S(1)}, u32[]{:S(2)}, u32[]{:S(2)}) %collective-permute-start) | collective-permute-done | bytes 1048608 | tf_op jit(solution)/shard_map/ppermute | solution.py:274
  33.6 1.3 collective-permute-start.4
  35.6 14.2 %collective-permute-done.4.refs_5_ = bf16[2,128,1024]{2,1,0:T(8,128)(2,1)S(1)} collective-permute-done((bf16[2,128,1024]{2,1,0:T(8,128)(2,1)S(1)}, bf16[2,128,1024]{2,1,0:T(8,128)(2,1)S(1)}, u32[]{:S(2)}, u32[]{:S(2)}) %collective-permute-start.4) | collective-permute-done | bytes 524320 | tf_op jit(solution)/shard_map/ppermute | solution.py:278
  49.7 1.3 collective-permute-start.7
  52.0 1.3 collective-permute-start.11
  53.3 1.5 %low_part.6 = f32[16,512]{1,0:T(8,128)S(1)} custom-call(s32[3]{0:T(128)S(1)} %pad_add_fusion.place_ref, s32[1,512]{1,0:T(1,128)S(1)} %bitcast.62, bf16[4,128,1024]{2,1,0:T(8,128)(2,1)S(1)} %pack_factors.5.refs_0_, bf16[2,4,128,1024]{3,2,1,0:T(8,128)(2,1)S(1)} %collective-permute-done.3.refs_1_.t_ref, ...), custom_call_target="tpu_custom_call" | custom-call | flops 805306368 | bytes 3670016 | tf_op jit(solution)/shard_map/low_part/pallas_call | solution.py:175
  54.8 3.6 %collective-permute-done.6.refs_0_.refs_3_ = bf16[4,128,1024]{2,1,0:T(8,128)(2,1)S(1)} collective-permute-done((bf16[4,128,1024]{2,1,0:T(8,128)(2,1)S(1)}, bf16[4,128,1024]{2,1,0:T(8,128)(2,1)S(1)}, u32[]{:S(2)}, u32[]{:S(2)}) %collective-permute-start.6) | collective-permute-done | bytes 1048608 | tf_op jit(solution)/shard_map/ppermute | solution.py:271
  58.4 1.4 %low_part.7 = f32[16,512]{1,0:T(8,128)S(1)} custom-call(s32[3]{0:T(128)S(1)} %pad_add_fusion.place_ref, s32[1,512]{1,0:T(1,128)S(1)} %bitcast.63, bf16[4,128,1024]{2,1,0:T(8,128)(2,1)S(1)} %collective-permute-done.6.refs_0_.refs_3_, bf16[4,128,1024]{2,1,0:T(8,128)(2,1)S(1)} %copy-done.2, bf16[4,128,1024]{2,1,0:T(8,128)(2,1)S(1)} %collective-permute-done.refs_4_.refs_2_), custom_call_target="tpu_custom_call" | custom-call | flops 268435456 | bytes 2621440 | tf_op jit(solution)/shard_map/low_part/pallas_call | solution.py:175
  59.8 1.1 low_part.8
  60.9 6.6 %collective-permute-done.7.refs_5_ = bf16[2,128,1024]{2,1,0:T(8,128)(2,1)S(1)} collective-permute-done((bf16[2,128,1024]{2,1,0:T(8,128)(2,1)S(1)}, bf16[2,128,1024]{2,1,0:T(8,128)(2,1)S(1)}, u32[]{:S(2)}, u32[]{:S(2)}) %collective-permute-start.7) | collective-permute-done | bytes 524320 | tf_op jit(solution)/shard_map/ppermute | solution.py:278
  67.5 1.1 low_part.9
  68.6 1.3 collective-permute-start.14
  70.0 1.2 collective-permute-done.8
  71.2 1.5 %collective-permute-start.9 = (f32[16,256]{1,0:T(8,128)S(1)}, f32[16,256]{1,0:T(8,128)S(1)}, u32[]{:S(2)}, u32[]{:S(2)}) collective-permute-start(f32[16,256]{1,0:T(8,128)S(1)} %add.82), channel_id=1, source_target_pairs={{0,2},{1,3},{2,0},{3,1},{4,6},{5,7},{6,4},{7,5},{8,10},{9,11},{10,... | collective-permute-start | bytes 49160 | tf_op jit(solution)/shard_map/ppermute | solution.py:271
  72.7 2.2 %collective-permute-done.9 = f32[16,256]{1,0:T(8,128)S(1)} collective-permute-done((f32[16,256]{1,0:T(8,128)S(1)}, f32[16,256]{1,0:T(8,128)S(1)}, u32[]{:S(2)}, u32[]{:S(2)}) %collective-permute-start.9) | collective-permute-done | bytes 16416 | tf_op jit(solution)/shard_map/ppermute | solution.py:271
  74.9 1.1 add_extra.4
  76.0 1.6 %collective-permute-start.12 = (bf16[4,160,512]{2,1,0:T(8,128)(2,1)S(1)}, bf16[4,160,512]{2,1,0:T(8,128)(2,1)S(1)}, u32[]{:S(2)}, u32[]{:S(2)}) collective-permute-start(bf16[4,160,512]{2,1,0:T(8,128)(2,1)S(1)} %bitcast.59), channel_id=1, source_target_pairs={{0,2},{1,3},{2,0},{3,1},{4,6},{5,7},{6,4},{7,5},{8,10},{9,11},{10,... | collective-permute-start | bytes 1966088 | tf_op jit(solution)/shard_map/ppermute | solution.py:271
  77.6 1.1 collective-permute-done.11.refs_5_
  78.7 1.5 %add_extra.5 = (f32[1,4,160,512]{3,2,1,0:T(8,128)S(1)}, bf16[2,2,96,512]{3,2,1,0:T(8,128)(2,1)S(1)}, f32[2,2,96,512]{3,2,1,0:T(8,128)S(1)}) custom-call(s32[3]{0:T(128)S(1)} %pad_add_fusion.place_ref, f32[16,256]{1,0:T(8,128)S(1)} %add.83.low_ref, s32[1,256]{1,0:T(1,128)S(1)} %get-tuple-element.122.slots_ref, bf16[128,8192]{1,0:T(8,128)(2,1)S(1)} %bitcast.52, ...), custom_call_target="tpu_custom_call" | custom-call | flops 268435 | bytes 5242 | tf_op jit(solution)/shard_map/add_extra/pallas_call | solution.py:235
  80.3 1.1 low_part.10
  81.4 7.2 %collective-permute-done.14.refs_5_ = bf16[2,128,1024]{2,1,0:T(8,128)(2,1)S(1)} collective-permute-done((bf16[2,128,1024]{2,1,0:T(8,128)(2,1)S(1)}, bf16[2,128,1024]{2,1,0:T(8,128)(2,1)S(1)}, u32[]{:S(2)}, u32[]{:S(2)}) %collective-permute-start.14) | collective-permute-done | bytes 524320 | tf_op jit(solution)/shard_map/ppermute | solution.py:278
  88.6 1.2 low_part.11
  89.9 1.2 collective-permute-done.15
  91.1 1.5 %collective-permute-start.17 = (f32[16,256]{1,0:T(8,128)S(1)}, f32[16,256]{1,0:T(8,128)S(1)}, u32[]{:S(2)}, u32[]{:S(2)}) collective-permute-start(f32[16,256]{1,0:T(8,128)S(1)} %add.86), channel_id=1, source_target_pairs={{0,2},{1,3},{2,0},{3,1},{4,6},{5,7},{6,4},{7,5},{8,10},{9,11},{10,... | collective-permute-start | bytes 49160 | tf_op jit(solution)/shard_map/ppermute | solution.py:271
  92.9 1.9 %collective-permute-done.17 = f32[16,256]{1,0:T(8,128)S(1)} collective-permute-done((f32[16,256]{1,0:T(8,128)S(1)}, f32[16,256]{1,0:T(8,128)S(1)}, u32[]{:S(2)}, u32[]{:S(2)}) %collective-permute-start.17) | collective-permute-done | bytes 16416 | tf_op jit(solution)/shard_map/ppermute | solution.py:271
  94.8 2.0 %collective-permute-start.16 = (bf16[2,160,512]{2,1,0:T(8,128)(2,1)S(1)}, bf16[2,160,512]{2,1,0:T(8,128)(2,1)S(1)}, u32[]{:S(2)}, u32[]{:S(2)}) collective-permute-start(bf16[2,160,512]{2,1,0:T(8,128)(2,1)S(1)} %slice.192), channel_id=1, source_target_pairs={{0,4},{1,5},{2,6},{3,7},{4,0},{5,1},{6,2},{7,3},{8,12},{9,13},{10,... | collective-permute-start | bytes 983048 | tf_op jit(solution)/shard_map/ppermute | solution.py:274
  96.9 1.0 add_extra.6
  97.9 1.6 %collective-permute-done.18 = bf16[2,2,96,512]{3,2,1,0:T(8,128)(2,1)S(1)} collective-permute-done((bf16[2,2,96,512]{3,2,1,0:T(8,128)(2,1)S(1)}, bf16[2,2,96,512]{3,2,1,0:T(8,128)(2,1)S(1)}, u32[]{:S(2)}, u32[]{:S(2)}) %collective-permute-start.18) | collective-permute-done | bytes 393248 | tf_op jit(solution)/shard_map/ppermute | solution.py:274
  99.5 1.5 %collective-permute-start.22 = (bf16[4,128,512]{2,1,0:T(8,128)(2,1)S(1)}, bf16[4,128,512]{2,1,0:T(8,128)(2,1)S(1)}, u32[]{:S(2)}, u32[]{:S(2)}) collective-permute-start(bf16[4,128,512]{2,1,0:T(8,128)(2,1)S(1)} %bitcast.60), channel_id=1, source_target_pairs={{0,2},{1,3},{2,0},{3,1},{4,6},{5,7},{6,4},{7,5},{8,10},{9,11},{10,... | collective-permute-start | bytes 1572872 | tf_op jit(solution)/shard_map/ppermute | solution.py:271
  101.7 1.6 %add_extra.7 = (f32[1,4,128,512]{3,2,1,0:T(8,128)S(1)}, bf16[2,2,64,512]{3,2,1,0:T(8,128)(2,1)S(1)}, f32[2,2,64,512]{3,2,1,0:T(8,128)S(1)}, bf16[1,4,64,512]{3,2,1,0:T(8,128)(2,1)S(1)}, f32[1,4,64,512]{3,2,1,0:T(8,128)S(1)}) custom-call(s32[3]{0:T(128)S(1)} %pad_add_fusion.place_ref, f32[16,256]{1,0:T(8,128)S(1)} %add.88.low_ref, ...), custom_call_target="tpu_custom_call" | custom-call | flops 268435 | bytes 5242 | tf_op jit(solution)/shard_map/add_extra/pallas_call | solution.py:235
  103.4 1.6 %collective-permute-start.24 = (bf16[4,64,512]{2,1,0:T(8,128)(2,1)S(1)}, bf16[4,64,512]{2,1,0:T(8,128)(2,1)S(1)}, u32[]{:S(2)}, u32[]{:S(2)}) collective-permute-start(bf16[4,64,512]{2,1,0:T(8,128)(2,1)S(1)} %bitcast.64), channel_id=1, source_target_pairs={{0,2},{1,3},{2,0},{3,1},{4,6},{5,7},{6,4},{7,5},{8,10},{9,11},{10,... | collective-permute-start | bytes 786440 | tf_op jit(solution)/shard_map/ppermute | solution.py:271
  105.0 1.5 %collective-permute-done.16 = bf16[2,160,512]{2,1,0:T(8,128)(2,1)S(1)} collective-permute-done((bf16[2,160,512]{2,1,0:T(8,128)(2,1)S(1)}, bf16[2,160,512]{2,1,0:T(8,128)(2,1)S(1)}, u32[]{:S(2)}, u32[]{:S(2)}) %collective-permute-start.16) | collective-permute-done | bytes 327712 | tf_op jit(solution)/shard_map/ppermute | solution.py:274
  107.6 6.8 %collective-permute-done.22 = bf16[4,128,512]{2,1,0:T(8,128)(2,1)S(1)} collective-permute-done((bf16[4,128,512]{2,1,0:T(8,128)(2,1)S(1)}, bf16[4,128,512]{2,1,0:T(8,128)(2,1)S(1)}, u32[]{:S(2)}, u32[]{:S(2)}) %collective-permute-start.22) | collective-permute-done | bytes 524320 | tf_op jit(solution)/shard_map/ppermute | solution.py:271
  114.6 3.9 %collective-permute-done.21 = bf16[2,96,512]{2,1,0:T(8,128)(2,1)S(1)} collective-permute-done((bf16[2,96,512]{2,1,0:T(8,128)(2,1)S(1)}, bf16[2,96,512]{2,1,0:T(8,128)(2,1)S(1)}, u32[]{:S(2)}, u32[]{:S(2)}) %collective-permute-start.21) | collective-permute-done | bytes 196640 | tf_op jit(solution)/shard_map/ppermute | solution.py:271
  118.9 1.6 %collective-permute-start.23 = (bf16[2,64,512]{2,1,0:T(8,128)(2,1)S(1)}, bf16[2,64,512]{2,1,0:T(8,128)(2,1)S(1)}, u32[]{:S(2)}, u32[]{:S(2)}) collective-permute-start(bf16[2,64,512]{2,1,0:T(8,128)(2,1)S(1)} %fusion.3), channel_id=1, source_target_pairs={{0,2},{1,3},{2,0},{3,1},{4,6},{5,7},{6,4},{7,5},{8,10},{9,11},{10,... | collective-permute-start | bytes 393224 | tf_op jit(solution)/shard_map/ppermute | solution.py:271
  120.5 1.6 %collective-permute-done.24 = bf16[4,64,512]{2,1,0:T(8,128)(2,1)S(1)} collective-permute-done((bf16[4,64,512]{2,1,0:T(8,128)(2,1)S(1)}, bf16[4,64,512]{2,1,0:T(8,128)(2,1)S(1)}, u32[]{:S(2)}, u32[]{:S(2)}) %collective-permute-start.24) | collective-permute-done | bytes 262176 | tf_op jit(solution)/shard_map/ppermute | solution.py:271
  122.6 1.7 %collective-permute-start.28 = (bf16[1,128,512]{2,1,0:T(8,128)(2,1)S(1)}, bf16[1,128,512]{2,1,0:T(8,128)(2,1)S(1)}, u32[]{:S(2)}, u32[]{:S(2)}) collective-permute-start(bf16[1,128,512]{2,1,0:T(8,128)(2,1)S(1)} %slice.195), channel_id=1, source_target_pairs={{0,8},{1,9},{2,10},{3,11},{4,12},{5,13},{6,14},{7,15},{8,0},{9,1},... | collective-permute-start | bytes 393224 | tf_op jit(solution)/shard_map/ppermute | solution.py:274
  124.3 5.1 %collective-permute-done.25 = bf16[2,64,512]{2,1,0:T(8,128)(2,1)S(1)} collective-permute-done((bf16[2,64,512]{2,1,0:T(8,128)(2,1)S(1)}, bf16[2,64,512]{2,1,0:T(8,128)(2,1)S(1)}, u32[]{:S(2)}, u32[]{:S(2)}) %collective-permute-start.25) | collective-permute-done | bytes 131104 | tf_op jit(solution)/shard_map/ppermute | solution.py:274
  129.6 3.0 %collective-permute-start.29 = (bf16[1,64,512]{2,1,0:T(8,128)(2,1)S(1)}, bf16[1,64,512]{2,1,0:T(8,128)(2,1)S(1)}, u32[]{:S(2)}, u32[]{:S(2)}) collective-permute-start(bf16[1,64,512]{2,1,0:T(8,128)(2,1)S(1)} %slice.198), channel_id=1, source_target_pairs={{0,8},{1,9},{2,10},{3,11},{4,12},{5,13},{6,14},{7,15},{8,0},{9,1},... | collective-permute-start | bytes 196616 | tf_op jit(solution)/shard_map/ppermute | solution.py:274
  132.7 2.0 %collective-permute-done.30 = bf16[1,64,512]{2,1,0:T(8,128)(2,1)S(1)} collective-permute-done((bf16[1,64,512]{2,1,0:T(8,128)(2,1)S(1)}, bf16[1,64,512]{2,1,0:T(8,128)(2,1)S(1)}, u32[]{:S(2)}, u32[]{:S(2)}) %collective-permute-start.30) | collective-permute-done | bytes 65568 | tf_op jit(solution)/shard_map/ppermute | solution.py:274
  134.8 1.4 %collective-permute-done.29 = bf16[1,64,512]{2,1,0:T(8,128)(2,1)S(1)} collective-permute-done((bf16[1,64,512]{2,1,0:T(8,128)(2,1)S(1)}, bf16[1,64,512]{2,1,0:T(8,128)(2,1)S(1)}, u32[]{:S(2)}, u32[]{:S(2)}) %collective-permute-start.29) | collective-permute-done | bytes 65568 | tf_op jit(solution)/shard_map/ppermute | solution.py:274
  (81 shorter events, 7.7 us)
Async XLA Ops:
  0.2 4.8 %copy-start.1 = (bf16[4,128,1024]{2,1,0:T(8,128)(2,1)S(1)}, bf16[4,128,1024]{2,1,0:T(8,128)(2,1)}, u32[]{:S(2)}) copy-start(bf16[4,128,1024]{2,1,0:T(8,128)(2,1)} %refs_1_.1) | copy-start | bytes 3145732
  2.0 28.8 %collective-permute-start.2 = (bf16[4,128,1024]{2,1,0:T(8,128)(2,1)S(1)}, bf16[4,128,1024]{2,1,0:T(8,128)(2,1)S(1)}, u32[]{:S(2)}, u32[]{:S(2)}) collective-permute-start(bf16[4,128,1024]{2,1,0:T(8,128)(2,1)S(1)} %pack_factors.3), channel_id=1, source_target_pairs={{0,2},{1,3},{2,0},{3,1},{4,6},{5,7},{6,4},{7,5},{8,10},{9,11},{10,... | collective-permute-start | bytes 3145736 | tf_op jit(solution)/shard_map/ppermute | solution.py:271
  5.0 25.8 %collective-permute-start.1 = (bf16[4,128,1024]{2,1,0:T(8,128)(2,1)S(1)}, bf16[4,128,1024]{2,1,0:T(8,128)(2,1)S(1)}, u32[]{:S(2)}, u32[]{:S(2)}) collective-permute-start(bf16[4,128,1024]{2,1,0:T(8,128)(2,1)S(1)} %copy-done.1), channel_id=1, source_target_pairs={{4,8},{5,9},{6,10},{7,11},{8,4},{9,5},{10,6},{11,7},{20,24},{21,25... | collective-permute-start | bytes 3145736 | tf_op jit(solution)/shard_map/ppermute | solution.py:278
  5.7 27.0 %collective-permute-start = (bf16[4,128,1024]{2,1,0:T(8,128)(2,1)S(1)}, bf16[4,128,1024]{2,1,0:T(8,128)(2,1)S(1)}, u32[]{:S(2)}, u32[]{:S(2)}) collective-permute-start(bf16[4,128,1024]{2,1,0:T(8,128)(2,1)S(1)} %copy-done.1), channel_id=1, source_target_pairs={{0,4},{1,5},{2,6},{3,7},{4,0},{5,1},{6,2},{7,3},{8,12},{9,13},{10,... | collective-permute-start | bytes 3145736 | tf_op jit(solution)/shard_map/ppermute | solution.py:274
  32.7 19.0 %copy-start.4 = (s32[128]{0:T(128)S(1)}, s32[128]{0:T(128)}, u32[]{:S(2)}) copy-start(s32[128]{0:T(128)} %param.10) | copy-start | bytes 1540
  32.7 19.0 %copy-start.5 = (s32[128]{0:T(128)S(1)}, s32[128]{0:T(128)}, u32[]{:S(2)}) copy-start(s32[128]{0:T(128)} %param.11) | copy-start | bytes 1540
  32.7 20.5 %copy-start.2 = (bf16[4,128,1024]{2,1,0:T(8,128)(2,1)S(1)}, bf16[4,128,1024]{2,1,0:T(8,128)(2,1)}, u32[]{:S(2)}) copy-start(bf16[4,128,1024]{2,1,0:T(8,128)(2,1)} %refs_1_.1) | copy-start | bytes 3145732
  32.7 42.2 %collective-permute-start.10 = (bf16[2,4,4,128,512]{4,3,2,1,0:T(8,128)(2,1)S(1)}, bf16[2,4,4,128,512]{4,3,2,1,0:T(8,128)(2,1)S(1)}, u32[]{:S(2)}, u32[]{:S(2)}) collective-permute-start(bf16[2,4,4,128,512]{4,3,2,1,0:T(8,128)(2,1)S(1)} %get-tuple-element.74), channel_id=1, source_target_pairs={{0,1},{1,0},{2,3},{3,2},{4,5},{5,4},{6,7},{7,6},{8,9},{9,8},{10,11... | collective-permute-start | bytes 12582920 | tf_op jit(solution)/shard_map/ppermute | solution.py:271
  32.7 19.2 %collective-permute-start.3 = (bf16[2,4,128,1024]{3,2,1,0:T(8,128)(2,1)S(1)}, bf16[2,4,128,1024]{3,2,1,0:T(8,128)(2,1)S(1)}, u32[]{:S(2)}, u32[]{:S(2)}) collective-permute-start(bf16[2,4,128,1024]{3,2,1,0:T(8,128)(2,1)S(1)} %pack_core.1), channel_id=1, source_target_pairs={{0,1},{1,0},{2,3},{3,2},{4,5},{5,4},{6,7},{7,6},{8,9},{9,8},{10,11... | collective-permute-start | bytes 6291464 | tf_op jit(solution)/shard_map/ppermute | solution.py:271
  33.2 25.2 %collective-permute-start.6 = (bf16[4,128,1024]{2,1,0:T(8,128)(2,1)S(1)}, bf16[4,128,1024]{2,1,0:T(8,128)(2,1)S(1)}, u32[]{:S(2)}, u32[]{:S(2)}) collective-permute-start(bf16[4,128,1024]{2,1,0:T(8,128)(2,1)S(1)} %pack_factors.4), channel_id=1, source_target_pairs={{0,3},{1,2},{2,1},{3,0},{4,7},{5,6},{6,5},{7,4},{8,11},{9,10},{10,... | collective-permute-start | bytes 3145736 | tf_op jit(solution)/shard_map/ppermute | solution.py:271
  33.6 16.2 %collective-permute-start.4 = (bf16[2,128,1024]{2,1,0:T(8,128)(2,1)S(1)}, bf16[2,128,1024]{2,1,0:T(8,128)(2,1)S(1)}, u32[]{:S(2)}, u32[]{:S(2)}) collective-permute-start(bf16[2,128,1024]{2,1,0:T(8,128)(2,1)S(1)} %get-tuple-element.120), channel_id=1, source_target_pairs={{4,0},{5,1},{6,2},{7,3},{8,12},{9,13},{10,14},{11,15},{20,16},{21,... | collective-permute-start | bytes 1572872 | tf_op jit(solution)/shard_map/ppermute | solution.py:278
  34.9 14.9 %collective-permute-start.5 = (bf16[2,128,1024]{2,1,0:T(8,128)(2,1)S(1)}, bf16[2,128,1024]{2,1,0:T(8,128)(2,1)S(1)}, u32[]{:S(2)}, u32[]{:S(2)}) collective-permute-start(bf16[2,128,1024]{2,1,0:T(8,128)(2,1)S(1)} %get-tuple-element.118), channel_id=1, source_target_pairs={{4,8},{5,9},{6,10},{7,11},{8,4},{9,5},{10,6},{11,7},{20,24},{21,25... | collective-permute-start | bytes 1572872 | tf_op jit(solution)/shard_map/ppermute | solution.py:278
  49.7 17.8 %collective-permute-start.7 = (bf16[2,128,1024]{2,1,0:T(8,128)(2,1)S(1)}, bf16[2,128,1024]{2,1,0:T(8,128)(2,1)S(1)}, u32[]{:S(2)}, u32[]{:S(2)}) collective-permute-start(bf16[2,128,1024]{2,1,0:T(8,128)(2,1)S(1)} %collective-permute-done.5.refs_4_), channel_id=1, source_target_pairs={{4,0},{5,1},{6,2},{7,3},{8,12},{9,13},{10,14},{11,15},{20,16},{21,... | collective-permute-start | bytes 1572872 | tf_op jit(solution)/shard_map/ppermute | solution.py:278
  51.0 17.5 %collective-permute-start.13 = (bf16[2,128,1024]{2,1,0:T(8,128)(2,1)S(1)}, bf16[2,128,1024]{2,1,0:T(8,128)(2,1)S(1)}, u32[]{:S(2)}, u32[]{:S(2)}) collective-permute-start(bf16[2,128,1024]{2,1,0:T(8,128)(2,1)S(1)} %get-tuple-element.84), channel_id=1, source_target_pairs={{4,8},{5,9},{6,10},{7,11},{8,4},{9,5},{10,6},{11,7},{20,24},{21,25... | collective-permute-start | bytes 1572872 | tf_op jit(solution)/shard_map/ppermute | solution.py:278
  52.0 26.8 %collective-permute-start.11 = (bf16[2,128,1024]{2,1,0:T(8,128)(2,1)S(1)}, bf16[2,128,1024]{2,1,0:T(8,128)(2,1)S(1)}, u32[]{:S(2)}, u32[]{:S(2)}) collective-permute-start(bf16[2,128,1024]{2,1,0:T(8,128)(2,1)S(1)} %get-tuple-element.75), channel_id=1, source_target_pairs={{4,0},{5,1},{6,2},{7,3},{8,12},{9,13},{10,14},{11,15},{20,16},{21,... | collective-permute-start | bytes 1572872 | tf_op jit(solution)/shard_map/ppermute | solution.py:278
  60.9 14.0 %copy-start = (bf16[8,16,8192]{2,1,0:T(8,128)(2,1)S(1)}, bf16[8,16,8192]{2,1,0:T(8,128)(2,1)}, u32[]{:S(2)}) copy-start(bf16[8,16,8192]{2,1,0:T(8,128)(2,1)} %param.9) | copy-start | bytes 6291460
  68.6 20.0 %collective-permute-start.14 = (bf16[2,128,1024]{2,1,0:T(8,128)(2,1)S(1)}, bf16[2,128,1024]{2,1,0:T(8,128)(2,1)S(1)}, u32[]{:S(2)}, u32[]{:S(2)}) collective-permute-start(bf16[2,128,1024]{2,1,0:T(8,128)(2,1)S(1)} %collective-permute-done.13.refs_4_), channel_id=1, source_target_pairs={{4,0},{5,1},{6,2},{7,3},{8,12},{9,13},{10,14},{11,15},{20,16},{21,... | collective-permute-start | bytes 1572872 | tf_op jit(solution)/shard_map/ppermute | solution.py:278
  69.9 1.2 collective-permute-start.8
  71.2 3.7 %collective-permute-start.9 = (f32[16,256]{1,0:T(8,128)S(1)}, f32[16,256]{1,0:T(8,128)S(1)}, u32[]{:S(2)}, u32[]{:S(2)}) collective-permute-start(f32[16,256]{1,0:T(8,128)S(1)} %add.82), channel_id=1, source_target_pairs={{0,2},{1,3},{2,0},{3,1},{4,6},{5,7},{6,4},{7,5},{8,10},{9,11},{10,... | collective-permute-start | bytes 49160 | tf_op jit(solution)/shard_map/ppermute | solution.py:271
  76.0 16.6 %collective-permute-start.12 = (bf16[4,160,512]{2,1,0:T(8,128)(2,1)S(1)}, bf16[4,160,512]{2,1,0:T(8,128)(2,1)S(1)}, u32[]{:S(2)}, u32[]{:S(2)}) collective-permute-start(bf16[4,160,512]{2,1,0:T(8,128)(2,1)S(1)} %bitcast.59), channel_id=1, source_target_pairs={{0,2},{1,3},{2,0},{3,1},{4,6},{5,7},{6,4},{7,5},{8,10},{9,11},{10,... | collective-permute-start | bytes 1966088 | tf_op jit(solution)/shard_map/ppermute | solution.py:271
  88.6 10.9 %collective-permute-start.18 = (bf16[2,2,96,512]{3,2,1,0:T(8,128)(2,1)S(1)}, bf16[2,2,96,512]{3,2,1,0:T(8,128)(2,1)S(1)}, u32[]{:S(2)}, u32[]{:S(2)}) collective-permute-start(bf16[2,2,96,512]{3,2,1,0:T(8,128)(2,1)S(1)} %get-tuple-element.90), channel_id=1, source_target_pairs={{0,4},{1,5},{2,6},{3,7},{4,0},{5,1},{6,2},{7,3},{8,12},{9,13},{10,... | collective-permute-start | bytes 1179656 | tf_op jit(solution)/shard_map/ppermute | solution.py:274
  89.8 1.2 collective-permute-start.15
  91.1 3.7 %collective-permute-start.17 = (f32[16,256]{1,0:T(8,128)S(1)}, f32[16,256]{1,0:T(8,128)S(1)}, u32[]{:S(2)}, u32[]{:S(2)}) collective-permute-start(f32[16,256]{1,0:T(8,128)S(1)} %add.86), channel_id=1, source_target_pairs={{0,2},{1,3},{2,0},{3,1},{4,6},{5,7},{6,4},{7,5},{8,10},{9,11},{10,... | collective-permute-start | bytes 49160 | tf_op jit(solution)/shard_map/ppermute | solution.py:271
  94.8 11.7 %collective-permute-start.16 = (bf16[2,160,512]{2,1,0:T(8,128)(2,1)S(1)}, bf16[2,160,512]{2,1,0:T(8,128)(2,1)S(1)}, u32[]{:S(2)}, u32[]{:S(2)}) collective-permute-start(bf16[2,160,512]{2,1,0:T(8,128)(2,1)S(1)} %slice.192), channel_id=1, source_target_pairs={{0,4},{1,5},{2,6},{3,7},{4,0},{5,1},{6,2},{7,3},{8,12},{9,13},{10,... | collective-permute-start | bytes 983048 | tf_op jit(solution)/shard_map/ppermute | solution.py:274
  99.5 14.9 %collective-permute-start.22 = (bf16[4,128,512]{2,1,0:T(8,128)(2,1)S(1)}, bf16[4,128,512]{2,1,0:T(8,128)(2,1)S(1)}, u32[]{:S(2)}, u32[]{:S(2)}) collective-permute-start(bf16[4,128,512]{2,1,0:T(8,128)(2,1)S(1)} %bitcast.60), channel_id=1, source_target_pairs={{0,2},{1,3},{2,0},{3,1},{4,6},{5,7},{6,4},{7,5},{8,10},{9,11},{10,... | collective-permute-start | bytes 1572872 | tf_op jit(solution)/shard_map/ppermute | solution.py:271
  101.2 17.4 %collective-permute-start.21 = (bf16[2,96,512]{2,1,0:T(8,128)(2,1)S(1)}, bf16[2,96,512]{2,1,0:T(8,128)(2,1)S(1)}, u32[]{:S(2)}, u32[]{:S(2)}) collective-permute-start(bf16[2,96,512]{2,1,0:T(8,128)(2,1)S(1)} %fusion.2), channel_id=1, source_target_pairs={{0,2},{1,3},{2,0},{3,1},{4,6},{5,7},{6,4},{7,5},{8,10},{9,11},{10,... | collective-permute-start | bytes 589832 | tf_op jit(solution)/shard_map/ppermute | solution.py:271
  103.4 15.4 %collective-permute-start.20 = (bf16[2,2,64,512]{3,2,1,0:T(8,128)(2,1)S(1)}, bf16[2,2,64,512]{3,2,1,0:T(8,128)(2,1)S(1)}, u32[]{:S(2)}, u32[]{:S(2)}) collective-permute-start(bf16[2,2,64,512]{3,2,1,0:T(8,128)(2,1)S(1)} %get-tuple-element.95), channel_id=1, source_target_pairs={{0,4},{1,5},{2,6},{3,7},{4,0},{5,1},{6,2},{7,3},{8,12},{9,13},{10,... | collective-permute-start | bytes 786440 | tf_op jit(solution)/shard_map/ppermute | solution.py:274
  103.4 18.6 %collective-permute-start.24 = (bf16[4,64,512]{2,1,0:T(8,128)(2,1)S(1)}, bf16[4,64,512]{2,1,0:T(8,128)(2,1)S(1)}, u32[]{:S(2)}, u32[]{:S(2)}) collective-permute-start(bf16[4,64,512]{2,1,0:T(8,128)(2,1)S(1)} %bitcast.64), channel_id=1, source_target_pairs={{0,2},{1,3},{2,0},{3,1},{4,6},{5,7},{6,4},{7,5},{8,10},{9,11},{10,... | collective-permute-start | bytes 786440 | tf_op jit(solution)/shard_map/ppermute | solution.py:271
  106.7 26.0 %collective-permute-start.19 = (bf16[1,160,512]{2,1,0:T(8,128)(2,1)S(1)}, bf16[1,160,512]{2,1,0:T(8,128)(2,1)S(1)}, u32[]{:S(2)}, u32[]{:S(2)}) collective-permute-start(bf16[1,160,512]{2,1,0:T(8,128)(2,1)S(1)} %slice.194), channel_id=1, source_target_pairs={{0,8},{1,9},{2,10},{3,11},{4,12},{5,13},{6,14},{7,15},{8,0},{9,1},... | collective-permute-start | bytes 491528 | tf_op jit(solution)/shard_map/ppermute | solution.py:274
  114.6 8.0 %collective-permute-start.26 = (bf16[2,128,512]{2,1,0:T(8,128)(2,1)S(1)}, bf16[2,128,512]{2,1,0:T(8,128)(2,1)S(1)}, u32[]{:S(2)}, u32[]{:S(2)}) collective-permute-start(bf16[2,128,512]{2,1,0:T(8,128)(2,1)S(1)} %slice.193), channel_id=1, source_target_pairs={{0,4},{1,5},{2,6},{3,7},{4,0},{5,1},{6,2},{7,3},{8,12},{9,13},{10,... | collective-permute-start | bytes 786440 | tf_op jit(solution)/shard_map/ppermute | solution.py:274
  118.7 14.0 %collective-permute-start.27 = (bf16[1,96,512]{2,1,0:T(8,128)(2,1)S(1)}, bf16[1,96,512]{2,1,0:T(8,128)(2,1)S(1)}, u32[]{:S(2)}, u32[]{:S(2)}) collective-permute-start(bf16[1,96,512]{2,1,0:T(8,128)(2,1)S(1)} %slice.197), channel_id=1, source_target_pairs={{0,8},{1,9},{2,10},{3,11},{4,12},{5,13},{6,14},{7,15},{8,0},{9,1},... | collective-permute-start | bytes 294920 | tf_op jit(solution)/shard_map/ppermute | solution.py:274
  118.9 10.7 %collective-permute-start.23 = (bf16[2,64,512]{2,1,0:T(8,128)(2,1)S(1)}, bf16[2,64,512]{2,1,0:T(8,128)(2,1)S(1)}, u32[]{:S(2)}, u32[]{:S(2)}) collective-permute-start(bf16[2,64,512]{2,1,0:T(8,128)(2,1)S(1)} %fusion.3), channel_id=1, source_target_pairs={{0,2},{1,3},{2,0},{3,1},{4,6},{5,7},{6,4},{7,5},{8,10},{9,11},{10,... | collective-permute-start | bytes 393224 | tf_op jit(solution)/shard_map/ppermute | solution.py:271
  122.2 7.3 %collective-permute-start.25 = (bf16[2,64,512]{2,1,0:T(8,128)(2,1)S(1)}, bf16[2,64,512]{2,1,0:T(8,128)(2,1)S(1)}, u32[]{:S(2)}, u32[]{:S(2)}) collective-permute-start(bf16[2,64,512]{2,1,0:T(8,128)(2,1)S(1)} %slice.196), channel_id=1, source_target_pairs={{0,4},{1,5},{2,6},{3,7},{4,0},{5,1},{6,2},{7,3},{8,12},{9,13},{10,... | collective-permute-start | bytes 393224 | tf_op jit(solution)/shard_map/ppermute | solution.py:274
  122.6 10.1 %collective-permute-start.28 = (bf16[1,128,512]{2,1,0:T(8,128)(2,1)S(1)}, bf16[1,128,512]{2,1,0:T(8,128)(2,1)S(1)}, u32[]{:S(2)}, u32[]{:S(2)}) collective-permute-start(bf16[1,128,512]{2,1,0:T(8,128)(2,1)S(1)} %slice.195), channel_id=1, source_target_pairs={{0,8},{1,9},{2,10},{3,11},{4,12},{5,13},{6,14},{7,15},{8,0},{9,1},... | collective-permute-start | bytes 393224 | tf_op jit(solution)/shard_map/ppermute | solution.py:274
  129.5 5.2 %collective-permute-start.30 = (bf16[1,64,512]{2,1,0:T(8,128)(2,1)S(1)}, bf16[1,64,512]{2,1,0:T(8,128)(2,1)S(1)}, u32[]{:S(2)}, u32[]{:S(2)}) collective-permute-start(bf16[1,64,512]{2,1,0:T(8,128)(2,1)S(1)} %slice.199), channel_id=1, source_target_pairs={{0,8},{1,9},{2,10},{3,11},{4,12},{5,13},{6,14},{7,15},{8,0},{9,1},... | collective-permute-start | bytes 196616 | tf_op jit(solution)/shard_map/ppermute | solution.py:274
  129.6 6.5 %collective-permute-start.29 = (bf16[1,64,512]{2,1,0:T(8,128)(2,1)S(1)}, bf16[1,64,512]{2,1,0:T(8,128)(2,1)S(1)}, u32[]{:S(2)}, u32[]{:S(2)}) collective-permute-start(bf16[1,64,512]{2,1,0:T(8,128)(2,1)S(1)} %slice.198), channel_id=1, source_target_pairs={{0,8},{1,9},{2,10},{3,11},{4,12},{5,13},{6,14},{7,15},{8,0},{9,1},... | collective-permute-start | bytes 196616 | tf_op jit(solution)/shard_map/ppermute | solution.py:274
  136.2 0.8 copy-start.3
